TPU v7x, 32 devices: a whole 2x2x4 slice. The times are simulated.
32 devices in a mesh: dp: 16 (over z, y, x), head: 2 (over core).
Axes of the slice: x: 2, y: 2, z: 4, core: 2. Of those that a mesh axis runs over, the one named last changes fastest.
Arguments:
- tokens: bfloat16 [24576, 768], P('dp'), may hold values from -6 to 6
- teacher: bfloat16 [24576, 768], P('dp'), may hold values from -12 to 12
- lengths: int32 [48, 6], P('dp'), may hold values from 0 to 512, as said below
- head_gate: float32 [12], P('head'), may hold values from 0.25 to 1
- unit_gate: float32 [3072], P('head'), may hold values from 0.25 to 1
- hidden_gate: float32 [768], replicated, may hold values from 0.5 to 1
- layer_gates: float32 [2], replicated, may hold values from 0.5 to 1
- master_qkv: float32 [768, 3, 768], P('dp', None, 'head'), may hold values from -4 to 4
- first_qkv: float32 [768, 3, 768], P('dp', None, 'head'), may hold values from -1881.2081 to 1881.2081
- second_qkv: float32 [768, 3, 768], P('dp', None, 'head'), may hold values from 49152 to 393216
- master_attn_out: float32 [768, 768], P('head', 'dp'), may hold values from -4 to 4
- first_attn_out: float32 [768, 768], P('head', 'dp'), may hold values from -1881.2081 to 1881.2081
- second_attn_out: float32 [768, 768], P('head', 'dp'), may hold values from 49152 to 393216
- master_ffn_in: float32 [768, 3072], P('dp', 'head'), may hold values from -4 to 4
- first_ffn_in: float32 [768, 3072], P('dp', 'head'), may hold values from -1881.2081 to 1881.2081
- second_ffn_in: float32 [768, 3072], P('dp', 'head'), may hold values from 49152 to 393216
- master_ffn_out: float32 [3072, 768], P('head', 'dp'), may hold values from -4 to 4
- first_ffn_out: float32 [3072, 768], P('head', 'dp'), may hold values from -1881.2081 to 1881.2081
- second_ffn_out: float32 [3072, 768], P('head', 'dp'), may hold values from 49152 to 393216
- master_norms: float32 [4, 768], P(None, 'dp'), may hold values from -1 to 2.5
- first_norms: float32 [4, 768], P(None, 'dp'), may hold values from -1881.2081 to 1881.2081
- second_norms: float32 [4, 768], P(None, 'dp'), may hold values from 49152 to 393216
Outputs:
- student: bfloat16 [24576, 768], P('dp')
- grad_tokens: float32 [24576, 768], P('dp')
- grad_head_gate: float32 [12], P('head')
- grad_unit_gate: float32 [3072], P('head')
- grad_hidden_gate: float32 [768], replicated
- grad_layer_gates: float32 [2], replicated
- grad_qkv: float32 [768, 3, 768], P('dp', None, 'head')
- new_first_qkv: float32 [768, 3, 768], P('dp', None, 'head')
- new_second_qkv: float32 [768, 3, 768], P('dp', None, 'head')
- new_master_qkv: float32 [768, 3, 768], P('dp', None, 'head')
- copy_qkv: bfloat16 [768, 3, 768], P('dp', None, 'head')
- grad_attn_out: float32 [768, 768], P('head', 'dp')
- new_first_attn_out: float32 [768, 768], P('head', 'dp')
- new_second_attn_out: float32 [768, 768], P('head', 'dp')
- new_master_attn_out: float32 [768, 768], P('head', 'dp')
- copy_attn_out: bfloat16 [768, 768], P('head', 'dp')
- grad_ffn_in: float32 [768, 3072], P('dp', 'head')
- new_first_ffn_in: float32 [768, 3072], P('dp', 'head')
- new_second_ffn_in: float32 [768, 3072], P('dp', 'head')
- new_master_ffn_in: float32 [768, 3072], P('dp', 'head')
- copy_ffn_in: bfloat16 [768, 3072], P('dp', 'head')
- grad_ffn_out: float32 [3072, 768], P('head', 'dp')
- new_first_ffn_out: float32 [3072, 768], P('head', 'dp')
- new_second_ffn_out: float32 [3072, 768], P('head', 'dp')
- new_master_ffn_out: float32 [3072, 768], P('head', 'dp')
- copy_ffn_out: bfloat16 [3072, 768], P('head', 'dp')
- grad_norms: float32 [4, 768], P(None, 'dp')
- new_first_norms: float32 [4, 768], P(None, 'dp')
- new_second_norms: float32 [4, 768], P(None, 'dp')
- new_master_norms: float32 [4, 768], P(None, 'dp')
- copy_norms: bfloat16 [4, 768], P(None, 'dp')
- lamb_stats: float32 [3, 8], replicated
Inputs may be any that keep to these rules, and one draw needn't show every extreme that they name: `lengths`: each row of 512 tokens holds whole sequences from its first position on, of 64 to 128 tokens, or one sequence of 512 tokens, with zeros after the last; the rest of a row is padding.
All inputs are finite; a program needn't handle non-finite values.
Results may differ from a plain program's by a relative error of at most 0.012.
The roundings to bfloat16 on the way count: a program that leaves them out, or rounds other values in their place, can miss the bound.
Values may be sent and summed in bfloat16 or wider, within the bound.
A program may use at most 192 MiB of HBM per device.

v0:
```python
from functools import partial

import jax
import jax.numpy as jnp
from jax import lax
from jax.sharding import PartitionSpec as P

D = 768
HEAD_DIM = 64
ROW = 512
STEP_COUNT = 5


LN_EPS = 1e-05
LAMB_EPS = 1e-06
WEIGHT_DECAY = 0.01
LEARN_RATE = 0.5
MOMENT_DECAY = 0.5
MASK_FILL = -1000000000.0


def layer_norm(rows_in, norm_gain, norm_bias):
    center = rows_in - jnp.mean(rows_in, axis=-1, keepdims=True)
    spread = jnp.mean(center * center, axis=-1, keepdims=True)
    return center * lax.rsqrt(spread + LN_EPS) * norm_gain + norm_bias


def lamb_moments(master, first, second, grad, decay):
    new_first = MOMENT_DECAY * first + (1.0 - MOMENT_DECAY) * grad
    new_second = MOMENT_DECAY * second + (1.0 - MOMENT_DECAY) * grad * grad
    correction = 1.0 - MOMENT_DECAY**STEP_COUNT
    update = (
        new_first / correction / (jnp.sqrt(new_second / correction) + LAMB_EPS) + decay * master
    )
    return (new_first, new_second, update)


def masked_scores(queries, key_rows, same_seq):
    scores = jnp.einsum(
        "rihd,rjhd->rhij", queries, key_rows, preferred_element_type=jnp.float32
    ) * HEAD_DIM ** (-0.5)
    return jnp.where(same_seq[:, None], scores, MASK_FILL)


def local(
    tokens,
    teacher,
    lengths,
    head_gate,
    unit_gate,
    hidden_gate,
    layer_gates,
    master_qkv,
    first_qkv,
    second_qkv,
    master_attn_out,
    first_attn_out,
    second_attn_out,
    master_ffn_in,
    first_ffn_in,
    second_ffn_in,
    master_ffn_out,
    first_ffn_out,
    second_ffn_out,
    master_norms,
    first_norms,
    second_norms,
):
    heads_here = head_gate.shape[0]
    local_width = heads_here * HEAD_DIM
    rows_here = lengths.shape[0]
    head_count = lax.axis_size("head")
    weight_squares = jnp.concatenate(
        [
            jnp.stack(
                [
                    jnp.sum(master_qkv * master_qkv),
                    jnp.sum(master_attn_out * master_attn_out),
                    jnp.sum(master_ffn_in * master_ffn_in),
                    jnp.sum(master_ffn_out * master_ffn_out),
                ]
            ),
            jnp.sum(master_norms * master_norms, axis=1) / head_count,
        ]
    )
    w_qkv, w_in, w_out, w_fo, norm_copy = (
        lax.all_gather(master_qkv.astype(jnp.bfloat16), "dp", axis=0, tiled=True),
        lax.all_gather(master_ffn_in.astype(jnp.bfloat16), "dp", axis=0, tiled=True),
        lax.all_gather(master_attn_out.astype(jnp.bfloat16), "dp", axis=1, tiled=True),
        lax.all_gather(master_ffn_out.astype(jnp.bfloat16), "dp", axis=1, tiled=True),
        lax.all_gather(master_norms.astype(jnp.bfloat16), "dp", axis=1, tiled=True),
    )
    norm_p = norm_copy.astype(jnp.float32)
    w_qkv_flat = w_qkv.reshape(D, 3 * local_width)
    seq_ends = jnp.cumsum(lengths, axis=1, dtype=jnp.int32)
    positions = jnp.arange(ROW, dtype=jnp.int32)
    seg_index = jnp.sum(
        (positions[None, :, None] >= seq_ends[:, None, :]).astype(jnp.int32),
        axis=2,
        dtype=jnp.int32,
    )
    valid_mask = (positions[None, :] < seq_ends[:, -1:]).astype(jnp.float32).reshape(-1, 1)
    same_seq = seg_index[:, :, None] == seg_index[:, None, :]
    qkv_all = jnp.dot(tokens, w_qkv_flat, preferred_element_type=jnp.float32).astype(jnp.bfloat16)
    qkv_all = qkv_all.reshape(rows_here, ROW, 3, heads_here, HEAD_DIM)
    queries = qkv_all[:, :, 0]
    key_rows = qkv_all[:, :, 1]
    value_rows = qkv_all[:, :, 2]
    scores = masked_scores(queries, key_rows, same_seq)
    row_max = jnp.max(scores, axis=-1, keepdims=True)
    expo = jnp.exp(scores - row_max)
    row_total = jnp.sum(expo, axis=-1, keepdims=True)
    log_total = row_max + jnp.log(row_total)
    prob_low = (expo / row_total).astype(jnp.bfloat16)
    head_mix = jnp.einsum(
        "rhij,rjhd->rihd", prob_low, value_rows, preferred_element_type=jnp.float32
    )
    context = (
        (head_mix * head_gate[None, None, :, None]).astype(jnp.bfloat16).reshape(-1, local_width)
    )
    attn_part = jnp.dot(context, w_out, preferred_element_type=jnp.float32)
    attn_sum = lax.psum(attn_part, "head")
    residual_in = tokens.astype(jnp.float32)
    teach_rows = teacher.astype(jnp.float32)
    attention = attn_sum * layer_gates[0] * hidden_gate
    hidden, first_norm_back = jax.vjp(layer_norm, residual_in + attention, norm_p[0], norm_p[1])
    hidden_low = hidden.astype(jnp.bfloat16)
    up_proj = jnp.dot(hidden_low, w_in, preferred_element_type=jnp.float32)
    gelu_out, gelu_back = jax.vjp(partial(jax.nn.gelu, approximate=False), up_proj)
    gated = (gelu_out * unit_gate).astype(jnp.bfloat16)
    ffn_part = jnp.dot(gated, w_fo, preferred_element_type=jnp.float32)
    ffn_sum = lax.psum(ffn_part.astype(jnp.bfloat16), "head").astype(jnp.float32)
    ffn_out = ffn_sum * layer_gates[1] * hidden_gate
    student, second_norm_back = jax.vjp(layer_norm, hidden + ffn_out, norm_p[2], norm_p[3])
    d_out = valid_mask * (student - teach_rows)
    d_res2, d_gain2, d_bias2 = second_norm_back(d_out)
    d_layer1 = jnp.sum(d_res2 * ffn_sum * hidden_gate)
    d_hidden_gate = jnp.sum(d_res2 * ffn_sum, axis=0) * layer_gates[1]
    d_ffn_part = (d_res2 * hidden_gate * layer_gates[1]).astype(jnp.bfloat16)
    student_low = student.astype(jnp.bfloat16)
    grad_fo = jnp.einsum("tu,td->ud", gated, d_ffn_part, preferred_element_type=jnp.float32)
    d_gated = jnp.einsum("td,ud->tu", d_ffn_part, w_fo, preferred_element_type=jnp.float32)
    d_unit = jnp.sum(d_gated * gelu_out, axis=0)
    (d_up,) = gelu_back(d_gated * unit_gate)
    d_up_low = d_up.astype(jnp.bfloat16)
    grad_in = jnp.einsum("tc,tu->cu", hidden_low, d_up_low, preferred_element_type=jnp.float32)
    back_part = jnp.einsum("tu,cu->tc", d_up_low, w_in, preferred_element_type=jnp.float32)
    d_hidden = d_res2 + lax.psum(back_part.astype(jnp.bfloat16), "head").astype(jnp.float32)
    d_res1, d_gain1, d_bias1 = first_norm_back(d_hidden)
    d_layer0 = jnp.sum(d_res1 * attn_sum * hidden_gate)
    d_hidden_gate = d_hidden_gate + jnp.sum(d_res1 * attn_sum, axis=0) * layer_gates[0]
    d_attn_part = (d_res1 * hidden_gate * layer_gates[0]).astype(jnp.bfloat16)
    grad_out = jnp.einsum("tc,td->cd", context, d_attn_part, preferred_element_type=jnp.float32)
    d_context = jnp.einsum("td,cd->tc", d_attn_part, w_out, preferred_element_type=jnp.float32)
    d_context = d_context.reshape(rows_here, ROW, heads_here, HEAD_DIM)
    d_heads = jnp.sum(d_context * head_mix, axis=(0, 1, 3))
    d_mix = (d_context * head_gate[None, None, :, None]).astype(jnp.bfloat16)
    probs_again = jnp.exp(masked_scores(queries, key_rows, same_seq) - log_total)
    d_probs = jnp.einsum("rihd,rjhd->rhij", d_mix, value_rows, preferred_element_type=jnp.float32)
    d_values = jnp.einsum(
        "rhij,rihd->rjhd",
        probs_again.astype(jnp.bfloat16),
        d_mix,
        preferred_element_type=jnp.float32,
    )
    d_scores = probs_again * (d_probs - jnp.sum(probs_again * d_probs, axis=-1, keepdims=True))
    d_scores = d_scores.astype(jnp.bfloat16)
    d_queries = jnp.einsum(
        "rhij,rjhd->rihd", d_scores, key_rows, preferred_element_type=jnp.float32
    ) * HEAD_DIM ** (-0.5)
    d_keys = jnp.einsum(
        "rhij,rihd->rjhd", d_scores, queries, preferred_element_type=jnp.float32
    ) * HEAD_DIM ** (-0.5)
    d_qkv = (
        jnp.stack([d_queries, d_keys, d_values], axis=2)
        .astype(jnp.bfloat16)
        .reshape(-1, 3 * local_width)
    )
    grad_qkv = jnp.einsum("tc,tk->ck", tokens, d_qkv, preferred_element_type=jnp.float32).reshape(
        D, 3, local_width
    )
    input_part = jnp.einsum("tk,ck->tc", d_qkv, w_qkv_flat, preferred_element_type=jnp.float32)
    grad_norm_rows = jnp.stack([d_gain1, d_bias1, d_gain2, d_bias2])
    layer_pair = jnp.stack([d_layer0, d_layer1])
    grad_tokens = d_res1 + lax.psum(input_part.astype(jnp.bfloat16), "head").astype(jnp.float32)
    sum_qkv, sum_in, sum_out, sum_fo, sum_norm = (
        lax.psum_scatter(grad_qkv, "dp", scatter_dimension=0, tiled=True),
        lax.psum_scatter(grad_in, "dp", scatter_dimension=0, tiled=True),
        lax.psum_scatter(grad_out, "dp", scatter_dimension=1, tiled=True),
        lax.psum_scatter(grad_fo, "dp", scatter_dimension=1, tiled=True),
        lax.psum_scatter(grad_norm_rows, "dp", scatter_dimension=1, tiled=True),
    )
    gate_heads, gate_units, gate_hidden, gate_layers = lax.psum(
        (d_heads, d_unit, d_hidden_gate, layer_pair), "dp"
    )
    mats = [
        (master_qkv, first_qkv, second_qkv, sum_qkv),
        (master_attn_out, first_attn_out, second_attn_out, sum_out),
        (master_ffn_in, first_ffn_in, second_ffn_in, sum_in),
        (master_ffn_out, first_ffn_out, second_ffn_out, sum_fo),
    ]
    moments = [
        lamb_moments(master, first, second, grad, WEIGHT_DECAY)
        for master, first, second, grad in mats
    ]
    nf_norms, ns_norms, upd_norms = lamb_moments(
        master_norms, first_norms, second_norms, sum_norm, 0.0
    )
    update_squares = jnp.concatenate(
        [
            jnp.stack([jnp.sum(entry[2] * entry[2]) for entry in moments]),
            jnp.sum(upd_norms * upd_norms, axis=1) / head_count,
        ]
    )
    weight_total, update_total = lax.psum((weight_squares, update_squares), ("dp", "head"))
    weight_norm = jnp.sqrt(weight_total)
    update_norm = jnp.sqrt(update_total)
    trust_ratio = weight_norm / update_norm
    results = []
    for index in range(4):
        master, first, second, grad = mats[index]
        new_first, new_second, update = moments[index]
        new_master = master - LEARN_RATE * trust_ratio[index] * update
        results.append((grad, new_first, new_second, new_master, new_master.astype(jnp.bfloat16)))
    new_norms = master_norms - LEARN_RATE * trust_ratio[4:][:, None] * upd_norms
    lamb_stats = jnp.stack([weight_norm, update_norm, trust_ratio])
    return (
        student_low,
        grad_tokens,
        gate_heads,
        gate_units,
        gate_hidden,
        gate_layers,
        results[0][0],
        results[0][1],
        results[0][2],
        results[0][3],
        results[0][4],
        results[1][0],
        results[1][1],
        results[1][2],
        results[1][3],
        results[1][4],
        results[2][0],
        results[2][1],
        results[2][2],
        results[2][3],
        results[2][4],
        results[3][0],
        results[3][1],
        results[3][2],
        results[3][3],
        results[3][4],
        sum_norm,
        nf_norms,
        ns_norms,
        new_norms,
        new_norms.astype(jnp.bfloat16),
        lamb_stats,
    )


def solution(mesh):
    return jax.shard_map(
        local,
        mesh=mesh,
        in_specs=(
            P("dp", None),
            P("dp", None),
            P("dp", None),
            P("head"),
            P("head"),
            P(),
            P(),
            P("dp", None, "head"),
            P("dp", None, "head"),
            P("dp", None, "head"),
            P("head", "dp"),
            P("head", "dp"),
            P("head", "dp"),
            P("dp", "head"),
            P("dp", "head"),
            P("dp", "head"),
            P("head", "dp"),
            P("head", "dp"),
            P("head", "dp"),
            P(None, "dp"),
            P(None, "dp"),
            P(None, "dp"),
        ),
        out_specs=(
            P("dp", None),
            P("dp", None),
            P("head"),
            P("head"),
            P(),
            P(),
            P("dp", None, "head"),
            P("dp", None, "head"),
            P("dp", None, "head"),
            P("dp", None, "head"),
            P("dp", None, "head"),
            P("head", "dp"),
            P("head", "dp"),
            P("head", "dp"),
            P("head", "dp"),
            P("head", "dp"),
            P("dp", "head"),
            P("dp", "head"),
            P("dp", "head"),
            P("dp", "head"),
            P("dp", "head"),
            P("head", "dp"),
            P("head", "dp"),
            P("head", "dp"),
            P("head", "dp"),
            P("head", "dp"),
            P(None, "dp"),
            P(None, "dp"),
            P(None, "dp"),
            P(None, "dp"),
            P(None, "dp"),
            P(),
        ),
        check_vma=False,
    )
```

profile of v0, /device:TPU:0, one launch (start us, length us, event | category | flops | bytes accessed | tf_op | source)
XLA Modules:
  0.0 1288.6 jit_solution(17413625497979769582)
XLA Ops:
  7.2 1.6 convert_element_type.121
  12.2 49.5 %all_gather.16 = bf16[384,768]{0,1:T(8,128)(2,1)} all-gather(bf16[384,48]{0,1:T(8,128)(2,1)S(1)} %convert_element_type.126), channel_id=1, replica_groups=mesh['dp'=16,'head'=2] {'dp'}, dimensions={1}, use_global_device_ids=true | all-gather | bytes 626688 | tf_op jit(solution)/shard_map/all_gather | solution.py:89
  61.7 12.5 all-gather.5.cloned.1.call-done
  74.2 3.9 copy.110
  78.0 5.4 convolution_convert_fusion
  83.5 8.5 reshape.218
  92.0 6.2 fusion.64
  98.2 2.7 copy.135
  100.9 3.6 copy.136
  104.6 3.9 copy.137
  108.5 8.2 fusion.67
  116.8 9.4 fusion
  126.2 10.3 fusion.18
  139.0 3.6 fusion.68
  146.3 38.5 %all-gather = bf16[16,48,4]{1,2,0:T(4,128)(2,1)S(1)} all-gather(bf16[1,48,4]{1,2,0:T(4,128)(2,1)S(1)} %get-tuple-element.102), channel_id=1, replica_groups=mesh['dp'=16,'head'=2] {'dp'}, dimensions={0}, use_global_device_ids=true | all-gather | bytes 6528 | tf_op jit(solution)/shard_map/all_gather | solution.py:91
  184.9 4.6 fusion.63
  189.5 2.2 copy-done
  192.4 45.6 %all-gather.7.cloned.1.call-done = bf16[768,1536]{1,0:T(8,128)(2,1)} async-done(((bf16[48,1536]{1,0:T(8,128)(2,1)}), bf16[768,1536]{1,0:T(8,128)(2,1)}) %all-gather.7.cloned.1.call-update) | async-done | bytes 2359312 | tf_op jit(solution)/shard_map/all_gather | solution.py:88
  238.0 28.0 %multiply_convert_fusion.1 = (bf16[1536,1536]{1,0:T(8,128)(2,1)}, f32[1536,1536]{1,0:T(8,128)}, f32[1536,1536]{1,0:T(8,128)}) fusion(f32[1536]{0:T(1024)S(1)} %copy-done.50, bf16[768,1536]{1,0:T(8,128)(2,1)} %all-gather.7.cloned.1.call-done, f32[1536,768]{1,0:T(8,128)} %copy-done, f32[768]{0:T(1024)S(1)} %get-tuple-element.54, ...), kind=kOutput, calls=%fused_computation.14 | convolution fusion | flops 3785490432 | bytes 30695424 | tf_op jit(solution)/shard_map/dot_general | solution.py:128
  265.9 36.8 %all-gather.9.cloned.1.call-done = bf16[1536,768]{0,1:T(8,128)(2,1)} async-done(((bf16[1536,48]{0,1:T(8,128)(2,1)}), bf16[1536,768]{0,1:T(8,128)(2,1)}) %all-gather.9.cloned.1.call-update) | async-done | bytes 2359312 | tf_op jit(solution)/shard_map/all_gather | solution.py:90
  302.7 8.4 convolution_convert_fusion.3
  311.4 20.3 %all-reduce.9.cloned.1.call-done = bf16[1536,768]{1,0:T(8,128)(2,1)} async-done(((bf16[1536,768]{1,0:T(8,128)(2,1)}), bf16[1536,768]{1,0:T(8,128)(2,1)}) %all-reduce.9.cloned.1.call-update) | async-done | bytes 2359312 | tf_op jit(solution)/shard_map/psum | solution.py:132
  331.7 5.1 fusion.60
  338.4 2.8 multiply_reduce_fusion.2
  341.3 4.6 fusion.59
  345.9 13.4 %multiply_reduce_fusion.1 = (f32[1536]{0:T(1024)S(1)}, bf16[1536,1536]{1,0:T(8,128)(2,1)S(1)}) fusion(f32[1536,1536]{1,0:T(8,128)} %get-tuple-element.91, f32[1536,1536]{1,0:T(8,128)} %get-tuple-element.116, f32[1536]{0:T(1024)S(1)} %copy-done.50, bf16[1536,768]{0,1:T(8,128)(2,1)S(1)} %copy-done.49, f32[1536,768]{1,0:T(8,128)S(1)} %get-tuple-element.87, ...), kind=kOutput, calls=%fused_computation.11 | convolution fusion | flops 3671063040 | bytes 30692356 | tf_op jit(solution)/shard_map/td,ud->tu/dot_general | solution.py:142
  359.3 2.1 copy-done.51
  361.5 5.1 convolution_convert_fusion.2
  366.7 22.9 %all-reduce.11.cloned.1.call-done = bf16[1536,768]{1,0:T(8,128)(2,1)} async-done(((bf16[1536,768]{1,0:T(8,128)(2,1)}), bf16[1536,768]{1,0:T(8,128)(2,1)}) %all-reduce.11.cloned.1.call-update) | async-done | bytes 2359312 | tf_op jit(solution)/shard_map/psum | solution.py:148
  389.6 7.7 multiply_reduce_fusion.3
  397.3 5.0 fusion.58
  402.4 2.1 copy-done.2
  404.5 3.3 fusion.42
  407.8 3.5 reshape.206
  411.3 9.3 fusion.20
  420.6 12.6 multiply_reduce_fusion
  433.2 14.1 %multiply_convert_fusion = bf16[3,6,512,512]{2,3,1,0:T(8,128)(2,1)S(1)} fusion(f32[3,6,512,512]{2,3,1,0:T(8,128)} %get-tuple-element.118, f32[3,6,512,512]{2,3,1,0:T(8,128)} %get-tuple-element.113, f32[3,6,512]{2,1,0:T(8,128)S(1)} %get-tuple-element.117, f32[3,6,512]{2,1,0:T(8,128)S(1)} %log_add_fusion), kind=kLoop, calls=%fused_computation | loop fusion | flops 18874368 | bytes 47259648 | tf_op jit(solution)/shard_map/convert_element_type | solution.py:167
  447.3 4.0 multiply_bitcast_fusion
  451.3 2.7 multiply_bitcast_fusion.1
  455.0 2.2 maximum_convert_fusion
  457.2 3.1 copy.123
  461.8 1.8 copy-done.13
  463.6 4.6 convolution_convert_fusion.1
  468.3 6.1 fusion.41
  474.6 10.3 fusion.43
  485.0 10.6 fusion.39
  495.9 7.5 fusion.69
  503.4 5.2 copy.125
  508.6 2.6 fusion.19
  511.2 66.7 %reduce-scatter.16.cloned.1.call-done = f32[48,4]{1,0:T(8,128)} async-done(((f32[768,4]{1,0:T(8,128)}), f32[48,4]{1,0:T(8,128)}) %reduce-scatter.16.cloned.1.call-update) | async-done | bytes 784
  579.6 21.4 %all-reduce.13.cloned.1.call-done = bf16[1536,768]{1,0:T(8,128)(2,1)} async-done(((bf16[1536,768]{1,0:T(8,128)(2,1)}), bf16[1536,768]{1,0:T(8,128)(2,1)}) %all-reduce.13.cloned.1.call-update) | async-done | bytes 2359312 | tf_op jit(solution)/shard_map/psum | solution.py:185
  601.0 7.3 multiply_reduce_fusion.5
  611.0 120.9 %reduce-scatter.10.cloned.1.call-done = f32[384,48]{0,1:T(8,128)} async-done(((f32[384,768]{0,1:T(8,128)}), f32[384,48]{0,1:T(8,128)}) %reduce-scatter.10.cloned.1.call-update) | async-done | bytes 73744 | tf_op jit(solution)/shard_map/reduce_scatter | solution.py:189
  731.9 1.6 multiply_reduce_fusion.17
  733.5 140.3 %reduce-scatter.12.cloned.1.call-done = f32[48,1536]{1,0:T(8,128)} async-done(((f32[768,1536]{1,0:T(8,128)}), f32[48,1536]{1,0:T(8,128)}) %reduce-scatter.12.cloned.1.call-update) | async-done | bytes 294928 | tf_op jit(solution)/shard_map/reduce_scatter | solution.py:188
  873.7 1.8 multiply_reduce_fusion.13
  875.6 140.0 %reduce-scatter.14.cloned.1.call-done = f32[1536,48]{0,1:T(8,128)} async-done(((f32[1536,768]{0,1:T(8,128)}), f32[1536,48]{0,1:T(8,128)}) %reduce-scatter.14.cloned.1.call-update) | async-done | bytes 294928 | tf_op jit(solution)/shard_map/reduce_scatter | solution.py:190
  1015.6 1.8 multiply_reduce_fusion.12
  1017.4 137.2 %reduce-scatter.8.cloned.1.call-done = f32[48,3,384]{2,0,1:T(8,128)} async-done(((f32[768,3,384]{2,0,1:T(8,128)}), f32[48,3,384]{2,0,1:T(8,128)}) %reduce-scatter.8.cloned.1.call-update) | async-done | bytes 221200 | tf_op jit(solution)/shard_map/reduce_scatter | solution.py:187
  1154.6 1.7 multiply_reduce_fusion.15
  1156.3 2.7 concatenate.6
  1159.0 2.7 concatenate.7
  1161.6 75.0 %all-reduce.1 = (f32[6]{0:T(128)}, f32[1536]{0:T(1024)}, f32[768]{0:T(1024)}, f32[2]{0:T(128)}) all-reduce(f32[6]{0:T(128)S(1)} %fusion.19, f32[1536]{0:T(1024)S(1)} %get-tuple-element.94, f32[768]{0:T(1024)S(1)} %multiply_add_fusion.13, f32[2]{0:T(128)S(1)} %pad_maximum_fusion.2), channel_id=1, replica_groups=mesh['dp'=16,'head'=2] {'dp'}, use_global_device_ids=true, to_apply=%region_18.19 | all-reduce | flops 2312 | bytes 18496 | tf_op jit(solution)/shard_map/psum | solution.py:193
  1236.7 36.8 %all-reduce = (f32[8]{0:T(128)S(1)}, f32[8]{0:T(128)S(1)}) all-reduce(f32[8]{0:T(128)S(1)} %concatenate.7, f32[8]{0:T(128)S(1)} %concatenate.6), channel_id=1, replica_groups=mesh['dp'=16,'head'=2] {'dp','head'}, use_global_device_ids=true, to_apply=%region_47.48 | all-reduce | flops 16 | bytes 128 | tf_op jit(solution)/shard_map/psum | solution.py:215
  (174 shorter events, 25.1 us)
Async XLA Ops:
  7.2 67.0 %all-gather.5.cloned.1.call-start = ((), (), s32[]{:S(2)}) async-start(), calls=%async_computation.5 | async-start | bytes 1880064 | tf_op jit(solution)/shard_map/all_gather | solution.py:87
  8.9 176.0 %all-reduce.7.cloned.1.call-start = ((), (), s32[]{:S(2)}) async-start(), calls=%async_computation.6 | async-start | bytes 9437184 | tf_op jit(solution)/shard_map/psum | solution.py:122
  100.9 7.6 copy-start.14
  104.5 12.2 copy-start.3
  108.5 8.2 copy-start.5
  116.8 9.5 copy-start.11
  116.8 9.5 copy-start.42
  136.6 2.4 copy-start.19
  138.0 1.0 copy-start.10
  142.6 1.0 copy-start.17
  142.6 1.7 copy-start.15
  142.6 2.5 copy-start.44
  142.6 3.1 copy-start.40
  142.6 42.3 %copy-start.39 = (f32[768]{0:T(1024)S(1)}, f32[768]{0:T(1024)}, u32[]{:S(2)}) copy-start(f32[768]{0:T(1024)} %param.27) | copy-start | bytes 9220
  142.6 95.3 %all-gather.7.cloned.1.call-start = ((), (), s32[]{:S(2)}) async-start(), calls=%async_computation.7 | async-start | bytes 2506752 | tf_op jit(solution)/shard_map/all_gather | solution.py:88
  144.2 158.5 %all-gather.9.cloned.1.call-start = ((), (), s32[]{:S(2)}) async-start(), calls=%async_computation.8 | async-start | bytes 2506752 | tf_op jit(solution)/shard_map/all_gather | solution.py:90
  145.0 186.7 %all-reduce.9.cloned.1.call-start = ((), (), s32[]{:S(2)}) async-start(), calls=%async_computation.9 | async-start | bytes 4718592 | tf_op jit(solution)/shard_map/psum | solution.py:132
  189.5 2.2 copy-start
  189.5 48.4 %copy-start.50 = (f32[1536]{0:T(1024)S(1)}, f32[1536]{0:T(1024)}, u32[]{:S(2)}) copy-start(f32[1536]{0:T(1024)} %param.26) | copy-start | bytes 18436
  311.1 78.4 %all-reduce.11.cloned.1.call-start = ((), (), s32[]{:S(2)}) async-start(), calls=%async_computation.10 | async-start | bytes 4718592 | tf_op jit(solution)/shard_map/psum | solution.py:148
  336.8 1.7 copy-start.7
  341.3 4.6 copy-start.49
  345.9 13.5 %copy-start.1 = (f32[1536,768]{1,0:T(8,128)}, f32[1536,768]{1,0:T(8,128)S(1)}, u32[]{:S(2)}) copy-start(f32[1536,768]{1,0:T(8,128)S(1)} %get-tuple-element.87) | copy-start | bytes 14155780
  345.9 15.6 %copy-start.48 = (bf16[768,1536]{1,0:T(8,128)(2,1)S(1)}, bf16[768,1536]{1,0:T(8,128)(2,1)}, u32[]{:S(2)}) copy-start(bf16[768,1536]{1,0:T(8,128)(2,1)} %all-gather.7.cloned.1.call-done) | copy-start | bytes 7077892
  359.3 2.1 copy-start.51
  361.5 28.1 %copy-start.8 = (bf16[1536,768]{1,0:T(8,128)(2,1)S(1)}, bf16[1536,768]{1,0:T(8,128)(2,1)}, u32[]{:S(2)}) copy-start(bf16[1536,768]{1,0:T(8,128)(2,1)} %all-reduce.9.cloned.1.call-done) | copy-start | bytes 7077892
  366.6 211.3 %reduce-scatter.16.cloned.1.call-start = ((), (), s32[]{:S(2)}) async-start(), calls=%async_computation.16 | async-start | bytes 417792
  389.6 7.7 copy-start.9
  402.3 2.1 copy-start.2
  411.3 9.4 copy-start.12
  433.2 14.1 %copy-start.4 = (bf16[3,512,1,6,64]{1,4,3,0,2:T(8,128)(2,1)S(1)}, bf16[3,512,1,6,64]{1,4,3,0,2:T(8,128)(2,1)}, u32[]{:S(2)}) copy-start(bf16[3,512,1,6,64]{1,4,3,0,2:T(8,128)(2,1)} %copy-done.3) | copy-start | bytes 3538948
  447.3 4.0 copy-start.6
  455.0 146.0 %all-reduce.13.cloned.1.call-start = ((), (), s32[]{:S(2)}) async-start(), calls=%async_computation.11 | async-start | bytes 4718592 | tf_op jit(solution)/shard_map/psum | solution.py:185
  460.3 3.3 copy-start.21
  461.8 1.8 copy-start.13
  468.3 263.6 %reduce-scatter.10.cloned.1.call-start = ((), (), s32[]{:S(2)}) async-start(), calls=%async_computation.13 | async-start | bytes 1253376 | tf_op jit(solution)/shard_map/reduce_scatter | solution.py:189
  474.4 399.3 %reduce-scatter.12.cloned.1.call-start = ((), (), s32[]{:S(2)}) async-start(), calls=%async_computation.14 | async-start | bytes 5013504 | tf_op jit(solution)/shard_map/reduce_scatter | solution.py:188
  484.9 530.6 %reduce-scatter.14.cloned.1.call-start = ((), (), s32[]{:S(2)}) async-start(), calls=%async_computation.15 | async-start | bytes 5013504 | tf_op jit(solution)/shard_map/reduce_scatter | solution.py:190
  495.6 658.9 %reduce-scatter.8.cloned.1.call-start = ((), (), s32[]{:S(2)}) async-start(), calls=%async_computation.12 | async-start | bytes 3760128 | tf_op jit(solution)/shard_map/reduce_scatter | solution.py:187
  503.4 5.2 copy-start.47
  508.6 70.1 %copy-start.41 = (f32[4,48]{1,0:T(4,128)S(1)}, f32[4,48]{1,0:T(4,128)}, u32[]{:S(2)}) copy-start(f32[4,48]{1,0:T(4,128)} %param.41) | copy-start | bytes 2308
  508.6 70.1 %copy-start.45 = (f32[4,48]{1,0:T(4,128)S(1)}, f32[4,48]{1,0:T(4,128)}, u32[]{:S(2)}) copy-start(f32[4,48]{1,0:T(4,128)} %param.42) | copy-start | bytes 2308
  508.6 70.1 %copy-start.46 = (f32[4,48]{1,0:T(4,128)S(1)}, f32[4,48]{1,0:T(4,128)}, u32[]{:S(2)}) copy-start(f32[4,48]{1,0:T(4,128)} %param.43) | copy-start | bytes 2308
  578.7 29.6 %copy-start.43 = (f32[4,48]{1,0:T(4,128)}, f32[4,48]{1,0:T(4,128)S(1)}, u32[]{:S(2)}) copy-start(f32[4,48]{1,0:T(4,128)S(1)} %copy.132) | copy-start | bytes 2308
  579.5 152.5 %copy-start.28 = (f32[384,48]{0,1:T(8,128)S(1)}, f32[384,48]{0,1:T(8,128)}, u32[]{:S(2)}) copy-start(f32[384,48]{0,1:T(8,128)} %param.32) | copy-start | bytes 221188
  579.5 152.5 %copy-start.37 = (f32[384,48]{0,1:T(8,128)S(1)}, f32[384,48]{0,1:T(8,128)}, u32[]{:S(2)}) copy-start(f32[384,48]{0,1:T(8,128)} %param.33) | copy-start | bytes 221188
  579.5 152.4 %copy-start.38 = (f32[384,48]{0,1:T(8,128)S(1)}, f32[384,48]{0,1:T(8,128)}, u32[]{:S(2)}) copy-start(f32[384,48]{0,1:T(8,128)} %param.34) | copy-start | bytes 221188
  579.5 294.3 %copy-start.18 = (f32[48,1536]{1,0:T(8,128)S(1)}, f32[48,1536]{1,0:T(8,128)}, u32[]{:S(2)}) copy-start(f32[48,1536]{1,0:T(8,128)} %param.35) | copy-start | bytes 884740
  579.5 294.2 %copy-start.31 = (f32[48,1536]{1,0:T(8,128)S(1)}, f32[48,1536]{1,0:T(8,128)}, u32[]{:S(2)}) copy-start(f32[48,1536]{1,0:T(8,128)} %param.36) | copy-start | bytes 884740
  579.5 294.2 %copy-start.32 = (f32[48,1536]{1,0:T(8,128)S(1)}, f32[48,1536]{1,0:T(8,128)}, u32[]{:S(2)}) copy-start(f32[48,1536]{1,0:T(8,128)} %param.37) | copy-start | bytes 884740
  579.5 436.0 %copy-start.16 = (f32[1536,48]{0,1:T(8,128)S(1)}, f32[1536,48]{0,1:T(8,128)}, u32[]{:S(2)}) copy-start(f32[1536,48]{0,1:T(8,128)} %param.38) | copy-start | bytes 884740
  579.5 436.0 %copy-start.33 = (f32[1536,48]{0,1:T(8,128)S(1)}, f32[1536,48]{0,1:T(8,128)}, u32[]{:S(2)}) copy-start(f32[1536,48]{0,1:T(8,128)} %param.39) | copy-start | bytes 884740
  579.5 436.0 %copy-start.34 = (f32[1536,48]{0,1:T(8,128)S(1)}, f32[1536,48]{0,1:T(8,128)}, u32[]{:S(2)}) copy-start(f32[1536,48]{0,1:T(8,128)} %param.40) | copy-start | bytes 884740
  579.6 575.0 %copy-start.20 = (f32[48,3,384]{2,0,1:T(8,128)S(1)}, f32[48,3,384]{2,0,1:T(8,128)}, u32[]{:S(2)}) copy-start(f32[48,3,384]{2,0,1:T(8,128)} %param.29) | copy-start | bytes 663556
  579.6 575.0 %copy-start.35 = (f32[48,3,384]{2,0,1:T(8,128)S(1)}, f32[48,3,384]{2,0,1:T(8,128)}, u32[]{:S(2)}) copy-start(f32[48,3,384]{2,0,1:T(8,128)} %param.31) | copy-start | bytes 663556
  579.6 575.0 %copy-start.36 = (f32[48,3,384]{2,0,1:T(8,128)S(1)}, f32[48,3,384]{2,0,1:T(8,128)}, u32[]{:S(2)}) copy-start(f32[48,3,384]{2,0,1:T(8,128)} %param.30) | copy-start | bytes 663556
  733.5 547.9 %copy-start.29 = (f32[384,48]{0,1:T(8,128)}, f32[384,48]{0,1:T(8,128)S(1)}, u32[]{:S(2)}) copy-start(f32[384,48]{0,1:T(8,128)S(1)} %get-tuple-element.80) | copy-start | bytes 221188
  733.5 547.9 %copy-start.30 = (f32[384,48]{0,1:T(8,128)}, f32[384,48]{0,1:T(8,128)S(1)}, u32[]{:S(2)}) copy-start(f32[384,48]{0,1:T(8,128)S(1)} %get-tuple-element.81) | copy-start | bytes 221188
  875.6 405.9 %copy-start.22 = (f32[48,1536]{1,0:T(8,128)}, f32[48,1536]{1,0:T(8,128)S(1)}, u32[]{:S(2)}) copy-start(f32[48,1536]{1,0:T(8,128)S(1)} %get-tuple-element.78) | copy-start | bytes 884740
  875.6 405.9 %copy-start.23 = (f32[48,1536]{1,0:T(8,128)}, f32[48,1536]{1,0:T(8,128)S(1)}, u32[]{:S(2)}) copy-start(f32[48,1536]{1,0:T(8,128)S(1)} %get-tuple-element.79) | copy-start | bytes 884740
  1017.4 264.1 %copy-start.24 = (f32[1536,48]{0,1:T(8,128)}, f32[1536,48]{0,1:T(8,128)S(1)}, u32[]{:S(2)}) copy-start(f32[1536,48]{0,1:T(8,128)S(1)} %get-tuple-element.76) | copy-start | bytes 884740
  1017.4 264.1 %copy-start.25 = (f32[1536,48]{0,1:T(8,128)}, f32[1536,48]{0,1:T(8,128)S(1)}, u32[]{:S(2)}) copy-start(f32[1536,48]{0,1:T(8,128)S(1)} %get-tuple-element.77) | copy-start | bytes 884740
  1156.3 125.2 %copy-start.26 = (f32[48,3,384]{2,0,1:T(8,128)}, f32[48,3,384]{2,0,1:T(8,128)S(1)}, u32[]{:S(2)}) copy-start(f32[48,3,384]{2,0,1:T(8,128)S(1)} %get-tuple-element.82) | copy-start | bytes 663556
  1156.3 125.2 %copy-start.27 = (f32[48,3,384]{2,0,1:T(8,128)}, f32[48,3,384]{2,0,1:T(8,128)S(1)}, u32[]{:S(2)}) copy-start(f32[48,3,384]{2,0,1:T(8,128)S(1)} %get-tuple-element.83) | copy-start | bytes 663556
Sparse Core Ops, SparseCore 0:
  11.3 62.8 all-gather.4
  142.8 27.8 all-reduce.6
  174.5 63.4 all-gather.6
  241.6 61.0 all-gather.8
  311.2 20.4 all-reduce.8
  366.7 22.7 all-reduce.10
  455.1 122.7 reduce-scatter.15
  580.2 20.6 all-reduce.12
  607.0 124.8 reduce-scatter.9
  738.3 135.3 reduce-scatter.11
  879.5 136.0 reduce-scatter.13
  1021.9 132.6 reduce-scatter.7
where the time goes:
time: 1300 us; the launch traced here: 1290 us
  waiting for transfers between devices  765 us (59%)
  blocking collectives  200 us (15%)
  matrix products  154 us (12%)
  other arithmetic  88.8 us (7%)
  local copies, waits for them, and re-layouts  63.3 us (5%)
  between operations  17.7 us (1%)
    reduce_scatter x1, waiting for transfers between devices, local(): lax.psum_scatter(grad_in, 'dp', scatter_dimension=0, tiled=True)  140 us
    reduce_scatter x1, waiting for transfers between devices, local(): lax.psum_scatter(grad_fo, 'dp', scatter_dimension=1, tiled=True)  140 us
    reduce_scatter x1, waiting for transfers between devices, local(): lax.psum_scatter(grad_qkv, 'dp', scatter_dimension=0, tiled=True)  137 us
    reduce_scatter x1, waiting for transfers between devices, local(): lax.psum_scatter(grad_out, 'dp', scatter_dimension=1, tiled=True)  121 us
    psum x1, blocking collectives, local(): lax.psum((d_heads, d_unit, d_hidden_gate, layer_pair), 'dp')  75 us
    unnamed x13, waiting for transfers between devices  66.9 us
    all_gather x1, blocking collectives, local(): lax.all_gather(master_attn_out.astype(jnp.bfloat16), 'dp', axis=1, tiled=...  49.5 us
    all_gather x1, waiting for transfers between devices, local(): lax.all_gather(master_ffn_in.astype(jnp.bfloat16), 'dp', axis=0, tiled=True)  45.6 us
  transfers between devices with their start and end apart: 12, of which 11 were waited for; matrix products, arithmetic and copies ran while one was open for 9% of the time, Pallas kernels for 0%

commit v1 on v0

v1 whole, which is shorter than its diff:
```python
import functools

import jax
import jax.numpy as jnp
from jax import lax
from jax.experimental import pallas as pl
from jax.experimental.pallas import tpu as pltpu
from jax.sharding import PartitionSpec as P

D = 768
HEAD_DIM = 64
ROW = 512
STEP_COUNT = 5

LN_EPS = 1e-05
LAMB_EPS = 1e-06
WEIGHT_DECAY = 0.01
LEARN_RATE = 0.5
MOMENT_DECAY = 0.5
MASK_FILL = -1000000000.0


MESH = pl.DeviceIdType.MESH
NZ, NY, NX = 4, 2, 2
GRID = NZ * NY * NX
CHUNKS = (
    (0, 0, 640, 0),
    (0, 640, 512, 1),
    (1, 0, 128, 0),
    (1, 128, 256, 1),
    (2, 0, 768, 0),
    (2, 768, 768, 1),
    (3, 0, 768, 0),
    (3, 768, 768, 1),
)
NORM_CHUNK = (4, 0, 128, 0)


def place(me):
    return me // (NY * NX), (me // NX) % NY, me % NX


def index(z, y, x):
    return (z * NY + y) * NX + x


def relative(z, y, x, rz, ra, rb, order):
    zz = lax.rem(z + rz, NZ)
    flip_x, flip_y = (ra, rb) if order == 0 else (rb, ra)
    return index(zz, 1 - y if flip_y else y, 1 - x if flip_x else x)


def slot(rz, ra, rb):
    return rz + NZ * (ra + 2 * rb)


def greet(peers):
    barrier = pltpu.get_barrier_semaphore()
    for peer in peers:
        pl.semaphore_signal(barrier, inc=1, device_id=peer, device_id_type=MESH)
    pl.semaphore_wait(barrier, len(peers))


def grid_peers(z, y, x, core):
    ahead = [index(lax.rem(z + d, NZ), y, x) for d in (1, 2, 3)]
    beside = [index(z, y, 1 - x), index(z, 1 - y, x)]
    return [(p, core) for p in ahead + beside]


def gather_kernel(rows, count, *refs):
    chunks_here = (*CHUNKS, NORM_CHUNK)
    src, dst = refs[:count], refs[count : 2 * count]
    local_sem, send_sem, recv_sem = refs[2 * count :]
    me, core = lax.axis_index("dp"), lax.axis_index("head")
    z, y, x = place(me)
    greet(grid_peers(z, y, x, core))

    def rows_of(device):
        return pl.ds(pl.multiple_of(device * rows, rows), rows)

    def copy(c, rz, ra, rb, to, there, k, own=False):
        p, first, width, order = chunks_here[c]
        device = relative(z, y, x, rz, ra, rb, order)
        columns = pl.ds(first, width)
        source = src[p].at[:, columns] if own else dst[p].at[rows_of(device), columns]
        return pltpu.make_async_remote_copy(
            src_ref=source,
            dst_ref=dst[p].at[rows_of(device), columns],
            send_sem=send_sem.at[c, k],
            recv_sem=recv_sem.at[c, there],
            device_id=(to, core),
            device_id_type=MESH,
        )

    def arrived(c, rz, ra, rb):
        copy(c, rz, ra, rb, me, slot(rz, ra, rb), 0).wait_recv()

    sends = []

    def send(*args, **kwargs):
        one = copy(*args, **kwargs)
        one.start()
        sends.append(one)

    kept = [
        pltpu.make_async_copy(src[p], dst[p].at[rows_of(me)], local_sem.at[p]) for p in range(count)
    ]
    for one in kept:
        one.start()
    chunks = range(len(chunks_here))
    along = [
        (index(z, y, 1 - x), index(z, 1 - y, x))[:: 1 if chunks_here[c][3] == 0 else -1] for c in chunks
    ]
    for c in chunks:
        for i, dz in enumerate((1, 3, 2)):
            to = index(lax.rem(z + dz, NZ), y, x)
            send(c, 0, 0, 0, to, slot(NZ - dz, 0, 0), i, own=True)
        send(c, 0, 0, 0, along[c][0], slot(0, 1, 0), 3, own=True)
        send(c, 0, 0, 0, along[c][1], slot(0, 0, 1), 7, own=True)
    for pair in range(0, len(chunks_here), 2):
        both = chunks[pair : pair + 2]
        for c in both:
            for i, rz in enumerate((1, 3, 2)):
                arrived(c, rz, 0, 0)
                send(c, rz, 0, 0, along[c][0], slot(rz, 1, 0), 4 + i)
                send(c, rz, 0, 0, along[c][1], slot(rz, 0, 1), 8 + i)
        for c in both:
            for i, rz in enumerate((0, 1, 3, 2)):
                arrived(c, rz, 1, 0)
                send(c, rz, 1, 0, along[c][1], slot(rz, 1, 1), 11 + i)
    for c in chunks:
        for ra in (0, 1):
            for rz in range(NZ):
                arrived(c, rz, ra, 1)
    for one in sends:
        one.wait_send()
    for one in kept:
        one.wait()


def gather(shards):
    rows, count = shards[0].shape[0], len(shards)
    space = pl.BlockSpec(memory_space=pl.ANY)
    return pl.pallas_call(
        functools.partial(gather_kernel, rows, count),
        out_shape=[jax.ShapeDtypeStruct((rows * GRID, s.shape[1]), s.dtype) for s in shards],
        in_specs=[space] * count,
        out_specs=[space] * count,
        scratch_shapes=[
            pltpu.SemaphoreType.DMA((count,)),
            pltpu.SemaphoreType.DMA((len(CHUNKS) + 1, 15)),
            pltpu.SemaphoreType.DMA((len(CHUNKS) + 1, 16)),
        ],
        compiler_params=pltpu.CompilerParams(collective_id=0, has_side_effects=True),
        name="weights_gather",
    )(*shards)


def scatter_kernel(rows, count, *refs):
    grads, outs = refs[:count], refs[count : 2 * count]
    refs = refs[2 * count :]
    get1, get2, get3, put2, put3, keep = (refs[i * count : (i + 1) * count] for i in range(6))
    send_sem, recv_sem = refs[6 * count :]
    me, core = lax.axis_index("dp"), lax.axis_index("head")
    z, y, x = place(me)
    greet(grid_peers(z, y, x, core))

    def rows_of(device):
        return pl.ds(pl.multiple_of(device * rows, rows), rows)

    sends = []

    def send(source, target, c, k, to):
        one = pltpu.make_async_remote_copy(
            src_ref=source,
            dst_ref=target,
            send_sem=send_sem.at[c, k],
            recv_sem=recv_sem.at[c, k],
            device_id=(to, core),
            device_id_type=MESH,
        )
        one.start()
        sends.append(one)

    def arrived(target, c, k):
        pltpu.make_async_remote_copy(
            src_ref=target,
            dst_ref=target,
            send_sem=send_sem.at[c, k],
            recv_sem=recv_sem.at[c, k],
            device_id=(me, core),
            device_id_type=MESH,
        ).wait_recv()

    order_of = range(len(CHUNKS))[::-1]
    along = [
        (index(z, y, 1 - x), index(z, 1 - y, x))[:: 1 if chunk[3] == 0 else -1] for chunk in CHUNKS
    ]
    depth = (1, 3, 2, 0)
    for c in order_of:
        p, first, width, order = CHUNKS[c]
        columns = pl.ds(first, width)
        for ra in (1, 0):
            for rz in depth:
                k = rz + NZ * ra
                block = rows_of(relative(z, y, x, rz, ra, 1, order))
                send(grads[p].at[block, columns], get1[p].at[k, :, columns], c, k, along[c][1])

    def second(c):
        p, first, width, order = CHUNKS[c]
        columns = pl.ds(first, width)
        for ra in (1, 0):
            for rz in depth:
                k = rz + NZ * ra
                arrived(get1[p].at[k, :, columns], c, k)
                block = rows_of(relative(z, y, x, rz, ra, 0, order))
                total = grads[p][block, columns].astype(jnp.float32) + get1[p][
                    k, :, columns
                ].astype(jnp.float32)
                if ra:
                    put2[p][rz, :, columns] = total.astype(jnp.bfloat16)
                    send(
                        put2[p].at[rz, :, columns],
                        get2[p].at[rz, :, columns],
                        c,
                        8 + rz,
                        along[c][0],
                    )
                else:
                    keep[p][rz, :, columns] = total

    def third(c):
        p, first, width, order = CHUNKS[c]
        columns = pl.ds(first, width)
        for rz in depth:
            arrived(get2[p].at[rz, :, columns], c, 8 + rz)
            total = keep[p][rz, :, columns] + get2[p][rz, :, columns].astype(jnp.float32)
            if rz:
                put3[p][rz - 1, :, columns] = total.astype(jnp.bfloat16)
                there = NZ - rz
                send(
                    put3[p].at[rz - 1, :, columns],
                    get3[p].at[there - 1, :, columns],
                    c,
                    11 + there,
                    index(lax.rem(z + rz, NZ), y, x),
                )
            else:
                keep[p][0, :, columns] = total

    def last(c):
        p, first, width, order = CHUNKS[c]
        columns = pl.ds(first, width)
        total = keep[p][0, :, columns]
        for there in (1, 2, 3):
            arrived(get3[p].at[there - 1, :, columns], c, 11 + there)
            total = total + get3[p][there - 1, :, columns].astype(jnp.float32)
        outs[p][:, columns] = total

    for c in order_of:
        second(c)
        if c < len(CHUNKS) - 1:
            third(c + 1)
        if c < len(CHUNKS) - 2:
            last(c + 2)
    third(0)
    last(1)
    last(0)
    for one in sends:
        one.wait_send()


def scatter(grads):
    count, rows = len(grads), grads[0].shape[0] // GRID
    space = pl.BlockSpec(memory_space=pltpu.VMEM)
    widths = [g.shape[1] for g in grads]
    scratch = []
    for blocks, kind in ((8, jnp.bfloat16), (4, jnp.bfloat16), (3, jnp.bfloat16), (4, jnp.bfloat16), (3, jnp.bfloat16), (4, jnp.float32)):
        scratch += [pltpu.VMEM((blocks, rows, w), kind) for w in widths]
    return pl.pallas_call(
        functools.partial(scatter_kernel, rows, count),
        out_shape=[jax.ShapeDtypeStruct((rows, w), jnp.float32) for w in widths],
        in_specs=[space] * count,
        out_specs=[space] * count,
        scratch_shapes=[
            *scratch,
            pltpu.SemaphoreType.DMA((len(CHUNKS), 15)),
            pltpu.SemaphoreType.DMA((len(CHUNKS), 15)),
        ],
        compiler_params=pltpu.CompilerParams(
            collective_id=1, has_side_effects=True, vmem_limit_bytes=48 << 20
        ),
        name="grads_scatter",
    )(*grads)


def total_kernel(both, src, out, mine, landed, send_sem, recv_sem):
    me, core = lax.axis_index("dp"), lax.axis_index("head")
    z, y, x = place(me)
    peers = grid_peers(z, y, x, core)
    steps = [(index(z, y, 1 - x), core), (index(z, 1 - y, x), core)]
    if both:
        steps = [(me, 1 - core), *steps]
    greet(peers[:3] + steps)
    sends = []

    def send(source, k, to):
        one = pltpu.make_async_remote_copy(
            src_ref=source,
            dst_ref=landed.at[k],
            send_sem=send_sem.at[k],
            recv_sem=recv_sem.at[k],
            device_id=to,
            device_id_type=MESH,
        )
        one.start()
        sends.append(one)
        return one

    mine[0] = src[...]
    for k, to in enumerate(steps):
        send(mine.at[k], k, to).wait_recv()
        mine[k + 1] = mine[k] + landed[k]
    n = len(steps)
    for dz in (1, 2, 3):
        send(mine.at[n], n + NZ - dz - 1, peers[dz - 1])
    for one in sends[n:]:
        one.wait_recv()
    planes = [mine[n], *(landed[n + r - 1] for r in (1, 2, 3))]
    total = None
    for plane in range(NZ):
        turn = lax.rem(plane - z + NZ, NZ)
        part = planes[0]
        for r in (1, 2, 3):
            part = jnp.where(turn == r, planes[r], part)
        total = part if total is None else total + part
    out[...] = total
    for one in sends:
        one.wait_send()


def grid_total(packed, both):
    space = pl.BlockSpec(memory_space=pltpu.VMEM)
    return pl.pallas_call(
        functools.partial(total_kernel, both),
        out_shape=jax.ShapeDtypeStruct(packed.shape, jnp.float32),
        in_specs=[space],
        out_specs=space,
        scratch_shapes=[
            pltpu.VMEM((4, *packed.shape), jnp.float32),
            pltpu.VMEM((6, *packed.shape), jnp.float32),
            pltpu.SemaphoreType.DMA((6,)),
            pltpu.SemaphoreType.DMA((6,)),
        ],
        compiler_params=pltpu.CompilerParams(
            collective_id=3 if both else 2, has_side_effects=True, vmem_limit_bytes=16 << 20
        ),
        name="norms_total" if both else "gates_total",
    )(packed)


NT = (((1,), (1,)), ((), ()))
NN = (((1,), (0,)), ((), ()))
PAIR = 2 * HEAD_DIM


def mul(a, b, dims=NN):
    return lax.dot_general(a, b, dims, preferred_element_type=jnp.float32)


def segments(lengths_ref, row, shape, axis):
    positions = lax.broadcasted_iota(jnp.int32, shape, axis)
    end = jnp.int32(0)
    found = jnp.zeros(shape, jnp.int32)
    for k in range(lengths_ref.shape[1]):
        end = end + lengths_ref[row, k]
        found = found + (positions >= end).astype(jnp.int32)
    return found


def flip(block):
    return jnp.transpose(block.astype(jnp.float32)).astype(block.dtype)


def head_lanes(block, head):
    lane = lax.broadcasted_iota(jnp.int32, block.shape, 1)
    inside = (lane < HEAD_DIM) if head == 0 else (lane >= HEAD_DIM)
    return jnp.where(inside, block, jnp.zeros_like(block))


def attention_kernel(lengths_ref, gate_ref, q_ref, k_ref, v_ref, mix_ref, context_ref, stats_ref):
    row = pl.program_id(0)
    same = segments(lengths_ref, row, (ROW, 1), 0) == segments(lengths_ref, row, (1, ROW), 1)
    queries = q_ref[...] * jnp.bfloat16(HEAD_DIM**-0.5)
    values_t = flip(v_ref[...])
    mixes = []
    for head in (0, 1):
        scores = mul(k_ref[...], head_lanes(queries, head), NT)
        scores = jnp.where(same, scores, MASK_FILL)
        top = jnp.max(scores, axis=0, keepdims=True)
        expo = jnp.exp(scores - top)
        total = jnp.sum(expo, axis=0, keepdims=True)
        probs = (expo * (1.0 / total)).astype(jnp.bfloat16)
        mixes.append(mul(values_t[head * HEAD_DIM : (head + 1) * HEAD_DIM], probs))
        stats_ref[0, 0, head : head + 1, :] = top + jnp.log(total)
    mix = jnp.transpose(jnp.concatenate(mixes, axis=0))
    mix_ref[...] = mix
    context_ref[...] = (mix * gate_ref[...]).astype(jnp.bfloat16)


def attention(qkv, lengths, gate_lanes):
    tokens, width = qkv.shape
    rows, pairs = lengths.shape[0], width // 3 // PAIR
    block = lambda part: pl.BlockSpec((ROW, PAIR), lambda r, h: (r, part * pairs + h))
    own = pl.BlockSpec((ROW, PAIR), lambda r, h: (r, h))
    return pl.pallas_call(
        attention_kernel,
        grid=(rows, pairs),
        in_specs=[
            pl.BlockSpec(memory_space=pltpu.SMEM),
            pl.BlockSpec((1, PAIR), lambda r, h: (0, h)),
            block(0),
            block(1),
            block(2),
        ],
        out_specs=[own, own, pl.BlockSpec((1, 1, 8, ROW), lambda r, h: (r, h, 0, 0))],
        out_shape=[
            jax.ShapeDtypeStruct((tokens, width // 3), jnp.float32),
            jax.ShapeDtypeStruct((tokens, width // 3), jnp.bfloat16),
            jax.ShapeDtypeStruct((rows, pairs, 8, ROW), jnp.float32),
        ],
        compiler_params=pltpu.CompilerParams(vmem_limit_bytes=32 << 20),
        cost_estimate=pl.CostEstimate(
            flops=4 * rows * pairs * 2 * ROW * ROW * HEAD_DIM,
            bytes_accessed=tokens * width * 4,
            transcendentals=rows * pairs * 2 * ROW * ROW,
        ),
        name="attention",
    )(lengths, gate_lanes, qkv, qkv, qkv)


def attention_back_kernel(
    lengths_ref, gate_ref, q_ref, k_ref, v_ref, stats_ref, mix_ref, d_ref, out_ref, heads_ref
):
    row, pair = pl.program_id(0), pl.program_id(1)
    same = segments(lengths_ref, row, (ROW, 1), 0) == segments(lengths_ref, row, (1, ROW), 1)
    queries = q_ref[...] * jnp.bfloat16(HEAD_DIM**-0.5)
    keys, values = k_ref[...], v_ref[...]
    keys_t = flip(keys)
    d_context = d_ref[...]
    heads_ref[0, 0] = jnp.broadcast_to(
        jnp.sum(d_context * mix_ref[...], axis=0, keepdims=True), (8, PAIR)
    )
    d_mix = (d_context * gate_ref[...]).astype(jnp.bfloat16)
    d_queries, d_keys, d_values = [], None, None
    for head in (0, 1):
        q_one, d_one = head_lanes(queries, head), head_lanes(d_mix, head)
        scores = jnp.where(same, mul(keys, q_one, NT), MASK_FILL)
        probs = jnp.exp(scores - stats_ref[0, 0, head : head + 1, :])
        d_probs = mul(values, d_one, NT)
        weighed = jnp.sum(probs * d_probs, axis=0, keepdims=True)
        d_scores = (probs * (d_probs - weighed)).astype(jnp.bfloat16)
        dv = mul(probs.astype(jnp.bfloat16), d_one)
        dk = mul(d_scores, q_one)
        d_values = dv if head == 0 else d_values + dv
        d_keys = dk if head == 0 else d_keys + dk
        d_queries.append(mul(keys_t[head * HEAD_DIM : (head + 1) * HEAD_DIM], d_scores))
    dq = jnp.transpose(jnp.concatenate(d_queries, axis=0)) * HEAD_DIM**-0.5
    width = out_ref.shape[1] // 3
    for part, value in enumerate((dq, d_keys, d_values)):
        start = pl.multiple_of(part * width + pair * PAIR, PAIR)
        out_ref[:, pl.ds(start, PAIR)] = value.astype(jnp.bfloat16)


def attention_back(qkv, lengths, gate_lanes, stats, mix, d_context):
    tokens, width = qkv.shape
    rows, pairs = lengths.shape[0], width // 3 // PAIR
    block = lambda part: pl.BlockSpec((ROW, PAIR), lambda r, h: (r, part * pairs + h))
    own = pl.BlockSpec((ROW, PAIR), lambda r, h: (r, h))
    small = pl.BlockSpec((1, 1, 8, ROW), lambda r, h: (r, h, 0, 0))
    return pl.pallas_call(
        attention_back_kernel,
        grid=(rows, pairs),
        in_specs=[
            pl.BlockSpec(memory_space=pltpu.SMEM),
            pl.BlockSpec((1, PAIR), lambda r, h: (0, h)),
            block(0),
            block(1),
            block(2),
            small,
            own,
            own,
        ],
        out_specs=[
            pl.BlockSpec((ROW, width), lambda r, h: (r, 0)),
            pl.BlockSpec((1, 1, 8, PAIR), lambda r, h: (r, h, 0, 0)),
        ],
        out_shape=[
            jax.ShapeDtypeStruct((tokens, width), jnp.bfloat16),
            jax.ShapeDtypeStruct((rows, pairs, 8, PAIR), jnp.float32),
        ],
        compiler_params=pltpu.CompilerParams(vmem_limit_bytes=32 << 20),
        cost_estimate=pl.CostEstimate(
            flops=10 * rows * pairs * 2 * ROW * ROW * HEAD_DIM,
            bytes_accessed=tokens * width * 8,
            transcendentals=rows * pairs * 2 * ROW * ROW,
        ),
        name="attention_back",
    )(lengths, gate_lanes, qkv, qkv, qkv, stats, mix, d_context)


def layer_norm(rows_in, norm_gain, norm_bias):
    center = rows_in - jnp.mean(rows_in, axis=-1, keepdims=True)
    spread = jnp.mean(center * center, axis=-1, keepdims=True)
    return center * lax.rsqrt(spread + LN_EPS) * norm_gain + norm_bias


def lamb_moments(master, first, second, grad, decay):
    new_first = MOMENT_DECAY * first + (1.0 - MOMENT_DECAY) * grad
    new_second = MOMENT_DECAY * second + (1.0 - MOMENT_DECAY) * grad * grad
    correction = 1.0 - MOMENT_DECAY**STEP_COUNT
    update = (
        new_first / correction / (jnp.sqrt(new_second / correction) + LAMB_EPS) + decay * master
    )
    return (new_first, new_second, update)


def core_sum(part):
    part = part.astype(jnp.bfloat16)
    other = lax.ppermute(part, "head", [(0, 1), (1, 0)])
    return part.astype(jnp.float32) + other.astype(jnp.float32)


def pack(pieces):
    flat = []
    for piece in pieces:
        piece = piece.reshape(-1)
        flat.append(jnp.pad(piece, (0, -piece.size % 128)))
    flat = jnp.concatenate(flat)
    return jnp.pad(flat, (0, -flat.size % 1024)).reshape(-1, 128)


def unpack(packed, pieces):
    flat, first, found = packed.reshape(-1), 0, []
    for piece in pieces:
        found.append(flat[first : first + piece.size].reshape(piece.shape))
        first += piece.size + -piece.size % 128
    return found


def rows_first(qkv):
    return jnp.transpose(qkv, (1, 0, 2))


def local(
    tokens,
    teacher,
    lengths,
    head_gate,
    unit_gate,
    hidden_gate,
    layer_gates,
    master_qkv,
    first_qkv,
    second_qkv,
    master_attn_out,
    first_attn_out,
    second_attn_out,
    master_ffn_in,
    first_ffn_in,
    second_ffn_in,
    master_ffn_out,
    first_ffn_out,
    second_ffn_out,
    master_norms,
    first_norms,
    second_norms,
):
    heads_here = head_gate.shape[0]
    local_width = heads_here * HEAD_DIM
    head_count = lax.axis_size("head")
    ours = lax.axis_size("dp") == GRID and head_count == 2
    shard = master_qkv.shape[0]
    weight_squares = jnp.concatenate(
        [
            jnp.stack(
                [
                    jnp.sum(master_qkv * master_qkv),
                    jnp.sum(master_attn_out * master_attn_out),
                    jnp.sum(master_ffn_in * master_ffn_in),
                    jnp.sum(master_ffn_out * master_ffn_out),
                ]
            ),
            jnp.sum(master_norms * master_norms, axis=1) / head_count,
        ]
    )
    shards = [
        master_qkv.astype(jnp.bfloat16).reshape(shard, 3 * local_width),
        master_attn_out.T.astype(jnp.bfloat16),
        master_ffn_in.astype(jnp.bfloat16),
        master_ffn_out.T.astype(jnp.bfloat16),
        jnp.pad(master_norms.T, ((0, 0), (0, 124))).astype(jnp.bfloat16),
    ]
    if ours:
        w_qkv, w_out_t, w_in, w_fo_t, norm_t = gather(shards)
    else:
        w_qkv, w_out_t, w_in, w_fo_t, norm_t = (
            lax.all_gather(s, "dp", axis=0, tiled=True) for s in shards
        )
    norm_p = norm_t[:, :4].T.astype(jnp.float32)
    total = jnp.sum(lengths, axis=1, keepdims=True)
    positions = jnp.arange(ROW, dtype=jnp.int32)
    valid_mask = (positions[None, :] < total).astype(jnp.float32).reshape(-1, 1)
    gate_lanes = jnp.repeat(head_gate, HEAD_DIM)[None, :]
    qkv = jnp.dot(tokens, w_qkv, preferred_element_type=jnp.float32).astype(jnp.bfloat16)
    head_mix, context, stats = attention(qkv, lengths, gate_lanes)
    attn_part = jnp.einsum("tc,dc->td", context, w_out_t, preferred_element_type=jnp.float32)
    attn_sum = core_sum(attn_part)
    residual_in = tokens.astype(jnp.float32)
    teach_rows = teacher.astype(jnp.float32)
    attention_out = attn_sum * layer_gates[0] * hidden_gate
    hidden, first_norm_back = jax.vjp(
        layer_norm, residual_in + attention_out, norm_p[0], norm_p[1]
    )
    hidden_low = hidden.astype(jnp.bfloat16)
    up_proj = jnp.dot(hidden_low, w_in, preferred_element_type=jnp.float32)
    gelu_out, gelu_back = jax.vjp(
        functools.partial(jax.nn.gelu, approximate=False), up_proj
    )
    gated = (gelu_out * unit_gate).astype(jnp.bfloat16)
    ffn_part = jnp.einsum("tu,du->td", gated, w_fo_t, preferred_element_type=jnp.float32)
    ffn_sum = core_sum(ffn_part)
    ffn_out = ffn_sum * layer_gates[1] * hidden_gate
    student, second_norm_back = jax.vjp(layer_norm, hidden + ffn_out, norm_p[2], norm_p[3])
    d_out = valid_mask * (student - teach_rows)
    d_res2, d_gain2, d_bias2 = second_norm_back(d_out)
    d_layer1 = jnp.sum(d_res2 * ffn_sum * hidden_gate)
    d_hidden_gate = jnp.sum(d_res2 * ffn_sum, axis=0) * layer_gates[1]
    d_ffn_part = (d_res2 * hidden_gate * layer_gates[1]).astype(jnp.bfloat16)
    student_low = student.astype(jnp.bfloat16)
    grad_fo_t = jnp.einsum("td,tu->du", d_ffn_part, gated, preferred_element_type=jnp.float32)
    d_gated = jnp.dot(d_ffn_part, w_fo_t, preferred_element_type=jnp.float32)
    d_unit = jnp.sum(d_gated * gelu_out, axis=0)
    (d_up,) = gelu_back(d_gated * unit_gate)
    d_up_low = d_up.astype(jnp.bfloat16)
    grad_in = jnp.einsum("tc,tu->cu", hidden_low, d_up_low, preferred_element_type=jnp.float32)
    back_part = jnp.einsum("tu,cu->tc", d_up_low, w_in, preferred_element_type=jnp.float32)
    d_hidden = d_res2 + core_sum(back_part)
    d_res1, d_gain1, d_bias1 = first_norm_back(d_hidden)
    d_layer0 = jnp.sum(d_res1 * attn_sum * hidden_gate)
    d_hidden_gate = d_hidden_gate + jnp.sum(d_res1 * attn_sum, axis=0) * layer_gates[0]
    d_attn_part = (d_res1 * hidden_gate * layer_gates[0]).astype(jnp.bfloat16)
    grad_out_t = jnp.einsum("td,tc->dc", d_attn_part, context, preferred_element_type=jnp.float32)
    d_context = jnp.dot(d_attn_part, w_out_t, preferred_element_type=jnp.float32)
    d_qkv, head_lanes_sum = attention_back(qkv, lengths, gate_lanes, stats, head_mix, d_context)
    d_heads = jnp.sum(
        head_lanes_sum[:, :, 0, :].reshape(-1, heads_here, HEAD_DIM), axis=(0, 2)
    )
    grad_qkv = jnp.einsum("tc,tk->ck", tokens, d_qkv, preferred_element_type=jnp.float32)
    input_part = jnp.einsum("tk,ck->tc", d_qkv, w_qkv, preferred_element_type=jnp.float32)
    grad_norm_rows = jnp.stack([d_gain1, d_bias1, d_gain2, d_bias2])
    layer_pair = jnp.stack([d_layer0, d_layer1])
    grad_tokens = d_res1 + core_sum(input_part)
    grads = [grad_qkv, grad_out_t, grad_in, grad_fo_t]
    small = [d_heads, d_unit, d_hidden_gate, layer_pair, grad_norm_rows]
    if ours:
        sums = list(scatter([g.astype(jnp.bfloat16) for g in grads]))
        gate_heads, gate_units, gate_hidden, gate_layers, norm_total = unpack(
            grid_total(pack(small), False), small
        )
    else:
        sums = [lax.psum_scatter(g, "dp", scatter_dimension=0, tiled=True) for g in grads]
        gate_heads, gate_units, gate_hidden, gate_layers, norm_total = lax.psum(small, "dp")
    columns = master_norms.shape[1]
    sum_norm = lax.dynamic_slice_in_dim(norm_total, lax.axis_index("dp") * columns, columns, 1)
    sums[0] = sums[0].reshape(shard, 3, local_width)
    mats = [
        (master_qkv, first_qkv, second_qkv, sums[0]),
        (master_attn_out, first_attn_out, second_attn_out, sums[1].T),
        (master_ffn_in, first_ffn_in, second_ffn_in, sums[2]),
        (master_ffn_out, first_ffn_out, second_ffn_out, sums[3].T),
    ]
    moments = [
        lamb_moments(master, first, second, grad, WEIGHT_DECAY)
        for master, first, second, grad in mats
    ]
    nf_norms, ns_norms, upd_norms = lamb_moments(
        master_norms, first_norms, second_norms, sum_norm, 0.0
    )
    update_squares = jnp.concatenate(
        [
            jnp.stack([jnp.sum(entry[2] * entry[2]) for entry in moments]),
            jnp.sum(upd_norms * upd_norms, axis=1) / head_count,
        ]
    )
    squares = [weight_squares, update_squares]
    if ours:
        weight_total, update_total = unpack(grid_total(pack(squares), True), squares)
    else:
        weight_total, update_total = lax.psum(squares, ("dp", "head"))
    weight_norm = jnp.sqrt(weight_total)
    update_norm = jnp.sqrt(update_total)
    trust_ratio = weight_norm / update_norm
    results = []
    for at in range(4):
        master, first, second, grad = mats[at]
        new_first, new_second, update = moments[at]
        new_master = master - LEARN_RATE * trust_ratio[at] * update
        results += [grad, new_first, new_second, new_master, new_master.astype(jnp.bfloat16)]
    new_norms = master_norms - LEARN_RATE * trust_ratio[4:][:, None] * upd_norms
    lamb_stats = jnp.stack([weight_norm, update_norm, trust_ratio])
    return (
        student_low,
        grad_tokens,
        gate_heads,
        gate_units,
        gate_hidden,
        gate_layers,
        *results,
        sum_norm,
        nf_norms,
        ns_norms,
        new_norms,
        new_norms.astype(jnp.bfloat16),
        lamb_stats,
    )


def solution(mesh):
    return jax.shard_map(
        local,
        mesh=mesh,
        in_specs=(
            P("dp", None),
            P("dp", None),
            P("dp", None),
            P("head"),
            P("head"),
            P(),
            P(),
            P("dp", None, "head"),
            P("dp", None, "head"),
            P("dp", None, "head"),
            P("head", "dp"),
            P("head", "dp"),
            P("head", "dp"),
            P("dp", "head"),
            P("dp", "head"),
            P("dp", "head"),
            P("head", "dp"),
            P("head", "dp"),
            P("head", "dp"),
            P(None, "dp"),
            P(None, "dp"),
            P(None, "dp"),
        ),
        out_specs=(
            P("dp", None),
            P("dp", None),
            P("head"),
            P("head"),
            P(),
            P(),
            P("dp", None, "head"),
            P("dp", None, "head"),
            P("dp", None, "head"),
            P("dp", None, "head"),
            P("dp", None, "head"),
            P("head", "dp"),
            P("head", "dp"),
            P("head", "dp"),
            P("head", "dp"),
            P("head", "dp"),
            P("dp", "head"),
            P("dp", "head"),
            P("dp", "head"),
            P("dp", "head"),
            P("dp", "head"),
            P("head", "dp"),
            P("head", "dp"),
            P("head", "dp"),
            P("head", "dp"),
            P("head", "dp"),
            P(None, "dp"),
            P(None, "dp"),
            P(None, "dp"),
            P(None, "dp"),
            P(None, "dp"),
            P(),
        ),
        check_vma=False,
    )
```

time: 1300 us -> 439 us (0.34)
  waiting for transfers between devices: 765 us -> 1.83 us
  Pallas kernels: 0 us -> 220 us
  blocking collectives: 200 us -> 0 us
  matrix products: 154 us -> 98.1 us
  other arithmetic: 88.8 us -> 63.9 us
  local copies, waits for them, and re-layouts: 63.3 us -> 41.8 us
  between operations: 17.7 us -> 4.24 us
    reduce_scatter x4 -> x0, waiting for transfers between devices: 538 us -> none  [the longest x1 140 us: local(): lax.psum_scatter(grad_in, 'dp', scatter_dimension=0, tiled=True)]
    pallas_call x0 -> x6, Pallas kernels: none -> 220 us  [the longest x1 88.9 us: scatter(): pl.pallas_call(functools.partial(scatter_kernel, rows, count), out_shape=...]
    psum x2 -> x0, blocking collectives: 112 us -> none  [the longest x1 75 us: local(): lax.psum((d_heads, d_unit, d_hidden_gate, layer_pair), 'dp')]
    all_gather x3 -> x0, waiting for transfers between devices: 94.8 us -> none  [the longest x1 45.6 us: local(): lax.all_gather(master_ffn_in.astype(jnp.bfloat16), 'dp', axis=0, tiled=True)]
    all_gather x2 -> x0, blocking collectives: 88 us -> none  [the longest x1 49.5 us: local(): lax.all_gather(master_attn_out.astype(jnp.bfloat16), 'dp', axis=1, tiled=...]
    unnamed x13 -> x0, waiting for transfers between devices: 66.9 us -> none
    psum x4 -> x0, waiting for transfers between devices: 64.5 us -> none  [the longest x1 22.9 us: local(): lax.psum(back_part.astype(jnp.bfloat16), 'head').astype(jnp.float32)]
    dot_general x14 -> x8, matrix products: 103 us -> 54.7 us  [the longest x1 14.7 us: local(): d_gated = jnp.dot(d_ffn_part, w_fo_t, preferred_element_type=jnp.float32)]
  transfers between devices with their start and end apart: 12 -> 4, of which waited for: 11 -> 1; matrix products, arithmetic and copies ran while one was open for 9% -> 13% of each run, Pallas kernels for 0% -> 21%
where the time goes in v1:
time: 439 us; the launch traced here: 430 us
  Pallas kernels  220 us (50%)
  matrix products  98.1 us (22%)
  other arithmetic  63.9 us (15%)
  local copies, waits for them, and re-layouts  41.8 us (10%)
    pallas_call x1, Pallas kernels, scatter(): pl.pallas_call(functools.partial(scatter_kernel, rows, count), out_shape=...  88.9 us
    pallas_call x1, Pallas kernels, gather(): pl.pallas_call(functools.partial(gather_kernel, rows, count), out_shape=[...  72.3 us
    unnamed x113, local copies, waits for them, and re-layouts  28.6 us
    dot_general x1, matrix products, local(): up_proj = jnp.dot(hidden_low, w_in, preferred_element_type=jnp.float32)  28.1 us
    pallas_call x2, Pallas kernels, grid_total(): pl.pallas_call(functools.partial(total_kernel, both), out_shape=jax.Shape...  22.2 us
    pallas_call x1, Pallas kernels, attention_back(): pl.pallas_call(attention_back_kernel, grid=(rows, pairs), in_specs=[pl.Bl...  21.5 us
    reduce_sum x4, other arithmetic, layer_norm(): center = rows_in - jnp.mean(rows_in, axis=-1, keepdims=True)  16.8 us
    pallas_call x1, Pallas kernels, attention(): pl.pallas_call(attention_kernel, grid=(rows, pairs), in_specs=[pl.BlockSp...  15 us
  transfers between devices with their start and end apart: 4, of which 1 were waited for; matrix products, arithmetic and copies ran while one was open for 13% of the time, Pallas kernels for 21%

profile of v1, /device:TPU:0, one launch (start us, length us, event | category | flops | bytes accessed | tf_op | source)
XLA Modules:
  0.0 430.4 jit_solution(14045550085127743082)
XLA Ops:
  0.7 0.9 multiply_reduce_fusion.18
  1.6 1.0 convert_bitcast_fusion.2
  2.6 0.7 copy.128
  3.3 1.6 convert_bitcast_fusion.1.refs_3_
  4.9 1.6 convert_element_type.144.refs_2_
  6.5 1.5 convert_bitcast_fusion.3.refs_1_
  8.0 0.7 broadcast_in_dim.10
  8.8 0.6 pad.28.refs_4_
  9.5 72.3 %weights_gather.1 = (bf16[768,1152]{1,0:T(8,128)(2,1)}, bf16[768,384]{1,0:T(8,128)(2,1)}, bf16[768,1536]{1,0:T(8,128)(2,1)}, bf16[768,1536]{1,0:T(8,128)(2,1)}, bf16[768,128]{1,0:T(8,128)(2,1)}) custom-call(bf16[48,1152]{1,0:T(8,128)(2,1)} %bitcast.81, bf16[48,384]{1,0:T(8,128)(2,1)} %convert_bitcast_fusion.3.refs_1_, ...), custom_call_target="tpu_custom_call" | custom-call | tf_op jit(solution)/shard_map/weights_gather/pallas_call | solution.py:144
  81.7 5.4 %fusion.6.q_ref.k_ref.v_ref = bf16[1536,1152]{1,0:T(8,128)(2,1)S(1)} fusion(bf16[1536,768]{1,0:T(8,128)(2,1)} %param.22, bf16[768,1152]{1,0:T(8,128)(2,1)} %get-tuple-element.46), kind=kOutput, calls=%fused_computation.22 | convolution fusion | flops 2719678464 | bytes 7667712 | tf_op jit(solution)/shard_map/dot_general | solution.py:615
  87.2 15.0 %attention.1 = (f32[1536,384]{1,0:T(8,128)S(1)}, bf16[1536,384]{1,0:T(8,128)(2,1)S(1)}, f32[3,3,8,512]{3,2,1,0:T(8,128)S(1)}) custom-call(s32[3,6]{1,0:T(4,128)S(1)} %copy-done.4, f32[1,384]{1,0:T(1,128)S(1)} %broadcast_in_dim_reshape.3.gate_ref, bf16[1536,1152]{1,0:T(8,128)(2,1)S(1)} %fusion.6.q_ref.k_ref.v_ref, ...), custom_call_target="tpu_custom_call" | custom-call | flops 1207959552 | bytes 7077888 | tf_op jit(solution)/shard_map/attention/pallas_call | solution.py:416
  102.2 1.4 copy-done.2
  103.6 1.0 copy-done.9
  104.7 1.4 convolution_convert_fusion.7
  106.2 4.9 %copy.108 = bf16[1536,768]{0,1:T(8,128)(2,1)} copy(bf16[1536,768]{1,0:T(8,128)(2,1)} %param.22) | data formatting | bytes 4718592 | tf_op args[0]
  111.7 0.8 slice_reduce_fusion.1
  112.6 4.4 %fusion.47 = (f32[1536]{0:T(1024)S(1)}, f32[1536,768]{0,1:T(8,128)S(1)}) fusion(f32[768]{0:T(1024)S(1)} %copy-done.31, f32[]{:T(128)} %bitcast.4, bf16[1536,768]{0,1:T(8,128)(2,1)} %collective-permute-done, bf16[1536,768]{0,1:T(8,128)(2,1)S(1)} %convolution_convert_fusion.7, bf16[1536,768]{0,1:T(8,128)(2,1)} %copy.108), kind=kLoop, calls=%fused_computation.152 | loop fusion | flops 9435648 | bytes 11805700 | tf_op jit(solution)/shard_map/jvp()/reduce_sum | solution.py:513
  117.6 2.8 copy-done.39
  120.4 28.1 %multiply_convert_fusion = (bf16[1536,1536]{1,0:T(8,128)(2,1)S(1)}, f32[1536,1536]{1,0:T(8,128)}, f32[1536,1536]{1,0:T(8,128)}) fusion(f32[1536]{0:T(1024)S(1)} %copy-done.44, bf16[768,1536]{1,0:T(8,128)(2,1)S(1)} %copy-done.39, f32[1536,768]{0,1:T(8,128)S(1)} %get-tuple-element.246, f32[768]{0:T(1024)S(1)} %get-tuple-element.200, ...), kind=kOutput, calls=%fused_computation.4 | convolution fusion | flops 3785490432 | bytes 30695424 | tf_op jit(solution)/shard_map/dot_general | solution.py:626
  148.5 5.2 %convolution_convert_fusion.6 = bf16[1536,768]{0,1:T(8,128)(2,1)} fusion(bf16[1536,1536]{1,0:T(8,128)(2,1)S(1)} %get-tuple-element.243, bf16[768,1536]{1,0:T(8,128)(2,1)S(1)} %copy-done.41), kind=kOutput, calls=%fused_computation.52 | convolution fusion | flops 3625058304 | bytes 9437184 | tf_op jit(solution)/shard_map/tu,du->td/dot_general | solution.py:631
  153.7 2.8 copy.113
  156.7 1.8 collective-permute-done.1
  158.5 5.4 %fusion.45 = (f32[1536]{0:T(1024)S(1)}, f32[1536,768]{0,1:T(8,128)S(1)}) fusion(f32[768]{0:T(1024)S(1)} %copy-done.31, f32[]{:T(128)} %bitcast.6, bf16[1536,768]{0,1:T(8,128)(2,1)} %collective-permute-done.1, bf16[1536,768]{0,1:T(8,128)(2,1)} %convolution_convert_fusion.6, f32[768]{0:T(1024)S(1)} %get-tuple-element.200, f32[768]{0:T(1024)S(1)} %get-tuple-element.201, ...), kind=kLoop, calls=%fused_computation.151 | loop fusion | flops 12974592 | bytes 14183428 | tf_op jit(solution)/shard_map/jvp()/reduce_sum | solution.py:513
  164.5 2.8 multiply_reduce_fusion.1
  167.4 3.6 fusion.44
  170.9 14.7 %multiply_reduce_fusion = (f32[1536]{0:T(1024)}, bf16[1536,1536]{1,0:T(8,128)(2,1)S(1)}) fusion(f32[1536,1536]{1,0:T(8,128)} %get-tuple-element.244, f32[1536,1536]{1,0:T(8,128)} %get-tuple-element.262, f32[1536]{0:T(1024)S(1)} %copy-done.44, bf16[768,1536]{1,0:T(8,128)(2,1)S(1)} %copy-done.42, f32[1536,768]{0,1:T(8,128)S(1)} %get-tuple-element.240, ...), kind=kOutput, calls=%fused_computation.2 | convolution fusion | flops 3671063040 | bytes 30692356 | tf_op jit(solution)/shard_map/dot_general | solution.py:642
  185.6 5.2 %convolution_convert_fusion.5 = bf16[1536,768]{0,1:T(8,128)(2,1)} fusion(bf16[1536,1536]{1,0:T(8,128)(2,1)S(1)} %get-tuple-element.248, bf16[768,1536]{1,0:T(8,128)(2,1)S(1)} %copy-done.40), kind=kOutput, calls=%fused_computation.51 | convolution fusion | flops 3625058304 | bytes 9437184 | tf_op jit(solution)/shard_map/tu,cu->tc/dot_general | solution.py:647
  191.5 2.8 copy.119
  194.3 10.3 %convolution_convert_fusion.1.refs_3_ = bf16[768,1536]{1,0:T(8,128)(2,1)} fusion(bf16[1536,1536]{1,0:T(8,128)(2,1)} %copy-done.45, f32[1536,768]{0,1:T(8,128)} %copy-done.12, f32[1536]{0:T(1024)S(1)} %negate_multiply_fusion.2, f32[]{:T(128)} %bitcast.6, f32[768]{0:T(1024)S(1)} %copy-done.31), kind=kOutput, calls=%fused_computation.47 | convolution fusion | flops 3629776896 | bytes 11805700 | tf_op jit(solution)/shard_map/td,tu->du/dot_general | solution.py:641
  204.6 6.9 %convolution_convert_fusion.2.refs_2_ = bf16[768,1536]{1,0:T(8,128)(2,1)S(1)} fusion(bf16[1536,1536]{1,0:T(8,128)(2,1)S(1)} %copy-done.47, f32[1536,768]{0,1:T(8,128)} %copy-done.11, f32[768]{0:T(1024)S(1)} %get-tuple-element.200, f32[768]{0:T(1024)S(1)} %get-tuple-element.201, f32[1536]{0:T(1024)S(1)} %fusion.20, f32[1536]{0:T(1024)S(1)} %broadcast_multiply_fusion.1), kind=kOutput, calls=%fused_computation.48 | convolution fusion | flops 3630956544 | bytes 11814912 | tf_op jit(solution)/shard_map/tc,tu->cu/dot_general | solution.py:646
  211.6 4.4 %multiply_reduce_fusion.2 = (f32[768]{0:T(1024)S(1)}, f32[1536]{0:T(1024)S(1)}, f32[768]{0:T(1024)S(1)}, f32[1536,768]{0,1:T(8,128)S(1)}) fusion(f32[1536,768]{0,1:T(8,128)S(1)} %bitcast.78, f32[1536]{0:T(1024)S(1)} %fusion.20, f32[1536]{0:T(1024)S(1)} %broadcast_multiply_fusion.1, f32[768]{0:T(1024)S(1)} %get-tuple-element.201, ...), kind=kLoop, calls=%fused_computation.24 | loop fusion | flops 15332352 | bytes 18908160 | tf_op jit(solution)/shard_map/transpose(jvp())/reduce_sum | solution.py:515
  216.1 3.4 fusion.43
  219.6 0.6 reshape.199
  220.2 5.2 %fusion.29.d_ref = f32[1536,384]{1,0:T(8,128)S(1)} fusion(bf16[768,384]{1,0:T(8,128)(2,1)} %get-tuple-element.48, f32[1536,768]{0,1:T(8,128)} %get-tuple-element.237, f32[1536]{0:T(1024)S(1)} %negate_multiply_fusion.1, f32[768]{0:T(1024)S(1)} %copy-done.31, f32[]{:T(128)} %bitcast.4), kind=kOutput, calls=%fused_computation.142 | convolution fusion | flops 910688256 | bytes 7676932 | tf_op jit(solution)/shard_map/dot_general | solution.py:654
  225.4 21.5 %attention_back.1 = (bf16[1536,1152]{1,0:T(8,128)(2,1)S(1)}, f32[3,3,8,128]{3,2,1,0:T(8,128)S(1)}) custom-call(s32[3,6]{1,0:T(4,128)S(1)} %copy-done.4, f32[1,384]{1,0:T(1,128)S(1)} %copy-done.6, bf16[1536,1152]{1,0:T(8,128)(2,1)S(1)} %copy-done.1, bf16[1536,1152]{1,0:T(8,128)(2,1)S(1)} %copy-done.1, bf16[1536,1152]{1,0:T(8,128)(2,1)S(1)} %copy-done.1, ...), custom_call_target="tpu_custom_call" | custom-call | flops 3019898880 | bytes 14155776 | tf_op jit(solution)/shard_map/attention_back/pallas_call | solution.py:481
  247.0 1.7 copy-done.7
  248.8 7.4 %convolution_convert_fusion.4 = bf16[1536,768]{0,1:T(8,128)(2,1)} fusion(bf16[1536,1152]{1,0:T(8,128)(2,1)} %copy-done.7, bf16[768,1152]{1,0:T(8,128)(2,1)} %get-tuple-element.46), kind=kOutput, calls=%fused_computation.50 | convolution fusion | flops 2719088640 | bytes 7667712 | tf_op jit(solution)/shard_map/tk,ck->tc/dot_general | solution.py:660
  256.6 5.1 %convolution_convert_fusion.8.refs_1_ = bf16[768,384]{1,0:T(8,128)(2,1)S(1)} fusion(bf16[1536,384]{1,0:T(8,128)(2,1)S(1)} %copy-done.10, f32[1536,768]{0,1:T(8,128)} %get-tuple-element.237, f32[1536]{0:T(1024)S(1)} %negate_multiply_fusion.1, f32[768]{0:T(1024)S(1)} %copy-done.31, f32[]{:T(128)} %bitcast.4), kind=kOutput, calls=%fused_computation.57 | convolution fusion | flops 910983168 | bytes 6497284 | tf_op jit(solution)/shard_map/td,tc->dc/dot_general | solution.py:653
  261.7 3.3 fusion.12.refs_0_
  265.0 88.9 %grads_scatter.1 = (f32[48,1152]{1,0:T(8,128)S(1)}, f32[48,384]{1,0:T(8,128)S(1)}, f32[48,1536]{1,0:T(8,128)S(1)}, f32[48,1536]{1,0:T(8,128)S(1)}) custom-call(bf16[768,1152]{1,0:T(8,128)(2,1)S(1)} %fusion.12.refs_0_, bf16[768,384]{1,0:T(8,128)(2,1)S(1)} %convolution_convert_fusion.8.refs_1_, bf16[768,1536]{1,0:T(8,128)(2,1)S(1)} %convolution_convert_fusion.2.refs_2_, ...), custom_call_target="tpu_custom_call" | custom-call | tf_op jit(solution)/shard_map/grads_scatter/pallas_call | solution.py:280
  354.0 0.6 reduce_sum.311
  354.6 2.3 multiply_reduce_fusion.16
  357.0 2.6 multiply_reduce_fusion.14
  359.6 2.8 multiply_reduce_fusion.12
  362.4 2.7 multiply_reduce_fusion.11
  365.0 3.3 concatenate.13
  368.4 1.3 constant_dynamic-update-slice_fusion.3
  369.7 1.3 constant_dynamic-update-slice_fusion.4
  371.0 12.1 %multiply_reduce_fusion.4 = (f32[]{:T(128)}, f32[768]{0:T(1024)S(1)}, f32[768]{0:T(1024)S(1)}, f32[]{:T(128)}, f32[1536,768]{0,1:T(8,128)}) fusion(f32[768]{0:T(1024)S(1)} %copy-done.31, bf16[1536,768]{0,1:T(8,128)(2,1)} %collective-permute-done, bf16[1536,768]{0,1:T(8,128)(2,1)S(1)} %copy-done.14, f32[1536,768]{0,1:T(8,128)} %get-tuple-element.237, ...), kind=kLoop, calls=%fused_computation.26 | loop fusion | flops 23591424 | bytes 28333064 | tf_op jit(solution)/shard_map/reduce_sum | solution.py:650
  383.1 1.3 constant_dynamic-update-slice_fusion.2
  384.4 1.4 constant_dynamic-update-slice_fusion.1
  385.8 11.4 %gates_total.1 = f32[48,128]{1,0:T(8,128)S(1)} custom-call(f32[48,128]{1,0:T(8,128)S(1)} %pad_bitcast_fusion.src), custom_call_target="tpu_custom_call" | custom-call | tf_op jit(solution)/shard_map/gates_total/pallas_call | solution.py:344
  397.2 0.8 multiply_reduce_fusion.17
  398.0 2.7 concatenate.14
  400.7 10.9 %norms_total.1 = f32[8,128]{1,0:T(8,128)S(1)} custom-call(f32[8,128]{1,0:T(8,128)S(1)} %pad_bitcast_fusion.1.src), custom_call_target="tpu_custom_call" | custom-call | tf_op jit(solution)/shard_map/norms_total/pallas_call | solution.py:344
  417.2 6.2 %copy.120 = f32[1536,768]{1,0:T(8,128)} copy(f32[1536,768]{0,1:T(8,128)} %get-tuple-element.250) | data formatting | bytes 9437184
  423.4 0.6 fusion.33
  424.6 0.9 fusion.34
  425.6 0.9 fusion.35
  426.5 0.7 fusion.36
  427.2 0.9 fusion.37
  428.1 0.6 copy.139
  428.7 0.7 copy.140
  429.4 0.7 copy.141
  (150 shorter events, 7.2 us)
Async XLA Ops:
  8.8 78.3 %copy-start.5 = (f32[1,384]{1,0:T(1,128)}, f32[1,384]{1,0:T(1,128)S(1)}, u32[]{:S(2)}) copy-start(f32[1,384]{1,0:T(1,128)S(1)} %broadcast_in_dim_reshape.3.gate_ref) | copy-start | bytes 4612
  81.7 5.5 %copy-start.4 = (s32[3,6]{1,0:T(4,128)S(1)}, s32[3,6]{1,0:T(4,128)}, u32[]{:S(2)}) copy-start(s32[3,6]{1,0:T(4,128)} %lengths_ref.3) | copy-start | bytes 220
  87.2 15.0 %copy-start = (bf16[1536,1152]{1,0:T(8,128)(2,1)}, bf16[1536,1152]{1,0:T(8,128)(2,1)S(1)}, u32[]{:S(2)}) copy-start(bf16[1536,1152]{1,0:T(8,128)(2,1)S(1)} %fusion.6.q_ref.k_ref.v_ref) | copy-start | bytes 10616836
  87.2 17.5 %copy-start.43 = (bf16[768,384]{1,0:T(8,128)(2,1)S(1)}, bf16[768,384]{1,0:T(8,128)(2,1)}, u32[]{:S(2)}) copy-start(bf16[768,384]{1,0:T(8,128)(2,1)} %get-tuple-element.48) | copy-start | bytes 1769476
  102.2 1.4 copy-start.2
  103.6 1.0 copy-start.9
  104.7 6.5 %copy-start.37 = (f32[2]{0:T(128)S(1)}, f32[2]{0:T(128)}, u32[]{:S(2)}) copy-start(f32[2]{0:T(128)} %param.28) | copy-start | bytes 28
  104.7 7.0 %copy-start.29 = (bf16[768,128]{1,0:T(8,128)(2,1)S(1)}, bf16[768,128]{1,0:T(8,128)(2,1)}, u32[]{:S(2)}) copy-start(bf16[768,128]{1,0:T(8,128)(2,1)} %get-tuple-element.49) | copy-start | bytes 589828
  106.1 10.9 %copy-start.13 = (bf16[1536,768]{0,1:T(8,128)(2,1)}, bf16[1536,768]{0,1:T(8,128)(2,1)S(1)}, u32[]{:S(2)}) copy-start(bf16[1536,768]{0,1:T(8,128)(2,1)S(1)} %convolution_convert_fusion.7) | copy-start | bytes 7077892
  106.1 6.5 %copy-start.31 = (f32[768]{0:T(1024)S(1)}, f32[768]{0:T(1024)}, u32[]{:S(2)}) copy-start(f32[768]{0:T(1024)} %param.27) | copy-start | bytes 9220
  106.1 6.4 %collective-permute-start = (bf16[1536,768]{0,1:T(8,128)(2,1)S(1)}, bf16[1536,768]{0,1:T(8,128)(2,1)}, u32[]{:S(2)}, u32[]{:S(2)}) collective-permute-start(bf16[1536,768]{0,1:T(8,128)(2,1)S(1)} %convolution_convert_fusion.7), channel_id=1, source_target_pairs={{0,1},{1,0},{2,3},{3,2},{4,5},{5,4},{6,7},{7,6},{8,9},{9,8},{10,11... | collective-permute-start | bytes 7077896 | tf_op jit(solution)/shard_map/ppermute | solution.py:530
  117.0 31.4 %copy-start.11 = (f32[1536,768]{0,1:T(8,128)}, f32[1536,768]{0,1:T(8,128)S(1)}, u32[]{:S(2)}) copy-start(f32[1536,768]{0,1:T(8,128)S(1)} %get-tuple-element.246) | copy-start | bytes 14155780
  117.0 3.4 copy-start.39
  117.0 3.4 copy-start.44
  120.4 28.1 %copy-start.41 = (bf16[768,1536]{1,0:T(8,128)(2,1)S(1)}, bf16[768,1536]{1,0:T(8,128)(2,1)}, u32[]{:S(2)}) copy-start(bf16[768,1536]{1,0:T(8,128)(2,1)} %get-tuple-element.51) | copy-start | bytes 7077892
  148.5 5.2 %copy-start.45 = (bf16[1536,1536]{1,0:T(8,128)(2,1)}, bf16[1536,1536]{1,0:T(8,128)(2,1)S(1)}, u32[]{:S(2)}) copy-start(bf16[1536,1536]{1,0:T(8,128)(2,1)S(1)} %get-tuple-element.243) | copy-start | bytes 14155780
  153.7 4.9 %collective-permute-start.1 = (bf16[1536,768]{0,1:T(8,128)(2,1)}, bf16[1536,768]{0,1:T(8,128)(2,1)}, u32[]{:S(2)}, u32[]{:S(2)}) collective-permute-start(bf16[1536,768]{0,1:T(8,128)(2,1)} %convolution_convert_fusion.6), channel_id=1, source_target_pairs={{0,1},{1,0},{2,3},{3,2},{4,5},{5,4},{6,7},{7,6},{8,9},{9,8},{10,11... | collective-permute-start | bytes 7077896 | tf_op jit(solution)/shard_map/ppermute | solution.py:530
  167.4 3.6 copy-start.42
  170.9 14.7 %copy-start.12 = (f32[1536,768]{0,1:T(8,128)}, f32[1536,768]{0,1:T(8,128)S(1)}, u32[]{:S(2)}) copy-start(f32[1536,768]{0,1:T(8,128)S(1)} %get-tuple-element.240) | copy-start | bytes 14155780
  170.9 14.7 %copy-start.40 = (bf16[768,1536]{1,0:T(8,128)(2,1)S(1)}, bf16[768,1536]{1,0:T(8,128)(2,1)}, u32[]{:S(2)}) copy-start(bf16[768,1536]{1,0:T(8,128)(2,1)} %get-tuple-element.50) | copy-start | bytes 7077892
  185.6 5.2 %copy-start.46 = (bf16[1536,1536]{1,0:T(8,128)(2,1)}, bf16[1536,1536]{1,0:T(8,128)(2,1)S(1)}, u32[]{:S(2)}) copy-start(bf16[1536,1536]{1,0:T(8,128)(2,1)S(1)} %get-tuple-element.248) | copy-start | bytes 14155780
  185.6 5.8 %copy-start.15 = (bf16[1536,768]{0,1:T(8,128)(2,1)S(1)}, bf16[1536,768]{0,1:T(8,128)(2,1)}, u32[]{:S(2)}) copy-start(bf16[1536,768]{0,1:T(8,128)(2,1)} %get-tuple-element.249) | copy-start | bytes 7077892
  190.8 20.7 %collective-permute-start.2 = (bf16[1536,768]{0,1:T(8,128)(2,1)}, bf16[1536,768]{0,1:T(8,128)(2,1)}, u32[]{:S(2)}, u32[]{:S(2)}) collective-permute-start(bf16[1536,768]{0,1:T(8,128)(2,1)} %convolution_convert_fusion.5), channel_id=1, source_target_pairs={{0,1},{1,0},{2,3},{3,2},{4,5},{5,4},{6,7},{7,6},{8,9},{9,8},{10,11... | collective-permute-start | bytes 7077896 | tf_op jit(solution)/shard_map/ppermute | solution.py:530
  194.3 10.3 %copy-start.47 = (bf16[1536,1536]{1,0:T(8,128)(2,1)S(1)}, bf16[1536,1536]{1,0:T(8,128)(2,1)}, u32[]{:S(2)}) copy-start(bf16[1536,1536]{1,0:T(8,128)(2,1)} %copy-done.46) | copy-start | bytes 14155780
  194.3 17.3 %slice-start = ((s8[4718592]{0:T(1024)(128)(4,1)}), s8[4194304]{0:T(1024)(128)(4,1)S(1)}, s32[]{:S(2)}) async-start(s8[4718592]{0:T(1024)(128)(4,1)} %bitcast.77), calls=%async_computation | async-start | bytes 8388608
  194.3 17.3 %slice-start.2 = ((s8[4718592]{0:T(1024)(128)(4,1)}), s8[4194304]{0:T(1024)(128)(4,1)S(1)}, s32[]{:S(2)}) async-start(s8[4718592]{0:T(1024)(128)(4,1)} %bitcast.79), calls=%async_computation.2 | async-start | bytes 8388608
  204.6 7.0 %slice-start.1 = ((s8[4718592]{0:T(1024)(128)(4,1)}), s8[524288]{0:T(1024)(128)(4,1)S(1)}, s32[]{:S(2)}) async-start(s8[4718592]{0:T(1024)(128)(4,1)} %bitcast.77), calls=%async_computation.1 | async-start | bytes 1048576
  204.6 7.0 %slice-start.3 = ((s8[4718592]{0:T(1024)(128)(4,1)}), s8[524288]{0:T(1024)(128)(4,1)S(1)}, s32[]{:S(2)}) async-start(s8[4718592]{0:T(1024)(128)(4,1)} %bitcast.79), calls=%async_computation.3 | async-start | bytes 1048576
  219.5 37.1 %copy-start.32 = (f32[1536]{0:T(1024)}, f32[1536]{0:T(1024)S(1)}, u32[]{:S(2)}) copy-start(f32[1536]{0:T(1024)S(1)} %negate_multiply_fusion.1) | copy-start | bytes 18436
  220.2 5.2 %copy-start.1 = (bf16[1536,1152]{1,0:T(8,128)(2,1)S(1)}, bf16[1536,1152]{1,0:T(8,128)(2,1)}, u32[]{:S(2)}) copy-start(bf16[1536,1152]{1,0:T(8,128)(2,1)} %copy-done) | copy-start | bytes 10616836
  220.2 5.2 %copy-start.3 = (f32[1536,384]{1,0:T(8,128)S(1)}, f32[1536,384]{1,0:T(8,128)}, u32[]{:S(2)}) copy-start(f32[1536,384]{1,0:T(8,128)} %copy-done.2) | copy-start | bytes 7077892
  220.2 5.2 %copy-start.6 = (f32[1,384]{1,0:T(1,128)S(1)}, f32[1,384]{1,0:T(1,128)}, u32[]{:S(2)}) copy-start(f32[1,384]{1,0:T(1,128)} %copy-done.5) | copy-start | bytes 4612
  246.9 1.8 copy-start.7
  248.8 7.8 %copy-start.10 = (bf16[1536,384]{1,0:T(8,128)(2,1)S(1)}, bf16[1536,384]{1,0:T(8,128)(2,1)}, u32[]{:S(2)}) copy-start(bf16[1536,384]{1,0:T(8,128)(2,1)} %copy-done.9) | copy-start | bytes 3538948
  256.2 5.6 %copy-start.8 = (bf16[1536,1152]{1,0:T(8,128)(2,1)S(1)}, bf16[1536,1152]{1,0:T(8,128)(2,1)}, u32[]{:S(2)}) copy-start(bf16[1536,1152]{1,0:T(8,128)(2,1)} %copy-done.7) | copy-start | bytes 10616836
  256.2 5.6 %copy-start.18 = (bf16[1536,768]{1,0:T(8,128)(2,1)S(1)}, bf16[1536,768]{1,0:T(8,128)(2,1)}, u32[]{:S(2)}) copy-start(bf16[1536,768]{1,0:T(8,128)(2,1)} %param.22) | copy-start | bytes 7077892
  256.2 114.8 %collective-permute-start.3 = (bf16[1536,768]{0,1:T(8,128)(2,1)}, bf16[1536,768]{0,1:T(8,128)(2,1)}, u32[]{:S(2)}, u32[]{:S(2)}) collective-permute-start(bf16[1536,768]{0,1:T(8,128)(2,1)} %convolution_convert_fusion.4), channel_id=1, source_target_pairs={{0,1},{1,0},{2,3},{3,2},{4,5},{5,4},{6,7},{7,6},{8,9},{9,8},{10,11... | collective-permute-start | bytes 7077896 | tf_op jit(solution)/shard_map/ppermute | solution.py:530
  265.0 97.4 %copy-start.16 = (f32[1536,48]{0,1:T(8,128)S(1)}, f32[1536,48]{0,1:T(8,128)}, u32[]{:S(2)}) copy-start(f32[1536,48]{0,1:T(8,128)} %param.38) | copy-start | bytes 884740
  354.0 17.1 %copy-start.14 = (bf16[1536,768]{0,1:T(8,128)(2,1)S(1)}, bf16[1536,768]{0,1:T(8,128)(2,1)}, u32[]{:S(2)}) copy-start(bf16[1536,768]{0,1:T(8,128)(2,1)} %copy-done.13) | copy-start | bytes 7077892
  354.6 13.8 %copy-start.38 = (f32[6]{0:T(128)S(1)}, f32[6]{0:T(128)}, u32[]{:S(2)}) copy-start(f32[6]{0:T(128)} %reduce_sum.311) | copy-start | bytes 76
  371.0 12.1 %copy-start.33 = (f32[5632]{0:T(1024)S(1)}, f32[5632]{0:T(1024)}, u32[]{:S(2)}) copy-start(f32[5632]{0:T(1024)} %constant_dynamic-update-slice_fusion.4) | copy-start | bytes 67588
  371.0 14.8 %copy-start.30 = (f32[3072]{0:T(1024)S(1)}, f32[3072]{0:T(1024)}, u32[]{:S(2)}) copy-start(f32[3072]{0:T(1024)} %reshape.199) | copy-start | bytes 36868
  371.0 26.2 %copy-start.34 = (f32[4,48]{1,0:T(4,128)S(1)}, f32[4,48]{1,0:T(4,128)}, u32[]{:S(2)}) copy-start(f32[4,48]{1,0:T(4,128)} %param.41) | copy-start | bytes 2308
  371.0 26.2 %copy-start.35 = (f32[4,48]{1,0:T(4,128)S(1)}, f32[4,48]{1,0:T(4,128)}, u32[]{:S(2)}) copy-start(f32[4,48]{1,0:T(4,128)} %param.42) | copy-start | bytes 2308
  371.0 26.2 %copy-start.36 = (f32[4,48]{1,0:T(4,128)S(1)}, f32[4,48]{1,0:T(4,128)}, u32[]{:S(2)}) copy-start(f32[4,48]{1,0:T(4,128)} %param.43) | copy-start | bytes 2308
  417.1 7.6 %copy-start.22 = (f32[1536,48]{0,1:T(8,128)S(1)}, f32[1536,48]{0,1:T(8,128)}, u32[]{:S(2)}) copy-start(f32[1536,48]{0,1:T(8,128)} %get-tuple-element.317) | copy-start | bytes 884740
  417.1 7.6 %copy-start.23 = (f32[1536,48]{0,1:T(8,128)S(1)}, f32[1536,48]{0,1:T(8,128)}, u32[]{:S(2)}) copy-start(f32[1536,48]{0,1:T(8,128)} %get-tuple-element.318) | copy-start | bytes 884740
  417.1 8.5 %copy-start.17 = (f32[48,1536]{1,0:T(8,128)S(1)}, f32[48,1536]{1,0:T(8,128)}, u32[]{:S(2)}) copy-start(f32[48,1536]{1,0:T(8,128)} %param.35) | copy-start | bytes 884740
  417.1 8.5 %copy-start.20 = (f32[48,1536]{1,0:T(8,128)S(1)}, f32[48,1536]{1,0:T(8,128)}, u32[]{:S(2)}) copy-start(f32[48,1536]{1,0:T(8,128)} %get-tuple-element.312) | copy-start | bytes 884740
  417.1 8.5 %copy-start.21 = (f32[48,1536]{1,0:T(8,128)S(1)}, f32[48,1536]{1,0:T(8,128)}, u32[]{:S(2)}) copy-start(f32[48,1536]{1,0:T(8,128)} %get-tuple-element.313) | copy-start | bytes 884740
  417.1 9.4 %copy-start.26 = (f32[384,48]{0,1:T(8,128)S(1)}, f32[384,48]{0,1:T(8,128)}, u32[]{:S(2)}) copy-start(f32[384,48]{0,1:T(8,128)} %param.32) | copy-start | bytes 221188
  417.1 9.4 %copy-start.27 = (f32[384,48]{0,1:T(8,128)S(1)}, f32[384,48]{0,1:T(8,128)}, u32[]{:S(2)}) copy-start(f32[384,48]{0,1:T(8,128)} %get-tuple-element.307) | copy-start | bytes 221188
  417.2 9.4 %copy-start.28 = (f32[384,48]{0,1:T(8,128)S(1)}, f32[384,48]{0,1:T(8,128)}, u32[]{:S(2)}) copy-start(f32[384,48]{0,1:T(8,128)} %get-tuple-element.308) | copy-start | bytes 221188
  417.2 10.1 %copy-start.19 = (f32[48,3,384]{2,0,1:T(8,128)S(1)}, f32[48,3,384]{2,0,1:T(8,128)}, u32[]{:S(2)}) copy-start(f32[48,3,384]{2,0,1:T(8,128)} %param.29) | copy-start | bytes 663556
  417.2 10.0 %copy-start.24 = (f32[48,3,384]{2,0,1:T(8,128)S(1)}, f32[48,3,384]{2,0,1:T(8,128)}, u32[]{:S(2)}) copy-start(f32[48,3,384]{2,0,1:T(8,128)} %get-tuple-element.303) | copy-start | bytes 663556
  417.2 10.0 %copy-start.25 = (f32[48,3,384]{2,0,1:T(8,128)S(1)}, f32[48,3,384]{2,0,1:T(8,128)}, u32[]{:S(2)}) copy-start(f32[48,3,384]{2,0,1:T(8,128)} %get-tuple-element.302) | copy-start | bytes 663556

commit v2 on v1

v2 whole, which is shorter than its diff:
```python
import functools

import jax
import jax.numpy as jnp
from jax import lax
from jax.experimental import pallas as pl
from jax.experimental.pallas import tpu as pltpu
from jax.sharding import PartitionSpec as P

D = 768
HEAD_DIM = 64
ROW = 512
STEP_COUNT = 5

LN_EPS = 1e-05
LAMB_EPS = 1e-06
WEIGHT_DECAY = 0.01
LEARN_RATE = 0.5
MOMENT_DECAY = 0.5
MASK_FILL = -1000000000.0


MESH = pl.DeviceIdType.MESH
NZ, NY, NX = 4, 2, 2
GRID = NZ * NY * NX
CHUNKS = (
    (0, 0, 640, 0),
    (0, 640, 512, 1),
    (1, 0, 128, 0),
    (1, 128, 256, 1),
    (2, 0, 768, 0),
    (2, 768, 768, 1),
    (3, 0, 768, 0),
    (3, 768, 768, 1),
)
NORM_CHUNK = (4, 0, 128, 0)


def place(me):
    return me // (NY * NX), (me // NX) % NY, me % NX


def index(z, y, x):
    return (z * NY + y) * NX + x


def relative(z, y, x, rz, ra, rb, order):
    zz = lax.rem(z + rz, NZ)
    flip_x, flip_y = (ra, rb) if order == 0 else (rb, ra)
    return index(zz, 1 - y if flip_y else y, 1 - x if flip_x else x)


def slot(rz, ra, rb):
    return rz + NZ * (ra + 2 * rb)


def greet(peers):
    barrier = pltpu.get_barrier_semaphore()
    for peer in peers:
        pl.semaphore_signal(barrier, inc=1, device_id=peer, device_id_type=MESH)
    pl.semaphore_wait(barrier, len(peers))


def grid_peers(z, y, x, core):
    ahead = [index(lax.rem(z + d, NZ), y, x) for d in (1, 2, 3)]
    beside = [index(z, y, 1 - x), index(z, 1 - y, x)]
    return [(p, core) for p in ahead + beside]


def gather_kernel(rows, count, *refs):
    chunks_here = (*CHUNKS, NORM_CHUNK)
    src, dst = refs[:count], refs[count : 2 * count]
    local_sem, send_sem, recv_sem = refs[2 * count :]
    me, core = lax.axis_index("dp"), lax.axis_index("head")
    z, y, x = place(me)
    greet(grid_peers(z, y, x, core))

    def rows_of(device):
        return pl.ds(pl.multiple_of(device * rows, rows), rows)

    def copy(c, rz, ra, rb, to, there, k, own=False):
        p, first, width, order = chunks_here[c]
        device = relative(z, y, x, rz, ra, rb, order)
        columns = pl.ds(first, width)
        source = src[p].at[:, columns] if own else dst[p].at[rows_of(device), columns]
        return pltpu.make_async_remote_copy(
            src_ref=source,
            dst_ref=dst[p].at[rows_of(device), columns],
            send_sem=send_sem.at[c, k],
            recv_sem=recv_sem.at[c, there],
            device_id=(to, core),
            device_id_type=MESH,
        )

    def arrived(c, rz, ra, rb):
        copy(c, rz, ra, rb, me, slot(rz, ra, rb), 0).wait_recv()

    sends = []

    def send(*args, **kwargs):
        one = copy(*args, **kwargs)
        one.start()
        sends.append(one)

    kept = [
        pltpu.make_async_copy(src[p], dst[p].at[rows_of(me)], local_sem.at[p]) for p in range(count)
    ]
    for one in kept:
        one.start()
    chunks = range(len(chunks_here))
    along = [
        (index(z, y, 1 - x), index(z, 1 - y, x))[:: 1 if chunks_here[c][3] == 0 else -1] for c in chunks
    ]
    for c in chunks:
        for i, dz in enumerate((1, 3, 2)):
            to = index(lax.rem(z + dz, NZ), y, x)
            send(c, 0, 0, 0, to, slot(NZ - dz, 0, 0), i, own=True)
        send(c, 0, 0, 0, along[c][0], slot(0, 1, 0), 3, own=True)
        send(c, 0, 0, 0, along[c][1], slot(0, 0, 1), 7, own=True)
    for pair in range(0, len(chunks_here), 2):
        both = chunks[pair : pair + 2]
        for c in both:
            for i, rz in enumerate((1, 3, 2)):
                arrived(c, rz, 0, 0)
                send(c, rz, 0, 0, along[c][0], slot(rz, 1, 0), 4 + i)
                send(c, rz, 0, 0, along[c][1], slot(rz, 0, 1), 8 + i)
        for c in both:
            for i, rz in enumerate((0, 1, 3, 2)):
                arrived(c, rz, 1, 0)
                send(c, rz, 1, 0, along[c][1], slot(rz, 1, 1), 11 + i)
    for c in chunks:
        for ra in (0, 1):
            for rz in range(NZ):
                arrived(c, rz, ra, 1)
    for one in sends:
        one.wait_send()
    for one in kept:
        one.wait()


def gather(shards):
    rows, count = shards[0].shape[0], len(shards)
    space = pl.BlockSpec(memory_space=pl.ANY)
    return pl.pallas_call(
        functools.partial(gather_kernel, rows, count),
        out_shape=[jax.ShapeDtypeStruct((rows * GRID, s.shape[1]), s.dtype) for s in shards],
        in_specs=[space] * count,
        out_specs=[space] * count,
        scratch_shapes=[
            pltpu.SemaphoreType.DMA((count,)),
            pltpu.SemaphoreType.DMA((len(CHUNKS) + 1, 15)),
            pltpu.SemaphoreType.DMA((len(CHUNKS) + 1, 16)),
        ],
        compiler_params=pltpu.CompilerParams(collective_id=0, has_side_effects=True),
        name="weights_gather",
    )(*shards)


NT = (((1,), (1,)), ((), ()))
NN = (((1,), (0,)), ((), ()))
PAIR = 2 * HEAD_DIM


def mul(a, b, dims=NN):
    return lax.dot_general(a, b, dims, preferred_element_type=jnp.float32)


def segments(lengths_ref, row, shape, axis):
    positions = lax.broadcasted_iota(jnp.int32, shape, axis)
    end = jnp.int32(0)
    found = jnp.zeros(shape, jnp.int32)
    for k in range(lengths_ref.shape[1]):
        end = end + lengths_ref[row, k]
        found = found + (positions >= end).astype(jnp.int32)
    return found


def flip(block):
    return jnp.transpose(block.astype(jnp.float32)).astype(block.dtype)


def head_lanes(block, head):
    lane = lax.broadcasted_iota(jnp.int32, block.shape, 1)
    inside = (lane < HEAD_DIM) if head == 0 else (lane >= HEAD_DIM)
    return jnp.where(inside, block, jnp.zeros_like(block))


def attention_kernel(lengths_ref, gate_ref, q_ref, k_ref, v_ref, mix_ref, context_ref, stats_ref):
    row = pl.program_id(0)
    same = segments(lengths_ref, row, (ROW, 1), 0) == segments(lengths_ref, row, (1, ROW), 1)
    queries = q_ref[...] * jnp.bfloat16(HEAD_DIM**-0.5)
    values_t = flip(v_ref[...])
    mixes = []
    for head in (0, 1):
        scores = mul(k_ref[...], head_lanes(queries, head), NT)
        scores = jnp.where(same, scores, MASK_FILL)
        top = jnp.max(scores, axis=0, keepdims=True)
        expo = jnp.exp(scores - top)
        total = jnp.sum(expo, axis=0, keepdims=True)
        probs = (expo * (1.0 / total)).astype(jnp.bfloat16)
        mixes.append(mul(values_t[head * HEAD_DIM : (head + 1) * HEAD_DIM], probs))
        stats_ref[0, 0, head : head + 1, :] = top + jnp.log(total)
    mix = jnp.transpose(jnp.concatenate(mixes, axis=0))
    mix_ref[...] = mix
    context_ref[...] = (mix * gate_ref[...]).astype(jnp.bfloat16)


def attention(qkv, lengths, gate_lanes):
    tokens, width = qkv.shape
    rows, pairs = lengths.shape[0], width // 3 // PAIR
    block = lambda part: pl.BlockSpec((ROW, PAIR), lambda r, h: (r, part * pairs + h))
    own = pl.BlockSpec((ROW, PAIR), lambda r, h: (r, h))
    return pl.pallas_call(
        attention_kernel,
        grid=(rows, pairs),
        in_specs=[
            pl.BlockSpec(memory_space=pltpu.SMEM),
            pl.BlockSpec((1, PAIR), lambda r, h: (0, h)),
            block(0),
            block(1),
            block(2),
        ],
        out_specs=[own, own, pl.BlockSpec((1, 1, 8, ROW), lambda r, h: (r, h, 0, 0))],
        out_shape=[
            jax.ShapeDtypeStruct((tokens, width // 3), jnp.float32),
            jax.ShapeDtypeStruct((tokens, width // 3), jnp.bfloat16),
            jax.ShapeDtypeStruct((rows, pairs, 8, ROW), jnp.float32),
        ],
        compiler_params=pltpu.CompilerParams(vmem_limit_bytes=32 << 20),
        cost_estimate=pl.CostEstimate(
            flops=4 * rows * pairs * 2 * ROW * ROW * HEAD_DIM,
            bytes_accessed=tokens * width * 4,
            transcendentals=rows * pairs * 2 * ROW * ROW,
        ),
        name="attention",
    )(lengths, gate_lanes, qkv, qkv, qkv)


def attend_back(same, gate, queries, keys, values, stats, d_context):
    queries = queries * jnp.bfloat16(HEAD_DIM**-0.5)
    keys_t = flip(keys)
    d_mix = (d_context * gate).astype(jnp.bfloat16)
    d_queries, d_keys, d_values = [], None, None
    for head in (0, 1):
        q_one, d_one = head_lanes(queries, head), head_lanes(d_mix, head)
        scores = jnp.where(same, mul(keys, q_one, NT), MASK_FILL)
        probs = jnp.exp(scores - stats[head : head + 1, :])
        d_probs = mul(values, d_one, NT)
        weighed = jnp.sum(probs * d_probs, axis=0, keepdims=True)
        d_scores = (probs * (d_probs - weighed)).astype(jnp.bfloat16)
        dv = mul(probs.astype(jnp.bfloat16), d_one)
        dk = mul(d_scores, q_one)
        d_values = dv if head == 0 else d_values + dv
        d_keys = dk if head == 0 else d_keys + dk
        d_queries.append(mul(keys_t[head * HEAD_DIM : (head + 1) * HEAD_DIM], d_scores))
    dq = jnp.transpose(jnp.concatenate(d_queries, axis=0)) * HEAD_DIM**-0.5
    return dq, d_keys, d_values


def attention_back_kernel(
    lengths_ref, gate_ref, q_ref, k_ref, v_ref, stats_ref, mix_ref, d_ref, out_ref, heads_ref
):
    row, pair = pl.program_id(0), pl.program_id(1)
    same = segments(lengths_ref, row, (ROW, 1), 0) == segments(lengths_ref, row, (1, ROW), 1)
    d_context = d_ref[...]
    heads_ref[0, 0] = jnp.broadcast_to(
        jnp.sum(d_context * mix_ref[...], axis=0, keepdims=True), (8, PAIR)
    )
    parts = attend_back(
        same, gate_ref[...], q_ref[...], k_ref[...], v_ref[...], stats_ref[0, 0], d_context
    )
    width = out_ref.shape[1] // 3
    for part, value in enumerate(parts):
        start = pl.multiple_of(part * width + pair * PAIR, PAIR)
        out_ref[:, pl.ds(start, PAIR)] = value.astype(jnp.bfloat16)


def attention_back(qkv, lengths, gate_lanes, stats, mix, d_context):
    tokens, width = qkv.shape
    rows, pairs = lengths.shape[0], width // 3 // PAIR
    block = lambda part: pl.BlockSpec((ROW, PAIR), lambda r, h: (r, part * pairs + h))
    own = pl.BlockSpec((ROW, PAIR), lambda r, h: (r, h))
    small = pl.BlockSpec((1, 1, 8, ROW), lambda r, h: (r, h, 0, 0))
    return pl.pallas_call(
        attention_back_kernel,
        grid=(rows, pairs),
        in_specs=[
            pl.BlockSpec(memory_space=pltpu.SMEM),
            pl.BlockSpec((1, PAIR), lambda r, h: (0, h)),
            block(0),
            block(1),
            block(2),
            small,
            own,
            own,
        ],
        out_specs=[
            pl.BlockSpec((ROW, width), lambda r, h: (r, 0)),
            pl.BlockSpec((1, 1, 8, PAIR), lambda r, h: (r, h, 0, 0)),
        ],
        out_shape=[
            jax.ShapeDtypeStruct((tokens, width), jnp.bfloat16),
            jax.ShapeDtypeStruct((rows, pairs, 8, PAIR), jnp.float32),
        ],
        compiler_params=pltpu.CompilerParams(vmem_limit_bytes=32 << 20),
        cost_estimate=pl.CostEstimate(
            flops=10 * rows * pairs * 2 * ROW * ROW * HEAD_DIM,
            bytes_accessed=tokens * width * 8,
            transcendentals=rows * pairs * 2 * ROW * ROW,
        ),
        name="attention_back",
    )(lengths, gate_lanes, qkv, qkv, qkv, stats, mix, d_context)


TILE = 256
PART = 256
TAIL_STEP = 0.3
TAIL = (
    0.11963200569152832,
    0.12071217596530914,
    0.10017567127943039,
    0.1276927888393402,
    -0.052036140114068985,
    0.2045592963695526,
    -0.15616002678871155,
    0.035424139350652695,
)


def normal_parts(u):
    bell = jnp.exp(-0.5 * u * u)
    t = 1.0 / (1.0 + TAIL_STEP * jnp.abs(u))
    series = TAIL[-1]
    for term in TAIL[-2::-1]:
        series = series * t + term
    tail = series * t * bell
    return jnp.where(u < 0, tail, 1.0 - tail), u * bell * 0.3989422804014327


def fold(block):
    return jnp.sum(block.reshape(-1, 8, block.shape[1]), axis=0)


def norm_back(d_out, normal, scale, gain):
    d_normal = d_out * gain
    d_normal = (
        d_normal
        - jnp.mean(d_normal, axis=-1, keepdims=True)
        - normal * jnp.mean(d_normal * normal, axis=-1, keepdims=True)
    )
    return d_normal * scale


def normalize(rows_in):
    center = rows_in - jnp.mean(rows_in, axis=-1, keepdims=True)
    scale = lax.rsqrt(jnp.mean(center * center, axis=-1, keepdims=True) + LN_EPS)
    return center * scale, scale


def ffn_kernel(
    lengths_ref,
    gates_ref,
    norm_ref,
    hidden_gate_ref,
    unit_gate_ref,
    context_ref,
    w_out_ref,
    tokens_hbm,
    teacher_hbm,
    w_in_hbm,
    w_fo_hbm,
    student_hbm,
    d_res1_hbm,
    d_context_hbm,
    grads_hbm,
    small_ref,
    w_in,
    w_fo,
    tokens,
    teacher,
    own1,
    own2,
    got1,
    got2,
    got3,
    normal1,
    scale1,
    gated,
    slope,
    d_res,
    d_context,
    hidden_t,
    d_ffn_t,
    d_attn_t,
    grad_wide,
    grad_out,
    sums,
    unit_sum,
    load_sem,
    tile_sem,
    grad_sem,
    send_sem,
    recv_sem,
):
    dp, core = lax.axis_index("dp"), lax.axis_index("head")
    loads = [
        pltpu.make_async_copy(source, target, load_sem.at[i])
        for i, (source, target) in enumerate(
            ((tokens_hbm, tokens), (w_in_hbm, w_in), (w_fo_hbm, w_fo), (teacher_hbm, teacher))
        )
    ]
    for one in loads:
        one.start()
    greet([(dp, 1 - core)])
    tiles = tokens.shape[0] // TILE
    units, width = w_in.shape[1], w_in.shape[0]
    sums[...] = jnp.zeros_like(sums)
    unit_sum[...] = jnp.zeros_like(unit_sum)
    hidden_gate = hidden_gate_ref[...]
    gate0, gate1 = hidden_gate * gates_ref[0], hidden_gate * gates_ref[1]
    gain1, bias1, gain2, bias2 = (norm_ref[i : i + 1, :] for i in range(4))

    def rows(t):
        return pl.ds(pl.multiple_of(t * TILE, TILE), TILE)

    def lanes(n):
        return pl.ds(n * PART, PART)

    def exchange(step, t):
        source, target = ((own1, got1), (own2, got2), (own2, got3))[step]
        return pltpu.make_async_remote_copy(
            src_ref=source.at[rows(t)],
            dst_ref=target.at[rows(t)],
            send_sem=send_sem.at[step, t],
            recv_sem=recv_sem.at[step, t],
            device_id=(dp, 1 - core),
            device_id_type=MESH,
        )

    def tile_copy(which, t):
        source, target = ((own1, student_hbm), (d_res, d_res1_hbm), (d_context, d_context_hbm))[
            which
        ]
        return pltpu.make_async_copy(
            source.at[rows(t)], target.at[rows(t)], tile_sem.at[which, t]
        )

    def phase1(t, _):
        part = mul(context_ref[rows(t)], w_out_ref[...], NT)
        own1[rows(t)] = part.astype(jnp.bfloat16)
        exchange(0, t).start()

    lax.fori_loop(0, tiles, phase1, None)
    loads[0].wait()
    loads[1].wait()
    loads[2].wait()

    def summed(source, target, t):
        return source[rows(t)].astype(jnp.float32) + target[rows(t)].astype(jnp.float32)

    def phase2(t, _):
        exchange(0, t).wait()
        rows_in = tokens[rows(t)].astype(jnp.float32) + summed(own1, got1, t) * gate0
        normal, scale = normalize(rows_in)
        normal1[rows(t)] = normal
        scale1[rows(t)] = scale
        hidden = normal * gain1 + bias1
        low = hidden.astype(jnp.bfloat16)
        hidden_t[:, rows(t)] = jnp.transpose(hidden).astype(jnp.bfloat16)
        for n in range(units // PART):
            up = mul(low, w_in[:, lanes(n)])
            below, density = normal_parts(up)
            gate = unit_gate_ref[:, lanes(n)]
            gated[rows(t), lanes(n)] = (up * below * gate).astype(jnp.bfloat16)
            slope[rows(t), lanes(n)] = ((below + density) * gate).astype(jnp.bfloat16)
        part = mul(gated[rows(t)], w_fo[...], NT)
        own2[rows(t)] = part.astype(jnp.bfloat16)
        exchange(1, t).start()

    lax.fori_loop(0, tiles, phase2, None)
    loads[3].wait()

    def phase3(t, _):
        exchange(1, t).wait()
        ffn = summed(own2, got2, t)
        hidden = normal1[rows(t)] * gain1 + bias1
        normal, scale = normalize(hidden + ffn * gate1)
        student = normal * gain2 + bias2
        student_tile = student.astype(jnp.bfloat16)
        got2[rows(t)] = student_tile
        row = t // (ROW // TILE)
        end = lengths_ref[row, 0]
        for k in range(1, lengths_ref.shape[1]):
            end = end + lengths_ref[row, k]
        position = lax.broadcasted_iota(jnp.int32, (TILE, 1), 0) + (t % (ROW // TILE)) * TILE
        valid = (position < end).astype(jnp.float32)
        d_out = valid * (student - teacher[rows(t)].astype(jnp.float32))
        d_res2 = norm_back(d_out, normal, scale, gain2)
        d_res[rows(t)] = d_res2
        sums[2] += fold(d_out * normal)
        sums[3] += fold(d_out)
        sums[5] += fold(d_res2 * ffn)
        d_ffn = d_res2 * gate1
        d_ffn_t[:, rows(t)] = jnp.transpose(d_ffn).astype(jnp.bfloat16)
        d_ffn = d_ffn.astype(jnp.bfloat16)
        for n in range(units // PART):
            d_gated = mul(d_ffn, w_fo[:, lanes(n)])
            unit_sum[:, lanes(n)] += fold(
                d_gated * gated[rows(t), lanes(n)].astype(jnp.float32)
            )
            d_up = d_gated * slope[rows(t), lanes(n)].astype(jnp.float32)
            slope[rows(t), lanes(n)] = d_up.astype(jnp.bfloat16)
        part = mul(slope[rows(t)], w_in[...], NT)
        own2[rows(t)] = part.astype(jnp.bfloat16)
        exchange(2, t).start()
        pltpu.make_async_copy(
            got2.at[rows(t)], student_hbm.at[rows(t)], tile_sem.at[0, t]
        ).start()

    lax.fori_loop(0, tiles, phase3, None)

    def wide(which, n):
        target = grads_hbm.at[:, pl.ds(which * units + n * PART, PART)]
        return pltpu.make_async_copy(
            grad_wide.at[which, :, lanes(n)], target, grad_sem.at[which, n]
        )

    for n in range(units // PART):
        grad_wide[0, :, lanes(n)] = mul(d_ffn_t[...], gated[:, lanes(n)]).astype(jnp.bfloat16)
        wide(0, n).start()

    def phase4(t, _):
        exchange(2, t).wait()
        normal = normal1[rows(t)]
        d_hidden = d_res[rows(t)] + summed(own2, got3, t)
        sums[0] += fold(d_hidden * normal)
        sums[1] += fold(d_hidden)
        d_res1 = norm_back(d_hidden, normal, scale1[rows(t)], gain1)
        d_res[rows(t)] = d_res1
        tile_copy(1, t).start()
        sums[4] += fold(d_res1 * summed(own1, got1, t))
        d_attn = d_res1 * gate0
        d_attn_t[:, rows(t)] = jnp.transpose(d_attn).astype(jnp.bfloat16)
        d_context[rows(t)] = mul(d_attn.astype(jnp.bfloat16), w_out_ref[...])
        tile_copy(2, t).start()

    lax.fori_loop(0, tiles, phase4, None)
    for n in range(units // PART):
        grad_wide[1, :, lanes(n)] = mul(hidden_t[...], slope[:, lanes(n)]).astype(jnp.bfloat16)
        wide(1, n).start()
    grad_out[...] = mul(d_attn_t[...], context_ref[...]).astype(jnp.bfloat16)
    last = pltpu.make_async_copy(
        grad_out, grads_hbm.at[:, pl.ds(2 * units, grad_out.shape[1])], grad_sem.at[2, 0]
    )
    last.start()

    def line(i):
        return jnp.sum(sums[i], axis=0, keepdims=True)

    for i in range(4):
        small_ref[i : i + 1, :] = line(i)
    attn_line, ffn_line = line(4), line(5)
    small_ref[4:5, :] = ffn_line * gates_ref[1] + attn_line * gates_ref[0]
    unit_line = jnp.sum(unit_sum[...], axis=0, keepdims=True) / unit_gate_ref[...]
    for i in range(units // width):
        small_ref[5 + i : 6 + i, :] = unit_line[:, i * width : (i + 1) * width]
    lane = lax.broadcasted_iota(jnp.int32, (1, width), 1)
    layer0 = jnp.sum(attn_line * hidden_gate, axis=1, keepdims=True)
    layer1 = jnp.sum(ffn_line * hidden_gate, axis=1, keepdims=True)
    small_ref[7:8, :] = jnp.where(lane == 128, layer0, jnp.where(lane == 129, layer1, 0.0))

    def finish(t, _):
        pltpu.make_async_copy(
            got2.at[rows(t)], student_hbm.at[rows(t)], tile_sem.at[0, t]
        ).wait()
        tile_copy(1, t).wait()
        tile_copy(2, t).wait()

    lax.fori_loop(0, tiles, finish, None)
    for n in range(units // PART):
        wide(0, n).wait()
        wide(1, n).wait()
    last.wait()


def ffn(lengths, layer_gates, norm_p, hidden_gate, unit_gate, context, w_out_t, tokens, teacher, w_in, w_fo_t):
    count, width = tokens.shape
    units, heads = w_in.shape[1], context.shape[1]
    tiles = count // TILE
    vmem, smem = pl.BlockSpec(memory_space=pltpu.VMEM), pl.BlockSpec(memory_space=pltpu.SMEM)
    anywhere = pl.BlockSpec(memory_space=pl.ANY)
    low, full = jnp.bfloat16, jnp.float32
    return pl.pallas_call(
        ffn_kernel,
        in_specs=[smem, smem] + [vmem] * 5 + [anywhere] * 4,
        out_specs=[anywhere] * 4 + [vmem],
        out_shape=[
            jax.ShapeDtypeStruct((count, width), low),
            jax.ShapeDtypeStruct((count, width), full),
            jax.ShapeDtypeStruct((count, heads), full),
            jax.ShapeDtypeStruct((width, 2 * units + heads), low),
            jax.ShapeDtypeStruct((8, width), full),
        ],
        scratch_shapes=[
            pltpu.VMEM((width, units), low),
            pltpu.VMEM((width, units), low),
            pltpu.VMEM((count, width), low),
            pltpu.VMEM((count, width), low),
            *[pltpu.VMEM((count, width), low)] * 5,
            pltpu.VMEM((count, width), full),
            pltpu.VMEM((count, 1), full),
            pltpu.VMEM((count, units), low),
            pltpu.VMEM((count, units), low),
            pltpu.VMEM((count, width), full),
            pltpu.VMEM((count, heads), full),
            *[pltpu.VMEM((width, count), low)] * 3,
            pltpu.VMEM((2, width, units), low),
            pltpu.VMEM((width, heads), low),
            pltpu.VMEM((6, 8, width), full),
            pltpu.VMEM((8, units), full),
            pltpu.SemaphoreType.DMA((4,)),
            pltpu.SemaphoreType.DMA((3, tiles)),
            pltpu.SemaphoreType.DMA((3, units // PART)),
            pltpu.SemaphoreType.DMA((3, tiles)),
            pltpu.SemaphoreType.DMA((3, tiles)),
        ],
        compiler_params=pltpu.CompilerParams(
            collective_id=4, has_side_effects=True, vmem_limit_bytes=60 << 20
        ),
        name="ffn",
    )(lengths, layer_gates, norm_p, hidden_gate[None, :], unit_gate[None, :], context, w_out_t, tokens, teacher, w_in, w_fo_t)


def lamb_moments(master, first, second, grad, decay):
    new_first = MOMENT_DECAY * first + (1.0 - MOMENT_DECAY) * grad
    new_second = MOMENT_DECAY * second + (1.0 - MOMENT_DECAY) * grad * grad
    correction = 1.0 - MOMENT_DECAY**STEP_COUNT
    update = (
        new_first / correction / (jnp.sqrt(new_second / correction) + LAMB_EPS) + decay * master
    )
    return (new_first, new_second, update)


BLOCK = 384


def tail_kernel(
    lengths_ref,
    gate_ref,
    small_ref,
    stats_ref,
    norms_ref,
    *refs,
):
    params, refs = refs[:12], refs[12:]
    (
        grads_hbm,
        qkv_hbm,
        mix_hbm,
        d_context_hbm,
        tokens_hbm,
        w_qkv_hbm,
        d_res1_hbm,
        grad_tokens_hbm,
        sums_ref,
        small_out,
        norm_out,
        total_out,
        grads,
        qkv,
        mix,
        d_context,
        tokens,
        w_qkv,
        d_res,
        d_qkv,
        tokens_t,
        own,
        got,
        heads,
        get1,
        put2,
        get2,
        keep,
        put3,
        get3,
        small_plane,
        small_mine,
        small_line,
        norm_plane,
        norm_mine,
        norm_line,
        load_sem,
        out_sem,
        own_send,
        own_recv,
        send_sem,
        recv_sem,
        small_send,
        small_recv,
    ) = refs
    me, core = lax.axis_index("dp"), lax.axis_index("head")
    z, y, x = place(me)
    rows = sums_ref.shape[0]
    early, blocks = grads_hbm.shape[1] // BLOCK, sums_ref.shape[1] // BLOCK
    loads = [
        pltpu.make_async_copy(source, target, load_sem.at[i])
        for i, (source, target) in enumerate(
            (
                (grads_hbm, grads.at[:, : early * BLOCK]),
                (qkv_hbm, qkv),
                (d_context_hbm, d_context),
                (mix_hbm, mix),
                (tokens_hbm, tokens),
                (w_qkv_hbm, w_qkv),
                (d_res1_hbm, d_res),
            )
        )
    ]
    for one in loads:
        one.start()
    line_peers = [index(lax.rem(z + d, NZ), y, x) for d in (1, 2, 3)]
    plane_peers = [
        index(z, y + (1 - 2 * y) * (d // 2), x + (1 - 2 * x) * (d % 2)) for d in (0, 1, 2, 3)
    ]
    greet(
        [(p, core) for p in line_peers + plane_peers[1:]] + [(p, 1 - core) for p in plane_peers]
    )

    def rows_of(device):
        return pl.ds(pl.multiple_of(device * rows, rows), rows)

    def columns(c):
        return pl.ds(pl.multiple_of(c * BLOCK, BLOCK), BLOCK)

    def turned(c, rz, ra, rb):
        odd = c % 2
        flip_x = ra * (1 - odd) + rb * odd
        flip_y = rb * (1 - odd) + ra * odd
        return index(lax.rem(z + rz, NZ), y + (1 - 2 * y) * flip_y, x + (1 - 2 * x) * flip_x)

    def remote(source, target, c, k, to):
        return pltpu.make_async_remote_copy(
            src_ref=source,
            dst_ref=target,
            send_sem=send_sem.at[c, k],
            recv_sem=recv_sem.at[c, k],
            device_id=(to, core),
            device_id_type=MESH,
        )

    depth = (1, 3, 2, 0)

    def leg1(c, k):
        block = rows_of(turned(c, k % NZ, k // NZ, 1))
        return remote(grads.at[block, columns(c)], get1.at[c, k], c, k, turned(c, 0, 0, 1))

    def leg2(c, rz):
        return remote(put2.at[c, rz], get2.at[c, rz], c, 8 + rz, turned(c, 0, 1, 0))

    def leg3(c, rz):
        there = NZ - rz
        to = index(lax.rem(z + rz, NZ), y, x)
        return remote(put3.at[c, rz - 1], get3.at[c, there - 1], c, 11 + there, to)

    def first(c):
        for ra in (1, 0):
            for rz in depth:
                leg1(c, rz + NZ * ra).start()

    def second(c):
        for ra in (1, 0):
            for rz in depth:
                k = rz + NZ * ra
                leg1(c, k).wait_recv()
                block = rows_of(turned(c, rz, ra, 0))
                total = grads[block, columns(c)].astype(jnp.float32) + get1[c, k].astype(
                    jnp.float32
                )
                if ra:
                    put2[c, rz] = total.astype(jnp.bfloat16)
                    leg2(c, rz).start()
                else:
                    keep[c, rz] = total

    def third(c):
        for rz in depth:
            leg2(c, rz).wait_recv()
            total = keep[c, rz] + get2[c, rz].astype(jnp.float32)
            if rz:
                put3[c, rz - 1] = total.astype(jnp.bfloat16)
                leg3(c, rz).start()
            else:
                keep[c, 0] = total

    def last(c):
        total = keep[c, 0]
        for rz in (1, 2, 3):
            leg3(c, rz).wait_recv()
        for at in range(3):
            total = total + get3[c, at].astype(jnp.float32)
        sums_ref[:, columns(c)] = total

    def each(action, begin, end):
        lax.fori_loop(begin, end, lambda c, _: action(c), None)

    heads[...] = jnp.zeros_like(heads)
    loads[0].wait()
    each(first, 0, 4)
    for one in loads[1:]:
        one.wait()

    def exchange(r):
        here = pl.ds(pl.multiple_of(r * ROW, ROW), ROW)
        return pltpu.make_async_remote_copy(
            src_ref=own.at[here],
            dst_ref=got.at[here],
            send_sem=own_send.at[r],
            recv_sem=own_recv.at[r],
            device_id=(me, 1 - core),
            device_id_type=MESH,
        )

    width = qkv.shape[1] // 3

    def attend(r, _):
        here = pl.ds(pl.multiple_of(r * ROW, ROW), ROW)
        same = segments(lengths_ref, r, (ROW, 1), 0) == segments(lengths_ref, r, (1, ROW), 1)
        tokens_t[:, here] = jnp.transpose(tokens[here].astype(jnp.float32)).astype(jnp.bfloat16)
        for pair in range(width // PAIR):
            lanes = slice(pair * PAIR, (pair + 1) * PAIR)
            heads[:, lanes] += fold(d_context[here, lanes] * mix[here, lanes])
            parts = attend_back(
                same,
                gate_ref[:, lanes],
                *(qkv[here, part * width + pair * PAIR : part * width + (pair + 1) * PAIR] for part in range(3)),
                stats_ref[r, pair],
                d_context[here, lanes],
            )
            for part, value in enumerate(parts):
                start = part * width + pair * PAIR
                d_qkv[here, start : start + PAIR] = value.astype(jnp.bfloat16)
        part = mul(d_qkv[here], w_qkv[...], NT)
        own[here] = part.astype(jnp.bfloat16)
        exchange(r).start()
        each(second, 2 * r, 2 * r + 2)
        each(first, 2 * r + 4, jnp.minimum(2 * r + 6, early))

        @pl.when(r > 0)
        def _():
            each(third, 2 * r - 2, 2 * r)

        @pl.when(r > 1)
        def _():
            each(last, 2 * r - 4, 2 * r - 2)

    tall = tokens.shape[0] // ROW
    lax.fori_loop(0, tall, attend, None)

    def weigh(c, _):
        part = pl.ds(pl.multiple_of((c - early) * BLOCK, BLOCK), BLOCK)
        grads[:, columns(c)] = mul(tokens_t[...], d_qkv[:, part]).astype(jnp.bfloat16)
        first(c)

    lax.fori_loop(early, blocks, weigh, None)

    here_plane = y * NX + x
    small_plane[here_plane] = small_ref[...]
    line = jnp.sum(heads[...], axis=0, keepdims=True)
    lane = lax.broadcasted_iota(jnp.int32, (1, small_ref.shape[1]), 1)
    extra = small_ref[7:8, :]
    for head in range(width // HEAD_DIM):
        value = jnp.sum(line[:, head * HEAD_DIM : (head + 1) * HEAD_DIM], axis=1, keepdims=True)
        extra = jnp.where(lane == head, value, extra)
    small_plane[here_plane, 7:8, :] = extra

    def spread(plane, base, to, to_core, at):
        return pltpu.make_async_remote_copy(
            src_ref=plane.at[at],
            dst_ref=plane.at[at],
            send_sem=small_send.at[base],
            recv_sem=small_recv.at[base],
            device_id=(to, to_core),
            device_id_type=MESH,
        )

    def swap(plane, base, targets, at):
        copies = [
            spread(plane, base + i, to, to_core, at) for i, (to, to_core) in enumerate(targets)
        ]
        for one in copies:
            one.start()
        return copies

    sent = swap(small_plane, 0, [(p, core) for p in plane_peers[1:]], here_plane)
    each(second, 2 * tall, early)
    each(third, 2 * tall - 2, 2 * tall)
    each(last, 2 * tall - 4, 2 * tall - 2)
    each(third, 2 * tall, early)

    def finish(r, _):
        here = pl.ds(pl.multiple_of(r * ROW, ROW), ROW)
        exchange(r).wait()
        d_res[here] += own[here].astype(jnp.float32) + got[here].astype(jnp.float32)
        pltpu.make_async_copy(d_res.at[here], grad_tokens_hbm.at[here], out_sem.at[r]).start()

    lax.fori_loop(0, tall, finish, None)
    for one in sent:
        one.wait_recv()
    total = small_plane[0]
    for at in range(1, NX * NY):
        total = total + small_plane[at]
    small_line[z] = total
    sent_line = swap(small_line, 3, [(p, core) for p in line_peers], z)
    each(second, early, blocks)
    each(last, 2 * tall - 2, early)
    for one in sent_line:
        one.wait_recv()
    total = small_line[0]
    for at in range(1, NZ):
        total = total + small_line[at]
    small_out[...] = total
    norm_grad = pltpu.roll(total, (total.shape[1] - me * rows) % total.shape[1], 1)[:, :128]
    norm_out[...] = norm_grad
    each(third, early, blocks)

    row8 = lax.broadcasted_iota(jnp.int32, (8, 128), 0)
    lane8 = lax.broadcasted_iota(jnp.int32, (8, 128), 1)

    def put(tile, row, weight, update):
        here = row8 == row
        return jnp.where(here & (lane8 == 0), weight, jnp.where(here & (lane8 == 1), update, tile))

    def square(block):
        return jnp.sum(jnp.sum(block * block, axis=0, keepdims=True), axis=1, keepdims=True)

    tile = jnp.zeros((8, 128), jnp.float32)
    master, first_moment, second_moment = (norms_ref[i] for i in range(3))
    update = lamb_moments(master, first_moment, second_moment, norm_grad[:4, : master.shape[1]], 0.0)[2]
    for i in range(4):
        tile = put(tile, 4 + i, 0.5 * square(master[i : i + 1]), 0.5 * square(update[i : i + 1]))
    start = 0
    for row, p in ((3, 3), (2, 2), (1, 1)):
        master = params[p][...]
        span = slice(start, start + master.shape[1])
        update = lamb_moments(master, params[4 + p][...], params[8 + p][...], sums_ref[:, span], WEIGHT_DECAY)[2]
        tile = put(tile, row, square(master), square(update))
        start += master.shape[1]
    weights, updates = 0.0, 0.0
    each(last, early, blocks)
    for j in range(3):
        master = params[0][j]
        span = slice(start + j * width, start + (j + 1) * width)
        update = lamb_moments(master, params[4][j], params[8][j], sums_ref[:, span], WEIGHT_DECAY)[2]
        weights, updates = weights + square(master), updates + square(update)
    tile = put(tile, 0, weights, updates)
    here_cores = core * (NX * NY) + here_plane
    norm_plane[here_cores] = tile
    targets = [(p, core) for p in plane_peers[1:]] + [(p, 1 - core) for p in plane_peers]
    sent_tile = swap(norm_plane, 6, targets, here_cores)
    for one in sent_tile:
        one.wait_recv()
    total = norm_plane[0]
    for at in range(1, 2 * NX * NY):
        total = total + norm_plane[at]
    norm_line[z] = total
    sent_last = swap(norm_line, 13, [(p, core) for p in line_peers], z)
    for one in sent_last:
        one.wait_recv()
    total = norm_line[0]
    for at in range(1, NZ):
        total = total + norm_line[at]
    total_out[...] = total
    for one in (*sent, *sent_line, *sent_tile, *sent_last):
        one.wait_send()

    def drain(c, _):
        for k in range(8):
            leg1(c, k).wait_send()
        for rz in range(NZ):
            leg2(c, rz).wait_send()
        for rz in (1, 2, 3):
            leg3(c, rz).wait_send()

    lax.fori_loop(0, blocks, drain, None)

    def drain_rows(r, _):
        here = pl.ds(pl.multiple_of(r * ROW, ROW), ROW)
        pltpu.make_async_copy(d_res.at[here], grad_tokens_hbm.at[here], out_sem.at[r]).wait()

    lax.fori_loop(0, tall, drain_rows, None)


def tail(lengths, gate_lanes, small_rows, stats, norms, params, grads, qkv, mix, d_context, tokens, w_qkv, d_res1):
    count, width = tokens.shape
    heads3, rows = qkv.shape[1], norms.shape[2]
    columns = grads.shape[1] + heads3
    tall, blocks = count // ROW, columns // BLOCK
    vmem, smem = pl.BlockSpec(memory_space=pltpu.VMEM), pl.BlockSpec(memory_space=pltpu.SMEM)
    anywhere = pl.BlockSpec(memory_space=pl.ANY)
    low, full = jnp.bfloat16, jnp.float32
    landing = lambda n, kind: pltpu.VMEM((blocks, n, rows, BLOCK), kind)
    return pl.pallas_call(
        tail_kernel,
        in_specs=[smem] + [vmem] * (4 + len(params)) + [anywhere] * 7,
        out_specs=[anywhere] + [vmem] * 4,
        out_shape=[
            jax.ShapeDtypeStruct((count, width), full),
            jax.ShapeDtypeStruct((rows, columns), full),
            jax.ShapeDtypeStruct((8, width), full),
            jax.ShapeDtypeStruct((8, 128), full),
            jax.ShapeDtypeStruct((8, 128), full),
        ],
        scratch_shapes=[
            pltpu.VMEM((width, columns), low),
            pltpu.VMEM((count, heads3), low),
            pltpu.VMEM((count, heads3 // 3), full),
            pltpu.VMEM((count, heads3 // 3), full),
            pltpu.VMEM((count, width), low),
            pltpu.VMEM((width, heads3), low),
            pltpu.VMEM((count, width), full),
            pltpu.VMEM((count, heads3), low),
            pltpu.VMEM((width, count), low),
            pltpu.VMEM((count, width), low),
            pltpu.VMEM((count, width), low),
            pltpu.VMEM((8, heads3 // 3), full),
            landing(8, low),
            landing(NZ, low),
            landing(NZ, low),
            landing(NZ, full),
            landing(3, low),
            landing(3, low),
            pltpu.VMEM((NX * NY, 8, width), full),
            pltpu.VMEM((8, width), full),
            pltpu.VMEM((NZ, 8, width), full),
            pltpu.VMEM((2 * NX * NY, 8, 128), full),
            pltpu.VMEM((8, 128), full),
            pltpu.VMEM((NZ, 8, 128), full),
            pltpu.SemaphoreType.DMA((7,)),
            pltpu.SemaphoreType.DMA((tall,)),
            pltpu.SemaphoreType.DMA((tall,)),
            pltpu.SemaphoreType.DMA((tall,)),
            pltpu.SemaphoreType.DMA((blocks, 15)),
            pltpu.SemaphoreType.DMA((blocks, 15)),
            pltpu.SemaphoreType.DMA((16,)),
            pltpu.SemaphoreType.DMA((16,)),
        ],
        compiler_params=pltpu.CompilerParams(
            collective_id=5, has_side_effects=True, vmem_limit_bytes=61 << 20
        ),
        name="tail",
    )(lengths, gate_lanes, small_rows, stats, norms, *params, grads, qkv, mix, d_context, tokens, w_qkv, d_res1)


def update_kernel(order, sums_ref, small_ref, norm_ref, total_ref, norms_ref, *refs):
    params, outs = refs[:12], refs[12:]
    weight_norm = jnp.sqrt(total_ref[:, 0:1])
    update_norm = jnp.sqrt(total_ref[:, 1:2])
    trust = weight_norm / update_norm

    def step(row, targets, at, values, decay):
        master, first_moment, second_moment, grad = values
        new_first, new_second, update = lamb_moments(
            master, first_moment, second_moment, grad, decay
        )
        new_master = master - LEARN_RATE * trust[row] * update
        made = (grad, new_first, new_second, new_master, new_master.astype(jnp.bfloat16))
        for target, value in zip(targets, made, strict=True):
            target[at] = value

    start = 0
    for p in order:
        master = params[p]
        width = master.shape[-1]
        targets = outs[5 * p : 5 * p + 5]
        for j in range(3 if p == 0 else 1):
            at = (j,) if p == 0 else (Ellipsis,)
            grad = sums_ref[:, start : start + width]
            values = (*(params[4 * i + p][at] for i in range(3)), grad)
            step(slice(p, p + 1), targets, at, values, WEIGHT_DECAY)
            start += width
    norm_grad = norm_ref[:4, : norms_ref.shape[2]]
    values = (*(norms_ref[i] for i in range(3)), norm_grad)
    step(slice(4, 8), outs[20:25], (Ellipsis,), values, 0.0)
    stats_out, heads_out, units_out, hidden_out, layers_out = outs[25:]
    lane = lax.broadcasted_iota(jnp.int32, (8, 128), 1)
    stats_out[...] = jnp.where(lane == 0, weight_norm, jnp.where(lane == 1, update_norm, trust))
    heads_out[...] = small_ref[7:8, : heads_out.shape[1]]
    width = small_ref.shape[1]
    for i in range(units_out.shape[1] // width):
        units_out[:, i * width : (i + 1) * width] = small_ref[5 + i : 6 + i, :]
    hidden_out[...] = small_ref[4:5, :]
    layers_out[...] = small_ref[7:8, 128:130]


def update(sums, small, norm_grad, totals, norms, params, sizes):
    vmem = pl.BlockSpec(memory_space=pltpu.VMEM)
    shapes = []
    for master in params[:4]:
        shapes += [jax.ShapeDtypeStruct(master.shape, jnp.float32)] * 4
        shapes += [jax.ShapeDtypeStruct(master.shape, jnp.bfloat16)]
    shapes += [jax.ShapeDtypeStruct(norms.shape[1:], jnp.float32)] * 4
    shapes += [jax.ShapeDtypeStruct(norms.shape[1:], jnp.bfloat16)]
    shapes += [jax.ShapeDtypeStruct((8, 128), jnp.float32)]
    shapes += [jax.ShapeDtypeStruct((1, size), jnp.float32) for size in sizes]
    return pl.pallas_call(
        functools.partial(update_kernel, (3, 2, 1, 0)),
        in_specs=[vmem] * (5 + len(params)),
        out_specs=[vmem] * len(shapes),
        out_shape=shapes,
        compiler_params=pltpu.CompilerParams(vmem_limit_bytes=48 << 20),
        name="update",
    )(sums, small, norm_grad, totals, norms, *params)


def core_sum(part):
    part = part.astype(jnp.bfloat16)
    other = lax.ppermute(part, "head", [(0, 1), (1, 0)])
    return part.astype(jnp.float32) + other.astype(jnp.float32)


def plain_totals(sums, norm_grad, norms, params, head_count):
    pairs, start = [None] * 4, 0
    for p in (3, 2, 1, 0):
        master, first_moment, second_moment = params[p], params[4 + p], params[8 + p]
        width = master.size // norms.shape[2]
        grad = sums[:, start : start + width]
        if p == 0:
            grad = jnp.stack(jnp.split(grad, 3, axis=1))
        update = lamb_moments(master, first_moment, second_moment, grad, WEIGHT_DECAY)[2]
        pairs[p] = jnp.stack([jnp.sum(master * master), jnp.sum(update * update)])
        start += width
    master, first_moment, second_moment = norms
    update = lamb_moments(master, first_moment, second_moment, norm_grad[:4, : norms.shape[2]], 0.0)[2]
    rows = jnp.stack([jnp.sum(master * master, axis=1), jnp.sum(update * update, axis=1)], axis=1)
    found = jnp.concatenate([jnp.stack(pairs), rows / head_count])
    return jnp.pad(lax.psum(found, ("dp", "head")), ((0, 0), (0, 126)))


def rows_first(qkv):
    return jnp.transpose(qkv, (1, 0, 2))


def local(
    tokens,
    teacher,
    lengths,
    head_gate,
    unit_gate,
    hidden_gate,
    layer_gates,
    master_qkv,
    first_qkv,
    second_qkv,
    master_attn_out,
    first_attn_out,
    second_attn_out,
    master_ffn_in,
    first_ffn_in,
    second_ffn_in,
    master_ffn_out,
    first_ffn_out,
    second_ffn_out,
    master_norms,
    first_norms,
    second_norms,
):
    heads_here = head_gate.shape[0]
    local_width = heads_here * HEAD_DIM
    head_count = lax.axis_size("head")
    ours = lax.axis_size("dp") == GRID and head_count == 2
    shard = master_qkv.shape[0]
    shards = [
        master_qkv.astype(jnp.bfloat16).reshape(shard, 3 * local_width),
        master_attn_out.T.astype(jnp.bfloat16),
        master_ffn_in.astype(jnp.bfloat16),
        master_ffn_out.T.astype(jnp.bfloat16),
        jnp.pad(master_norms.T, ((0, 0), (0, 124))).astype(jnp.bfloat16),
    ]
    if ours:
        w_qkv, w_out_t, w_in, w_fo_t, norm_t = gather(shards)
    else:
        w_qkv, w_out_t, w_in, w_fo_t, norm_t = (
            lax.all_gather(s, "dp", axis=0, tiled=True) for s in shards
        )
    norm_p = norm_t[:, :4].T.astype(jnp.float32)
    gate_lanes = jnp.repeat(head_gate, HEAD_DIM)[None, :]
    qkv = jnp.dot(tokens, w_qkv, preferred_element_type=jnp.float32).astype(jnp.bfloat16)
    head_mix, context, stats = attention(qkv, lengths, gate_lanes)
    student_low, d_res1, d_context, grads, small_rows = ffn(
        lengths,
        layer_gates,
        norm_p,
        hidden_gate,
        unit_gate,
        context,
        w_out_t,
        tokens,
        teacher,
        w_in,
        w_fo_t,
    )
    params = [
        rows_first(master_qkv),
        master_attn_out.T,
        master_ffn_in,
        master_ffn_out.T,
        rows_first(first_qkv),
        first_attn_out.T,
        first_ffn_in,
        first_ffn_out.T,
        rows_first(second_qkv),
        second_attn_out.T,
        second_ffn_in,
        second_ffn_out.T,
    ]
    norms = jnp.stack([master_norms, first_norms, second_norms])
    if ours:
        grad_tokens, sums, small, norm_grad, totals = tail(
            lengths,
            gate_lanes,
            small_rows,
            stats,
            norms,
            params,
            grads,
            qkv,
            head_mix,
            d_context,
            tokens,
            w_qkv,
            d_res1,
        )
    else:
        d_qkv, head_sums = attention_back(qkv, lengths, gate_lanes, stats, head_mix, d_context)
        d_heads = jnp.sum(
            head_sums[:, :, 0, :].reshape(-1, heads_here, HEAD_DIM), axis=(0, 2)
        )
        grad_qkv = jnp.einsum("tc,tk->ck", tokens, d_qkv, preferred_element_type=jnp.float32)
        input_part = jnp.einsum("tk,ck->tc", d_qkv, w_qkv, preferred_element_type=jnp.float32)
        grad_tokens = d_res1 + core_sum(input_part)
        grads = jnp.concatenate([grads.astype(jnp.float32), grad_qkv], axis=1)
        sums = lax.psum_scatter(grads, "dp", scatter_dimension=0, tiled=True)
        small = lax.psum(small_rows.at[7, :heads_here].set(d_heads), "dp")
        start = lax.axis_index("dp") * shard
        norm_grad = lax.dynamic_slice_in_dim(small, start, shard, 1)
        norm_grad = jnp.pad(norm_grad, ((0, 0), (0, 128 - shard)))
        totals = plain_totals(sums, norm_grad, norms, params, head_count)
    made = update(
        sums, small, norm_grad, totals, norms, params, (heads_here, unit_gate.shape[0], D, 2)
    )
    results = []
    for p in range(4):
        for value in made[5 * p : 5 * p + 5]:
            results.append(rows_first(value) if p == 0 else value if p == 2 else value.T)
    norm_results, (stats_rows, *gate_rows) = made[20:25], made[25:]
    gate_results = [row.reshape(-1) for row in gate_rows]
    return (
        student_low,
        grad_tokens,
        *gate_results,
        *results,
        *norm_results,
        stats_rows[:, :3].T,
    )


def solution(mesh):
    return jax.shard_map(
        local,
        mesh=mesh,
        in_specs=(
            P("dp", None),
            P("dp", None),
            P("dp", None),
            P("head"),
            P("head"),
            P(),
            P(),
            P("dp", None, "head"),
            P("dp", None, "head"),
            P("dp", None, "head"),
            P("head", "dp"),
            P("head", "dp"),
            P("head", "dp"),
            P("dp", "head"),
            P("dp", "head"),
            P("dp", "head"),
            P("head", "dp"),
            P("head", "dp"),
            P("head", "dp"),
            P(None, "dp"),
            P(None, "dp"),
            P(None, "dp"),
        ),
        out_specs=(
            P("dp", None),
            P("dp", None),
            P("head"),
            P("head"),
            P(),
            P(),
            P("dp", None, "head"),
            P("dp", None, "head"),
            P("dp", None, "head"),
            P("dp", None, "head"),
            P("dp", None, "head"),
            P("head", "dp"),
            P("head", "dp"),
            P("head", "dp"),
            P("head", "dp"),
            P("head", "dp"),
            P("dp", "head"),
            P("dp", "head"),
            P("dp", "head"),
            P("dp", "head"),
            P("dp", "head"),
            P("head", "dp"),
            P("head", "dp"),
            P("head", "dp"),
            P("head", "dp"),
            P("head", "dp"),
            P(None, "dp"),
            P(None, "dp"),
            P(None, "dp"),
            P(None, "dp"),
            P(None, "dp"),
            P(),
        ),
        check_vma=False,
    )
```

time: 439 us -> 269 us (0.61); the launches traced: 430 us -> 269 us
  matrix products: 98.1 us -> 5.43 us
  other arithmetic: 63.9 us -> 8.84 us
  local copies, waits for them, and re-layouts: 41.8 us -> 17.2 us
  Pallas kernels: 220 us -> 236 us
    dot_general x11 -> x0, matrix products: 92.7 us -> none  [the longest x1 28.1 us: local(): up_proj = jnp.dot(hidden_low, w_in, preferred_element_type=jnp.float32)]
    reduce_sum x18 -> x0, other arithmetic: 50.1 us -> none  [the longest x4 16.8 us: layer_norm(): center = rows_in - jnp.mean(rows_in, axis=-1, keepdims=True)]
    pallas_call x4 -> x3, Pallas kernels: 133 us -> 149 us  [the longest x1 91.8 us: tail(): pl.pallas_call(tail_kernel, in_specs=[smem] + [vmem] * (4 + len(params))...]
    unnamed x113 -> x61, local copies, waits for them, and re-layouts: 28.6 us -> 12.7 us
    concatenate x3 -> x0, local copies, waits for them, and re-layouts: 5.99 us -> none  [the longest x1 3.32 us: local(): jnp.concatenate([jnp.stack([jnp.sum(master_qkv * master_qkv), jnp.sum(mas...]
  transfers between devices with their start and end apart: 4 -> 0, of which waited for: 1 -> 0; matrix products, arithmetic and copies ran while one was open for 13% -> 0% of each run, Pallas kernels for 21% -> 0%
where the time goes in v2:
time: 269 us
  Pallas kernels  236 us (88%)
  local copies, waits for them, and re-layouts  17.2 us (6%)
  other arithmetic  8.84 us (3%)
  matrix products  5.43 us (2%)
    pallas_call x1, Pallas kernels, tail(): pl.pallas_call(tail_kernel, in_specs=[smem] + [vmem] * (4 + len(params))...  91.8 us
    pallas_call x1, Pallas kernels, gather(): pl.pallas_call(functools.partial(gather_kernel, rows, count), out_shape=[...  72.3 us
    pallas_call x1, Pallas kernels, ffn(): pl.pallas_call(ffn_kernel, in_specs=[smem, smem] + [vmem] * 5 + [anywhere...  54.2 us
    pallas_call x1, Pallas kernels, attention(): pl.pallas_call(attention_kernel, grid=(rows, pairs), in_specs=[pl.BlockSp...  15.1 us
    unnamed x61, local copies, waits for them, and re-layouts  12.7 us
    dot_general x1, matrix products, local(): jnp.dot(tokens, w_qkv, preferred_element_type=jnp.float32)  5.43 us

profile of v2, /device:TPU:0, one launch (start us, length us, event | category | flops | bytes accessed | tf_op | source)
XLA Modules:
  0.0 268.8 jit_solution(15544106677714892321)
XLA Ops:
  0.7 1.0 convert_bitcast_fusion
  1.6 0.7 copy.65
  2.3 1.6 bitcast_convert_fusion.refs_3_
  3.9 1.6 convert_element_type.27.refs_2_
  5.6 1.5 bitcast_convert_fusion.1.refs_1_
  7.1 0.7 convert.6
  7.7 0.1 copy.60
  7.9 0.6 pad.5.refs_4_
  8.5 72.3 %weights_gather.1 = (bf16[768,1152]{1,0:T(8,128)(2,1)}, bf16[768,384]{1,0:T(8,128)(2,1)}, bf16[768,1536]{1,0:T(8,128)(2,1)}, bf16[768,1536]{1,0:T(8,128)(2,1)}, bf16[768,128]{1,0:T(8,128)(2,1)}) custom-call(bf16[48,1152]{1,0:T(8,128)(2,1)} %bitcast.61, bf16[48,384]{1,0:T(8,128)(2,1)} %bitcast_convert_fusion.1.refs_1_, ...), custom_call_target="tpu_custom_call" | custom-call | tf_op jit(solution)/shard_map/weights_gather/pallas_call | solution.py:144
  80.7 0.0 copy-start.28
  80.8 0.0 copy-start.19
  80.8 5.4 %fusion.q_ref.k_ref.v_ref.refs_13_ = bf16[1536,1152]{1,0:T(8,128)(2,1)S(1)} fusion(bf16[1536,768]{1,0:T(8,128)(2,1)} %refs_16_.1, bf16[768,1152]{1,0:T(8,128)(2,1)} %get-tuple-element.81.refs_17_), kind=kOutput, calls=%fused_computation.1 | convolution fusion | flops 2719678464 | bytes 7667712 | tf_op jit(solution)/shard_map/dot_general | solution.py:1188
  86.2 0.0 copy-done.28
  86.2 0.0 copy-start
  86.2 0.1 broadcast_in_dim.11
  86.3 0.1 broadcast_in_dim_reshape.3.gate_ref
  86.4 0.0 copy-done.19
  86.4 15.1 %attention.1 = (f32[1536,384]{1,0:T(8,128)S(1)}, bf16[1536,384]{1,0:T(8,128)(2,1)S(1)}, f32[3,3,8,512]{3,2,1,0:T(8,128)S(1)}) custom-call(s32[3,6]{1,0:T(4,128)S(1)} %copy-done.19, f32[1,384]{1,0:T(1,128)S(1)} %broadcast_in_dim_reshape.3.gate_ref, bf16[1536,1152]{1,0:T(8,128)(2,1)S(1)} %fusion.q_ref.k_ref.v_ref.refs_13_, ...), custom_call_target="tpu_custom_call" | custom-call | flops 1207959552 | bytes 7077888 | tf_op jit(solution)/shard_map/attention/pallas_call | solution.py:213
  101.5 0.0 copy-done
  101.5 0.0 copy-done.20
  101.6 0.0 copy-start.3
  101.6 1.4 copy-done.3
  103.0 1.1 copy-done.5
  104.0 0.7 copy-done.16
  104.7 1.1 copy.61
  105.8 0.6 convert_bitcast_fusion.1.norm_ref
  106.4 0.0 copy-done.24
  106.4 0.6 broadcast_in_dim.10.unit_gate_ref
  107.0 1.3 broadcast_in_dim.9.hidden_gate_ref
  108.2 54.2 %ffn.1 = (bf16[1536,768]{1,0:T(8,128)(2,1)}, f32[1536,768]{1,0:T(8,128)}, f32[1536,384]{1,0:T(8,128)}, bf16[768,3456]{1,0:T(8,128)(2,1)}, f32[8,768]{1,0:T(8,128)}) custom-call(s32[3,6]{1,0:T(4,128)} %lengths_ref.5, f32[2]{0:T(128)} %gates_ref.1, f32[4,768]{1,0:T(4,128)} %convert_bitcast_fusion.1.norm_ref, f32[1,768]{1,0:T(1,128)} %broadcast_in_dim.9.hidden_gate_ref, ...), custom_call_target="tpu_custom_call" | custom-call | tf_op jit(solution)/shard_map/ffn/pallas_call | solution.py:593
  162.5 0.0 copy-done.25
  162.5 0.0 copy-done.26
  162.5 0.0 copy-done.27
  162.5 0.6 pad_maximum_fusion.norms_ref
  163.1 0.0 copy-start.7
  163.1 0.0 copy-start.8
  163.2 0.0 copy-start.9
  163.2 0.0 copy-start.10
  163.2 0.0 copy-start.11
  163.2 0.0 copy-start.13
  163.2 0.0 copy-start.14
  163.2 0.0 copy-start.15
  163.2 0.0 copy-start.17
  163.2 91.8 %tail.1 = (f32[1536,768]{1,0:T(8,128)}, f32[48,4608]{1,0:T(8,128)}, f32[8,768]{1,0:T(8,128)}, f32[8,128]{1,0:T(8,128)}, f32[8,128]{1,0:T(8,128)}) custom-call(s32[3,6]{1,0:T(4,128)} %lengths_ref.5, f32[1,384]{1,0:T(1,128)} %copy-done.20, f32[8,768]{1,0:T(8,128)} %get-tuple-element.87.small_ref, f32[3,3,8,512]{3,2,1,0:T(8,128)} %copy-done.16, ...), custom_call_target="tpu_custom_call" | custom-call | tf_op jit(solution)/shard_map/tail/pallas_call | solution.py:1003
  255.0 0.0 copy-done.1
  255.0 0.0 copy-done.2
  255.0 0.0 copy-done.4
  255.0 0.0 copy-done.6
  255.0 0.0 copy-done.7
  255.1 0.0 copy-done.8
  255.1 0.0 copy-done.9
  255.1 0.0 copy-done.10
  255.1 0.0 copy-done.11
  255.1 1.2 copy-done.12
  256.3 0.7 copy-done.18
  257.0 0.7 copy-done.21
  257.7 0.7 copy-done.22
  258.4 2.9 %update.1 = (f32[3,48,384]{2,1,0:T(8,128)}, f32[3,48,384]{2,1,0:T(8,128)}, f32[3,48,384]{2,1,0:T(8,128)}, f32[3,48,384]{2,1,0:T(8,128)}, bf16[3,48,384]{2,1,0:T(...) custom-call(f32[48,4608]{1,0:T(8,128)S(1)} %copy-done.12, ...), custom_call_target="tpu_custom_call" | custom-call | tf_op jit(solution)/shard_map/update/pallas_call | solution.py:1106
  261.3 0.6 reduce
  261.9 0.7 copy.63
  262.6 0.6 reduce.1
  263.2 3.4 %copy.68 = bf16[1536,768]{1,0:T(8,128)(2,1)} copy(bf16[1536,768]{1,0:T(8,128)(2,1)} %get-tuple-element.224) | data formatting | bytes 4718592
  266.5 0.0 copy-done.23
  266.6 2.2 copy.69
  (21 shorter events, 0.0 us)
Async XLA Ops:
  80.7 5.5 %copy-start.28 = (f32[6]{0:T(128)S(1)}, f32[6]{0:T(128)}, u32[]{:S(2)}) copy-start(f32[6]{0:T(128)} %param.25) | copy-start | bytes 76
  80.8 5.6 %copy-start.19 = (s32[3,6]{1,0:T(4,128)S(1)}, s32[3,6]{1,0:T(4,128)}, u32[]{:S(2)}) copy-start(s32[3,6]{1,0:T(4,128)} %lengths_ref.5) | copy-start | bytes 220
  86.2 15.3 %copy-start = (bf16[1536,1152]{1,0:T(8,128)(2,1)}, bf16[1536,1152]{1,0:T(8,128)(2,1)S(1)}, u32[]{:S(2)}) copy-start(bf16[1536,1152]{1,0:T(8,128)(2,1)S(1)} %fusion.q_ref.k_ref.v_ref.refs_13_) | copy-start | bytes 10616836
  86.4 15.2 %copy-start.20 = (f32[1,384]{1,0:T(1,128)}, f32[1,384]{1,0:T(1,128)S(1)}, u32[]{:S(2)}) copy-start(f32[1,384]{1,0:T(1,128)S(1)} %broadcast_in_dim_reshape.3.gate_ref) | copy-start | bytes 4612
  86.4 20.0 %copy-start.24 = (f32[1536]{0:T(1024)S(1)}, f32[1536]{0:T(1024)}, u32[]{:S(2)}) copy-start(f32[1536]{0:T(1024)} %param.26) | copy-start | bytes 18436
  101.6 1.4 copy-start.3
  103.0 1.1 copy-start.5
  104.0 0.7 copy-start.16
  108.2 54.3 %copy-start.25 = (f32[4,48]{1,0:T(4,128)S(1)}, f32[4,48]{1,0:T(4,128)}, u32[]{:S(2)}) copy-start(f32[4,48]{1,0:T(4,128)} %param.41) | copy-start | bytes 2308
  108.2 54.3 %copy-start.26 = (f32[4,48]{1,0:T(4,128)S(1)}, f32[4,48]{1,0:T(4,128)}, u32[]{:S(2)}) copy-start(f32[4,48]{1,0:T(4,128)} %param.43) | copy-start | bytes 2308
  108.2 54.3 %copy-start.27 = (f32[4,48]{1,0:T(4,128)S(1)}, f32[4,48]{1,0:T(4,128)}, u32[]{:S(2)}) copy-start(f32[4,48]{1,0:T(4,128)} %param.42) | copy-start | bytes 2308
  163.1 91.9 %copy-start.1 = (f32[48,1536]{1,0:T(8,128)S(1)}, f32[48,1536]{1,0:T(8,128)}, u32[]{:S(2)}) copy-start(f32[48,1536]{1,0:T(8,128)} %refs_2_.3) | copy-start | bytes 884740
  163.1 91.9 %copy-start.2 = (f32[1536,48]{0,1:T(8,128)S(1)}, f32[1536,48]{0,1:T(8,128)}, u32[]{:S(2)}) copy-start(f32[1536,48]{0,1:T(8,128)} %param.38) | copy-start | bytes 884740
  163.1 91.9 %copy-start.4 = (f32[48,3,384]{2,0,1:T(8,128)S(1)}, f32[48,3,384]{2,0,1:T(8,128)}, u32[]{:S(2)}) copy-start(f32[48,3,384]{2,0,1:T(8,128)} %param.29) | copy-start | bytes 663556
  163.1 91.9 %copy-start.6 = (f32[48,1536]{1,0:T(8,128)S(1)}, f32[48,1536]{1,0:T(8,128)}, u32[]{:S(2)}) copy-start(f32[48,1536]{1,0:T(8,128)} %refs_6_.3) | copy-start | bytes 884740
  163.1 91.9 %copy-start.7 = (f32[1536,48]{0,1:T(8,128)S(1)}, f32[1536,48]{0,1:T(8,128)}, u32[]{:S(2)}) copy-start(f32[1536,48]{0,1:T(8,128)} %param.39) | copy-start | bytes 884740
  163.1 91.9 %copy-start.8 = (f32[48,1536]{1,0:T(8,128)S(1)}, f32[48,1536]{1,0:T(8,128)}, u32[]{:S(2)}) copy-start(f32[48,1536]{1,0:T(8,128)} %refs_10_.3) | copy-start | bytes 884740
  163.2 91.9 %copy-start.9 = (f32[1536,48]{0,1:T(8,128)S(1)}, f32[1536,48]{0,1:T(8,128)}, u32[]{:S(2)}) copy-start(f32[1536,48]{0,1:T(8,128)} %param.40) | copy-start | bytes 884740
  163.2 91.9 %copy-start.10 = (f32[48,3,384]{2,0,1:T(8,128)S(1)}, f32[48,3,384]{2,0,1:T(8,128)}, u32[]{:S(2)}) copy-start(f32[48,3,384]{2,0,1:T(8,128)} %param.30) | copy-start | bytes 663556
  163.2 91.9 %copy-start.11 = (f32[48,3,384]{2,0,1:T(8,128)S(1)}, f32[48,3,384]{2,0,1:T(8,128)}, u32[]{:S(2)}) copy-start(f32[48,3,384]{2,0,1:T(8,128)} %param.31) | copy-start | bytes 663556
  163.2 91.9 %copy-start.13 = (f32[384,48]{0,1:T(8,128)S(1)}, f32[384,48]{0,1:T(8,128)}, u32[]{:S(2)}) copy-start(f32[384,48]{0,1:T(8,128)} %param.32) | copy-start | bytes 221188
  163.2 91.9 %copy-start.14 = (f32[384,48]{0,1:T(8,128)S(1)}, f32[384,48]{0,1:T(8,128)}, u32[]{:S(2)}) copy-start(f32[384,48]{0,1:T(8,128)} %param.33) | copy-start | bytes 221188
  163.2 91.9 %copy-start.15 = (f32[384,48]{0,1:T(8,128)S(1)}, f32[384,48]{0,1:T(8,128)}, u32[]{:S(2)}) copy-start(f32[384,48]{0,1:T(8,128)} %param.34) | copy-start | bytes 221188
  163.2 91.9 %copy-start.17 = (f32[3,4,48]{2,1,0:T(4,128)S(1)}, f32[3,4,48]{2,1,0:T(4,128)}, u32[]{:S(2)}) copy-start(f32[3,4,48]{2,1,0:T(4,128)} %pad_maximum_fusion.norms_ref) | copy-start | bytes 6916
  255.1 1.2 copy-start.12
  256.3 0.7 copy-start.18
  257.0 0.7 copy-start.21
  257.7 0.7 copy-start.22
  263.2 3.4 %copy-start.23 = (f32[1536,768]{1,0:T(8,128)S(1)}, f32[1536,768]{1,0:T(8,128)}, u32[]{:S(2)}) copy-start(f32[1536,768]{1,0:T(8,128)} %get-tuple-element.225) | copy-start | bytes 14155780

commit v3 on v2

v3 whole, which is shorter than its diff:
```python
import functools

import jax
import jax.numpy as jnp
from jax import lax
from jax.experimental import pallas as pl
from jax.experimental.pallas import tpu as pltpu
from jax.sharding import PartitionSpec as P

D = 768
HEAD_DIM = 64
ROW = 512
STEP_COUNT = 5

LN_EPS = 1e-05
LAMB_EPS = 1e-06
WEIGHT_DECAY = 0.01
LEARN_RATE = 0.5
MOMENT_DECAY = 0.5
MASK_FILL = -1000000000.0


MESH = pl.DeviceIdType.MESH
NZ, NY, NX = 4, 2, 2
GRID = NZ * NY * NX


def place(me):
    return me // (NY * NX), (me // NX) % NY, me % NX


def index(z, y, x):
    return (z * NY + y) * NX + x


def slot(rz, ra, rb):
    return rz + NZ * (ra + 2 * rb)


def greet(peers):
    barrier = pltpu.get_barrier_semaphore()
    for peer in peers:
        pl.semaphore_signal(barrier, inc=1, device_id=peer, device_id_type=MESH)
    pl.semaphore_wait(barrier, len(peers))


NT = (((1,), (1,)), ((), ()))
NN = (((1,), (0,)), ((), ()))
PAIR = 2 * HEAD_DIM


def mul(a, b, dims=NN):
    return lax.dot_general(a, b, dims, preferred_element_type=jnp.float32)


def segments(lengths_ref, row, shape, axis):
    positions = lax.broadcasted_iota(jnp.int32, shape, axis)
    end = jnp.int32(0)
    found = jnp.zeros(shape, jnp.int32)
    for k in range(lengths_ref.shape[1]):
        end = end + lengths_ref[row, k]
        found = found + (positions >= end).astype(jnp.int32)
    return found


def flip(block):
    return jnp.transpose(block.astype(jnp.float32)).astype(block.dtype)


def head_lanes(block, head):
    lane = lax.broadcasted_iota(jnp.int32, block.shape, 1)
    inside = (lane < HEAD_DIM) if head == 0 else (lane >= HEAD_DIM)
    return jnp.where(inside, block, jnp.zeros_like(block))


def attend_pair(same, queries, keys, values):
    queries = queries * jnp.bfloat16(HEAD_DIM**-0.5)
    values_t = flip(values)
    mixes, totals = [], []
    for head in (0, 1):
        scores = mul(keys, head_lanes(queries, head), NT)
        scores = jnp.where(same, scores, MASK_FILL)
        top = jnp.max(scores, axis=0, keepdims=True)
        expo = jnp.exp(scores - top)
        total = jnp.sum(expo, axis=0, keepdims=True)
        probs = (expo * (1.0 / total)).astype(jnp.bfloat16)
        mixes.append(mul(values_t[head * HEAD_DIM : (head + 1) * HEAD_DIM], probs))
        totals.append(top + jnp.log(total))
    return jnp.transpose(jnp.concatenate(mixes, axis=0)), totals


def attend_back(same, queries, keys, values, stats, d_mix):
    queries = queries * jnp.bfloat16(HEAD_DIM**-0.5)
    keys_t = flip(keys)
    d_queries, d_keys, d_values, sums = [], None, None, []
    for head in (0, 1):
        q_one, d_one = head_lanes(queries, head), head_lanes(d_mix, head)
        scores = jnp.where(same, mul(keys, q_one, NT), MASK_FILL)
        probs = jnp.exp(scores - stats[head : head + 1, :])
        d_probs = mul(values, d_one, NT)
        weighed = jnp.sum(probs * d_probs, axis=0, keepdims=True)
        sums.append(jnp.sum(weighed, axis=1, keepdims=True))
        d_scores = (probs * (d_probs - weighed)).astype(jnp.bfloat16)
        dv = mul(probs.astype(jnp.bfloat16), d_one)
        dk = mul(d_scores, q_one)
        d_values = dv if head == 0 else d_values + dv
        d_keys = dk if head == 0 else d_keys + dk
        d_queries.append(mul(keys_t[head * HEAD_DIM : (head + 1) * HEAD_DIM], d_scores))
    dq = jnp.transpose(jnp.concatenate(d_queries, axis=0)) * HEAD_DIM**-0.5
    return (dq, d_keys, d_values), sums


def attention_kernel(lengths_ref, gate_ref, qkv_ref, context_ref, stats_ref):
    row = pl.program_id(0)
    same = segments(lengths_ref, row, (ROW, 1), 0) == segments(lengths_ref, row, (1, ROW), 1)
    mix, totals = attend_pair(same, *(qkv_ref[:, i * PAIR : (i + 1) * PAIR] for i in range(3)))
    for head in (0, 1):
        stats_ref[0, 0, head : head + 1, :] = totals[head]
    context_ref[...] = (mix * gate_ref[...]).astype(jnp.bfloat16)


def attention(qkv, lengths, gate_lanes):
    tokens, width = qkv.shape
    rows, pairs = lengths.shape[0], width // 3 // PAIR
    return pl.pallas_call(
        attention_kernel,
        grid=(rows, pairs),
        in_specs=[
            pl.BlockSpec(memory_space=pltpu.SMEM),
            pl.BlockSpec((1, PAIR), lambda r, h: (0, h)),
            pl.BlockSpec((ROW, 3 * PAIR), lambda r, h: (r, h)),
        ],
        out_specs=[
            pl.BlockSpec((ROW, PAIR), lambda r, h: (r, h)),
            pl.BlockSpec((1, 1, 8, ROW), lambda r, h: (r, h, 0, 0)),
        ],
        out_shape=[
            jax.ShapeDtypeStruct((tokens, width // 3), jnp.bfloat16),
            jax.ShapeDtypeStruct((rows, pairs, 8, ROW), jnp.float32),
        ],
        compiler_params=pltpu.CompilerParams(vmem_limit_bytes=32 << 20),
        name="attention",
    )(lengths, gate_lanes, qkv)


def attention_back_kernel(lengths_ref, gate_ref, qkv_ref, stats_ref, d_ref, out_ref, heads_ref):
    row = pl.program_id(0)
    same = segments(lengths_ref, row, (ROW, 1), 0) == segments(lengths_ref, row, (1, ROW), 1)
    gate = gate_ref[...]
    d_mix = (d_ref[...] * gate).astype(jnp.bfloat16)
    parts, weighed = attend_back(
        same, *(qkv_ref[:, i * PAIR : (i + 1) * PAIR] for i in range(3)), stats_ref[0, 0], d_mix
    )
    for i, value in enumerate(parts):
        out_ref[:, i * PAIR : (i + 1) * PAIR] = value.astype(jnp.bfloat16)
    lane = lax.broadcasted_iota(jnp.int32, (8, PAIR), 1)
    found = jnp.zeros((8, PAIR), jnp.float32)
    for head in (0, 1):
        value = weighed[head] / gate[:, head * HEAD_DIM : head * HEAD_DIM + 1]
        found = jnp.where(lane == head, value, found)
    heads_ref[0, 0] = found


def attention_back(qkv, lengths, gate_lanes, stats, d_context):
    tokens, width = qkv.shape
    rows, pairs = lengths.shape[0], width // 3 // PAIR
    wide = pl.BlockSpec((ROW, 3 * PAIR), lambda r, h: (r, h))
    return pl.pallas_call(
        attention_back_kernel,
        grid=(rows, pairs),
        in_specs=[
            pl.BlockSpec(memory_space=pltpu.SMEM),
            pl.BlockSpec((1, PAIR), lambda r, h: (0, h)),
            wide,
            pl.BlockSpec((1, 1, 8, ROW), lambda r, h: (r, h, 0, 0)),
            pl.BlockSpec((ROW, PAIR), lambda r, h: (r, h)),
        ],
        out_specs=[wide, pl.BlockSpec((1, 1, 8, PAIR), lambda r, h: (r, h, 0, 0))],
        out_shape=[
            jax.ShapeDtypeStruct((tokens, width), jnp.bfloat16),
            jax.ShapeDtypeStruct((rows, pairs, 8, PAIR), jnp.float32),
        ],
        compiler_params=pltpu.CompilerParams(vmem_limit_bytes=32 << 20),
        name="attention_back",
    )(lengths, gate_lanes, qkv, stats, d_context)


TILE = 256
PART = 256
TAIL_STEP = 0.3
TAIL = (
    0.11963200569152832,
    0.12071217596530914,
    0.10017567127943039,
    0.1276927888393402,
    -0.052036140114068985,
    0.2045592963695526,
    -0.15616002678871155,
    0.035424139350652695,
)


def normal_parts(u):
    bell = jnp.exp(-0.5 * u * u)
    t = 1.0 / (1.0 + TAIL_STEP * jnp.abs(u))
    series = TAIL[-1]
    for term in TAIL[-2::-1]:
        series = series * t + term
    tail = series * t * bell
    return jnp.where(u < 0, tail, 1.0 - tail), u * bell * 0.3989422804014327


def fold(block):
    return jnp.sum(block.reshape(-1, 8, block.shape[1]), axis=0)


def norm_back(d_out, normal, scale, gain):
    d_normal = d_out * gain
    d_normal = (
        d_normal
        - jnp.mean(d_normal, axis=-1, keepdims=True)
        - normal * jnp.mean(d_normal * normal, axis=-1, keepdims=True)
    )
    return d_normal * scale


def normalize(rows_in):
    center = rows_in - jnp.mean(rows_in, axis=-1, keepdims=True)
    scale = lax.rsqrt(jnp.mean(center * center, axis=-1, keepdims=True) + LN_EPS)
    return center * scale, scale


def ffn_kernel(
    lengths_ref,
    gates_ref,
    norm_ref,
    hidden_gate_ref,
    unit_gate_ref,
    context_ref,
    w_out_ref,
    tokens_hbm,
    teacher_hbm,
    w_in_hbm,
    w_fo_hbm,
    student_hbm,
    d_res1_hbm,
    d_context_hbm,
    grads_hbm,
    small_ref,
    w_in,
    w_fo,
    tokens,
    teacher,
    own1,
    own2,
    got1,
    got2,
    got3,
    normal1,
    scale1,
    gated,
    slope,
    d_res,
    d_context,
    hidden_t,
    d_ffn_t,
    d_attn_t,
    grad_wide,
    grad_out,
    sums,
    unit_sum,
    load_sem,
    tile_sem,
    grad_sem,
    send_sem,
    recv_sem,
):
    dp, core = lax.axis_index("dp"), lax.axis_index("head")
    loads = [
        pltpu.make_async_copy(source, target, load_sem.at[i])
        for i, (source, target) in enumerate(
            ((tokens_hbm, tokens), (w_in_hbm, w_in), (w_fo_hbm, w_fo), (teacher_hbm, teacher))
        )
    ]
    for one in loads:
        one.start()
    greet([(dp, 1 - core)])
    tiles = tokens.shape[0] // TILE
    units, width = w_in.shape[1], w_in.shape[0]
    sums[...] = jnp.zeros_like(sums)
    unit_sum[...] = jnp.zeros_like(unit_sum)
    hidden_gate = hidden_gate_ref[...]
    gate0, gate1 = hidden_gate * gates_ref[0], hidden_gate * gates_ref[1]
    gain1, bias1, gain2, bias2 = (norm_ref[i : i + 1, :] for i in range(4))

    def rows(t):
        return pl.ds(pl.multiple_of(t * TILE, TILE), TILE)

    def lanes(n):
        return pl.ds(n * PART, PART)

    def exchange(step, t):
        source, target = ((own1, got1), (own2, got2), (own2, got3))[step]
        return pltpu.make_async_remote_copy(
            src_ref=source.at[rows(t)],
            dst_ref=target.at[rows(t)],
            send_sem=send_sem.at[step, t],
            recv_sem=recv_sem.at[step, t],
            device_id=(dp, 1 - core),
            device_id_type=MESH,
        )

    def tile_copy(which, t):
        source, target = ((own1, student_hbm), (d_res, d_res1_hbm), (d_context, d_context_hbm))[
            which
        ]
        return pltpu.make_async_copy(
            source.at[rows(t)], target.at[rows(t)], tile_sem.at[which, t]
        )

    def phase1(t, _):
        part = mul(context_ref[rows(t)], w_out_ref[...], NT)
        own1[rows(t)] = part.astype(jnp.bfloat16)
        exchange(0, t).start()

    lax.fori_loop(0, tiles, phase1, None)
    loads[0].wait()
    loads[1].wait()
    loads[2].wait()

    def summed(source, target, t):
        return source[rows(t)].astype(jnp.float32) + target[rows(t)].astype(jnp.float32)

    def phase2(t, _):
        exchange(0, t).wait()
        rows_in = tokens[rows(t)].astype(jnp.float32) + summed(own1, got1, t) * gate0
        normal, scale = normalize(rows_in)
        normal1[rows(t)] = normal
        scale1[rows(t)] = scale
        hidden = normal * gain1 + bias1
        low = hidden.astype(jnp.bfloat16)
        hidden_t[:, rows(t)] = jnp.transpose(hidden).astype(jnp.bfloat16)
        for n in range(units // PART):
            up = mul(low, w_in[:, lanes(n)])
            below, density = normal_parts(up)
            gate = unit_gate_ref[:, lanes(n)]
            gated[rows(t), lanes(n)] = (up * below * gate).astype(jnp.bfloat16)
            slope[rows(t), lanes(n)] = ((below + density) * gate).astype(jnp.bfloat16)
        part = mul(gated[rows(t)], w_fo[...], NT)
        own2[rows(t)] = part.astype(jnp.bfloat16)
        exchange(1, t).start()

    lax.fori_loop(0, tiles, phase2, None)
    loads[3].wait()

    def phase3(t, _):
        exchange(1, t).wait()
        ffn = summed(own2, got2, t)
        hidden = normal1[rows(t)] * gain1 + bias1
        normal, scale = normalize(hidden + ffn * gate1)
        student = normal * gain2 + bias2
        student_tile = student.astype(jnp.bfloat16)
        got2[rows(t)] = student_tile
        row = t // (ROW // TILE)
        end = lengths_ref[row, 0]
        for k in range(1, lengths_ref.shape[1]):
            end = end + lengths_ref[row, k]
        position = lax.broadcasted_iota(jnp.int32, (TILE, 1), 0) + (t % (ROW // TILE)) * TILE
        valid = (position < end).astype(jnp.float32)
        d_out = valid * (student - teacher[rows(t)].astype(jnp.float32))
        d_res2 = norm_back(d_out, normal, scale, gain2)
        d_res[rows(t)] = d_res2
        sums[2] += fold(d_out * normal)
        sums[3] += fold(d_out)
        sums[5] += fold(d_res2 * ffn)
        d_ffn = d_res2 * gate1
        d_ffn_t[:, rows(t)] = jnp.transpose(d_ffn).astype(jnp.bfloat16)
        d_ffn = d_ffn.astype(jnp.bfloat16)
        for n in range(units // PART):
            d_gated = mul(d_ffn, w_fo[:, lanes(n)])
            unit_sum[:, lanes(n)] += fold(
                d_gated * gated[rows(t), lanes(n)].astype(jnp.float32)
            )
            d_up = d_gated * slope[rows(t), lanes(n)].astype(jnp.float32)
            slope[rows(t), lanes(n)] = d_up.astype(jnp.bfloat16)
        part = mul(slope[rows(t)], w_in[...], NT)
        own2[rows(t)] = part.astype(jnp.bfloat16)
        exchange(2, t).start()
        pltpu.make_async_copy(
            got2.at[rows(t)], student_hbm.at[rows(t)], tile_sem.at[0, t]
        ).start()

    lax.fori_loop(0, tiles, phase3, None)

    def wide(which, n):
        target = grads_hbm.at[:, pl.ds(which * units + n * PART, PART)]
        return pltpu.make_async_copy(
            grad_wide.at[which, :, lanes(n)], target, grad_sem.at[which, n]
        )

    for n in range(units // PART):
        grad_wide[0, :, lanes(n)] = mul(d_ffn_t[...], gated[:, lanes(n)]).astype(jnp.bfloat16)
        wide(0, n).start()

    def phase4(t, _):
        exchange(2, t).wait()
        normal = normal1[rows(t)]
        d_hidden = d_res[rows(t)] + summed(own2, got3, t)
        sums[0] += fold(d_hidden * normal)
        sums[1] += fold(d_hidden)
        d_res1 = norm_back(d_hidden, normal, scale1[rows(t)], gain1)
        d_res[rows(t)] = d_res1
        tile_copy(1, t).start()
        sums[4] += fold(d_res1 * summed(own1, got1, t))
        d_attn = d_res1 * gate0
        d_attn_t[:, rows(t)] = jnp.transpose(d_attn).astype(jnp.bfloat16)
        d_context[rows(t)] = mul(d_attn.astype(jnp.bfloat16), w_out_ref[...])
        tile_copy(2, t).start()

    lax.fori_loop(0, tiles, phase4, None)
    for n in range(units // PART):
        grad_wide[1, :, lanes(n)] = mul(hidden_t[...], slope[:, lanes(n)]).astype(jnp.bfloat16)
        wide(1, n).start()
    grad_out[...] = mul(d_attn_t[...], context_ref[...]).astype(jnp.bfloat16)
    last = pltpu.make_async_copy(
        grad_out, grads_hbm.at[:, pl.ds(2 * units, grad_out.shape[1])], grad_sem.at[2, 0]
    )
    last.start()

    def line(i):
        return jnp.sum(sums[i], axis=0, keepdims=True)

    for i in range(4):
        small_ref[i : i + 1, :] = line(i)
    attn_line, ffn_line = line(4), line(5)
    small_ref[4:5, :] = ffn_line * gates_ref[1] + attn_line * gates_ref[0]
    unit_line = jnp.sum(unit_sum[...], axis=0, keepdims=True) / unit_gate_ref[...]
    for i in range(units // width):
        small_ref[5 + i : 6 + i, :] = unit_line[:, i * width : (i + 1) * width]
    lane = lax.broadcasted_iota(jnp.int32, (1, width), 1)
    layer0 = jnp.sum(attn_line * hidden_gate, axis=1, keepdims=True)
    layer1 = jnp.sum(ffn_line * hidden_gate, axis=1, keepdims=True)
    small_ref[7:8, :] = jnp.where(lane == 128, layer0, jnp.where(lane == 129, layer1, 0.0))

    def finish(t, _):
        pltpu.make_async_copy(
            got2.at[rows(t)], student_hbm.at[rows(t)], tile_sem.at[0, t]
        ).wait()
        tile_copy(1, t).wait()
        tile_copy(2, t).wait()

    lax.fori_loop(0, tiles, finish, None)
    for n in range(units // PART):
        wide(0, n).wait()
        wide(1, n).wait()
    last.wait()


def ffn(lengths, layer_gates, norm_p, hidden_gate, unit_gate, context, w_out_t, tokens, teacher, w_in, w_fo_t):
    count, width = tokens.shape
    units, heads = w_in.shape[1], context.shape[1]
    tiles = count // TILE
    vmem, smem = pl.BlockSpec(memory_space=pltpu.VMEM), pl.BlockSpec(memory_space=pltpu.SMEM)
    anywhere = pl.BlockSpec(memory_space=pl.ANY)
    low, full = jnp.bfloat16, jnp.float32
    return pl.pallas_call(
        ffn_kernel,
        in_specs=[smem, smem] + [vmem] * 5 + [anywhere] * 4,
        out_specs=[anywhere] * 4 + [vmem],
        out_shape=[
            jax.ShapeDtypeStruct((count, width), low),
            jax.ShapeDtypeStruct((count, width), full),
            jax.ShapeDtypeStruct((count, heads), full),
            jax.ShapeDtypeStruct((width, 2 * units + heads), low),
            jax.ShapeDtypeStruct((8, width), full),
        ],
        scratch_shapes=[
            pltpu.VMEM((width, units), low),
            pltpu.VMEM((width, units), low),
            pltpu.VMEM((count, width), low),
            pltpu.VMEM((count, width), low),
            *[pltpu.VMEM((count, width), low)] * 5,
            pltpu.VMEM((count, width), full),
            pltpu.VMEM((count, 1), full),
            pltpu.VMEM((count, units), low),
            pltpu.VMEM((count, units), low),
            pltpu.VMEM((count, width), full),
            pltpu.VMEM((count, heads), full),
            *[pltpu.VMEM((width, count), low)] * 3,
            pltpu.VMEM((2, width, units), low),
            pltpu.VMEM((width, heads), low),
            pltpu.VMEM((6, 8, width), full),
            pltpu.VMEM((8, units), full),
            pltpu.SemaphoreType.DMA((4,)),
            pltpu.SemaphoreType.DMA((3, tiles)),
            pltpu.SemaphoreType.DMA((3, units // PART)),
            pltpu.SemaphoreType.DMA((3, tiles)),
            pltpu.SemaphoreType.DMA((3, tiles)),
        ],
        compiler_params=pltpu.CompilerParams(
            collective_id=4, has_side_effects=True, vmem_limit_bytes=60 << 20
        ),
        name="ffn",
    )(lengths, layer_gates, norm_p, hidden_gate[None, :], unit_gate[None, :], context, w_out_t, tokens, teacher, w_in, w_fo_t)


def lamb_moments(master, first, second, grad, decay):
    new_first = MOMENT_DECAY * first + (1.0 - MOMENT_DECAY) * grad
    new_second = MOMENT_DECAY * second + (1.0 - MOMENT_DECAY) * grad * grad
    correction = 1.0 - MOMENT_DECAY**STEP_COUNT
    update = (
        new_first / correction / (jnp.sqrt(new_second / correction) + LAMB_EPS) + decay * master
    )
    return (new_first, new_second, update)


BLOCK = 384
DEPTH = (1, 3, 2, 0)


def layer_kernel(
    lengths_ref,
    gates_ref,
    gate_ref,
    hidden_gate_ref,
    unit_gate_ref,
    norms_ref,
    norm_shard_ref,
    *refs,
):
    params, refs = refs[:12], refs[12:]
    (
        tokens_hbm,
        teacher_hbm,
        student_hbm,
        grad_tokens_hbm,
        sums_ref,
        small_out,
        norm_out,
        total_out,
        w,
        w_norm,
        tokens,
        qkv,
        d_mix,
        context,
        stats,
        left_t,
        hidden_t,
        own1,
        got1,
        own2,
        got2,
        got3,
        normal1,
        scale1,
        gated,
        slope,
        d_res,
        keep,
        gains,
        sums,
        unit_sum,
        heads,
        small_plane,
        small_line,
        norm_plane,
        norm_line,
        load_sem,
        tile_sem,
        all_send,
        all_recv,
        swap_send,
        swap_recv,
        send_sem,
        recv_sem,
        small_send,
        small_recv,
        free1,
        free2,
    ) = refs
    me, core = lax.axis_index("dp"), lax.axis_index("head")
    z, y, x = place(me)
    rows, blocks = sums_ref.shape[0], sums_ref.shape[1] // BLOCK
    count, width = tokens.shape
    tiles, tall = count // TILE, count // ROW
    units, own_width = unit_gate_ref.shape[1], gate_ref.shape[1]
    pairs = own_width // PAIR
    at_out, at_in = 3 * own_width, 4 * own_width
    at_fo = at_in + units

    def load(which, t):
        source = (tokens_hbm, teacher_hbm)[which % 2]
        return pltpu.make_async_copy(
            source.at[tile(t)], tokens.at[tile(t)], load_sem.at[which, t]
        )

    def tile(t):
        return pl.ds(pl.multiple_of(t * TILE, TILE), TILE)

    def tall_row(r):
        return pl.ds(pl.multiple_of(r * ROW, ROW), ROW)

    def each(action, begin, end):
        lax.fori_loop(begin, end, lambda i, _: action(i), None)

    each(lambda t: load(0, t).start(), 0, tiles)

    line_peers = [(index(lax.rem(z + d, NZ), y, x), core) for d in (1, 2, 3)]
    plane = [index(z, y + (1 - 2 * y) * (d // 2), x + (1 - 2 * x) * (d % 2)) for d in range(4)]
    ring = [(plane[1], core), (plane[2], core), *line_peers]
    sibling = (me, 1 - core)
    greet([(p, core) for p in plane[1:]] + [(p, 1 - core) for p in plane] + line_peers)

    def rows_of(device):
        return pl.ds(pl.multiple_of(device * rows, rows), rows)

    def columns(c):
        start = c * BLOCK
        return pl.ds(start if isinstance(c, int) else pl.multiple_of(start, BLOCK), BLOCK)

    def turned(odd, rz, ra, rb):
        flip_x = ra * (1 - odd) + rb * odd
        flip_y = rb * (1 - odd) + ra * odd
        return index(lax.rem(z + rz, NZ), y + (1 - 2 * y) * flip_y, x + (1 - 2 * x) * flip_x)

    def view(c, device):
        if isinstance(c, int) and c == blocks:
            return w_norm.at[rows_of(device)]
        return w.at[rows_of(device), columns(c)]

    def move(c, place_of, to, there, k):
        block = view(c, turned(c % 2, *place_of))
        return pltpu.make_async_remote_copy(
            src_ref=block,
            dst_ref=block,
            send_sem=all_send.at[c, k],
            recv_sem=all_recv.at[c, there],
            device_id=(to, core),
            device_id_type=MESH,
        )

    def near(c):
        return turned(c % 2, 0, 1, 0)

    def far(c):
        return turned(c % 2, 0, 0, 1)

    def arrived(c, rz, ra, rb):
        move(c, (rz, ra, rb), me, slot(rz, ra, rb), 0).wait_recv()

    def all_first(c):
        for i, dz in enumerate((1, 3, 2)):
            move(c, (0, 0, 0), line_peers[dz - 1][0], slot(NZ - dz, 0, 0), i).start()
        move(c, (0, 0, 0), near(c), slot(0, 1, 0), 3).start()
        move(c, (0, 0, 0), far(c), slot(0, 0, 1), 7).start()

    def all_second(c):
        for i, rz in enumerate((1, 3, 2)):
            arrived(c, rz, 0, 0)
            move(c, (rz, 0, 0), near(c), slot(rz, 1, 0), 4 + i).start()
            move(c, (rz, 0, 0), far(c), slot(rz, 0, 1), 8 + i).start()

    def all_third(c):
        for i, rz in enumerate((0, 1, 3, 2)):
            arrived(c, rz, 1, 0)
            move(c, (rz, 1, 0), far(c), slot(rz, 1, 1), 11 + i).start()

    def all_last(c):
        for ra in (0, 1):
            for rz in range(NZ):
                arrived(c, rz, ra, 1)

    def all_sent(c):
        for k in range(15):
            move(c, (0, 0, 0), me, 0, k).wait_send()

    mine = rows_of(me)
    for pair in range(pairs):
        for part in range(3):
            lanes = slice((3 * pair + part) * PAIR, (3 * pair + part + 1) * PAIR)
            w[mine, lanes] = params[0][part, :, pair * PAIR : (pair + 1) * PAIR].astype(jnp.bfloat16)
    w_norm[mine] = norm_shard_ref[...]
    w[mine, at_out:at_in] = params[1][...].astype(jnp.bfloat16)
    each(all_first, 0, 4)
    all_first(blocks)
    w[mine, at_in:at_fo] = params[2][...].astype(jnp.bfloat16)
    w[mine, at_fo:] = params[3][...].astype(jnp.bfloat16)
    sums[...] = jnp.zeros_like(sums)
    unit_sum[...] = jnp.zeros_like(unit_sum)
    heads[...] = jnp.zeros_like(heads)

    def upto(c):
        return min(c, blocks) if isinstance(c, int) else jnp.minimum(c, blocks)

    def serve(p):
        each(all_second, 2 * p, 2 * p + 2)
        each(all_first, 2 * p + 4, upto(2 * p + 6))
        each(all_third, 2 * p, 2 * p + 2)

    serve(0)
    all_second(blocks)
    serve(1)
    all_third(blocks)
    each(lambda t: load(0, t).wait(), 0, tiles)
    each(all_last, 0, 3)

    def attend(r, _):
        here = tall_row(r)
        same = segments(lengths_ref, r, (ROW, 1), 0) == segments(lengths_ref, r, (1, ROW), 1)
        for pair in range(pairs):
            span = slice(3 * pair * PAIR, 3 * (pair + 1) * PAIR)
            qkv[here, span] = mul(tokens[here], w[:, span]).astype(jnp.bfloat16)
        for pair in range(pairs):
            start = 3 * pair * PAIR
            mix, totals = attend_pair(
                same, *(qkv[here, start + i * PAIR : start + (i + 1) * PAIR] for i in range(3))
            )
            for head in (0, 1):
                stats[r, pair, head : head + 1, :] = totals[head]
            lanes = slice(pair * PAIR, (pair + 1) * PAIR)
            context[here, lanes] = (mix * gate_ref[:, lanes]).astype(jnp.bfloat16)
        serve(2 + r)

    lax.fori_loop(0, tall, attend, None)
    all_last(3)

    def swap(step, t):
        source, target = ((own1, got1), (own2, got2), (own2, got3), (own2, got2))[step]
        return pltpu.make_async_remote_copy(
            src_ref=source.at[tile(t)],
            dst_ref=target.at[tile(t)],
            send_sem=swap_send.at[step, t],
            recv_sem=swap_recv.at[step, t],
            device_id=sibling,
            device_id_type=MESH,
        )

    def phase1(t, _):
        part = mul(context[tile(t)], w[:, at_out:at_in], NT)
        own1[tile(t)] = part.astype(jnp.bfloat16)
        swap(0, t).start()

    lax.fori_loop(0, tiles, phase1, None)
    all_last(blocks)
    gains[...] = jnp.transpose(w_norm[...].astype(jnp.float32))[:8]
    gain1, bias1, gain2, bias2 = (gains[i : i + 1, :] for i in range(4))
    hidden_gate = hidden_gate_ref[...]
    gate0, gate1 = hidden_gate * gates_ref[0], hidden_gate * gates_ref[1]
    each(all_last, 4, 8)

    def summed(source, target, t):
        return source[tile(t)].astype(jnp.float32) + target[tile(t)].astype(jnp.float32)

    def part_lanes(n):
        return slice(n * PART, (n + 1) * PART)

    def phase2(t, _):
        swap(0, t).wait()
        rows_in = tokens[tile(t)].astype(jnp.float32) + summed(own1, got1, t) * gate0
        load(1, t).start()
        normal, scale = normalize(rows_in)
        normal1[tile(t)] = normal
        scale1[tile(t)] = scale
        hidden = normal * gain1 + bias1
        low = hidden.astype(jnp.bfloat16)
        hidden_t[:, tile(t)] = jnp.transpose(hidden).astype(jnp.bfloat16)
        for n in range(units // PART):
            up = mul(low, w[:, at_in + n * PART : at_in + (n + 1) * PART])
            below, density = normal_parts(up)
            gate = unit_gate_ref[:, part_lanes(n)]
            gated[tile(t), part_lanes(n)] = (up * below * gate).astype(jnp.bfloat16)
            slope[tile(t), part_lanes(n)] = ((below + density) * gate).astype(jnp.bfloat16)

        @pl.when(t == 2)
        def _():
            serve(5)

    lax.fori_loop(0, tiles, phase2, None)
    each(all_last, 8, blocks)

    def down(t, _):
        part = mul(gated[tile(t)], w[:, at_fo:], NT)
        own2[tile(t)] = part.astype(jnp.bfloat16)
        swap(1, t).start()

    lax.fori_loop(0, tiles, down, None)
    each(all_sent, 0, blocks)
    all_sent(blocks)

    def student_out(t):
        return pltpu.make_async_copy(
            got2.at[tile(t)], student_hbm.at[tile(t)], tile_sem.at[0, t]
        )

    def phase3(t, _):
        swap(1, t).wait()
        load(1, t).wait()
        ffn = summed(own2, got2, t)
        hidden = normal1[tile(t)] * gain1 + bias1
        normal, scale = normalize(hidden + ffn * gate1)
        student = normal * gain2 + bias2
        got2[tile(t)] = student.astype(jnp.bfloat16)
        student_out(t).start()
        row = t // (ROW // TILE)
        end = lengths_ref[row, 0]
        for k in range(1, lengths_ref.shape[1]):
            end = end + lengths_ref[row, k]
        position = lax.broadcasted_iota(jnp.int32, (TILE, 1), 0) + (t % (ROW // TILE)) * TILE
        valid = (position < end).astype(jnp.float32)
        d_out = valid * (student - tokens[tile(t)].astype(jnp.float32))
        load(2, t).start()
        d_res2 = norm_back(d_out, normal, scale, gain2)
        d_res[tile(t)] = d_res2
        sums[2] += fold(d_out * normal)
        sums[3] += fold(d_out)
        sums[5] += fold(d_res2 * ffn)
        d_ffn = d_res2 * gate1
        left_t[:, tile(t)] = jnp.transpose(d_ffn).astype(jnp.bfloat16)
        d_ffn = d_ffn.astype(jnp.bfloat16)
        for n in range(units // PART):
            d_gated = mul(d_ffn, w[:, at_fo + n * PART : at_fo + (n + 1) * PART])
            unit_sum[:, part_lanes(n)] += fold(
                d_gated * gated[tile(t), part_lanes(n)].astype(jnp.float32)
            )
            d_up = d_gated * slope[tile(t), part_lanes(n)].astype(jnp.float32)
            slope[tile(t), part_lanes(n)] = d_up.astype(jnp.bfloat16)
        part = mul(slope[tile(t)], w[:, at_in:at_fo], NT)
        own2[tile(t)] = part.astype(jnp.bfloat16)
        swap(2, t).start()

    lax.fori_loop(0, tiles, phase3, None)

    def spot(buffer, i):
        across = buffer.shape[1] // BLOCK
        return buffer.at[
            pl.ds(pl.multiple_of((i // across) * rows, rows), rows),
            pl.ds(pl.multiple_of((i % across) * BLOCK, BLOCK), BLOCK),
        ]

    def get1(c, k):
        return spot(gated, c * 8 + k)

    def get2(c, rz):
        return spot(slope, c * 7 + rz)

    def get3(c, i):
        return spot(slope, c * 7 + 4 + i)

    def remote(source, target, c, k, to):
        return pltpu.make_async_remote_copy(
            src_ref=source,
            dst_ref=target,
            send_sem=send_sem.at[c, k],
            recv_sem=recv_sem.at[c, k],
            device_id=(to, core),
            device_id_type=MESH,
        )

    def block_of(c, rz, ra, rb):
        return w.at[rows_of(turned(c % 2, rz, ra, rb)), columns(c)]

    def leg1(c, k):
        return remote(block_of(c, k % NZ, k // NZ, 1), get1(c, k), c, k, far(c))

    def leg2(c, rz):
        return remote(block_of(c, rz, 1, 0), get2(c, rz), c, 8 + rz, near(c))

    def leg3(c, rz):
        there = NZ - rz
        to = line_peers[rz - 1][0]
        return remote(block_of(c, rz, 0, 0), get3(c, there - 1), c, 11 + there, to)

    def first(c):
        for ra in (1, 0):
            for rz in DEPTH:
                leg1(c, rz + NZ * ra).start()

    def second(c):
        for ra in (1, 0):
            for rz in DEPTH:
                k = rz + NZ * ra
                leg1(c, k).wait_recv()
                block = block_of(c, rz, ra, 0)
                total = block[...].astype(jnp.float32) + get1(c, k)[...].astype(jnp.float32)
                if ra:
                    block[...] = total.astype(jnp.bfloat16)
                    leg2(c, rz).start()
                else:
                    keep[c, rz] = total

    def third(c):
        for rz in DEPTH:
            leg2(c, rz).wait_recv()
            total = keep[c, rz] + get2(c, rz)[...].astype(jnp.float32)
            if rz:
                block_of(c, rz, 0, 0)[...] = total.astype(jnp.bfloat16)
                leg3(c, rz).start()
            else:
                keep[c, 0] = total

    def last(c):
        total = keep[c, 0]
        for rz in (1, 2, 3):
            leg3(c, rz).wait_recv()
        for i in range(3):
            total = total + get3(c, i)[...].astype(jnp.float32)
        sums_ref[:, columns(c)] = total

    def weigh(left, right, start, size):
        for n in range(size // BLOCK):
            lanes = slice(start + n * BLOCK, start + (n + 1) * BLOCK)
            w[:, lanes] = mul(left[...], right[:, n * BLOCK : (n + 1) * BLOCK]).astype(jnp.bfloat16)

    def ready(semaphore, peers):
        for peer in peers:
            pl.semaphore_signal(semaphore, inc=1, device_id=peer, device_id_type=MESH)
        pl.semaphore_wait(semaphore, len(peers))

    weigh(left_t, gated, at_fo, units)
    ready(free1, ring[:2])
    for c in (11, 10, 9, 8):
        first(c)
    weigh(hidden_t, slope, at_in, units)
    each(lambda t: student_out(t).wait(), 0, tiles)
    ready(free2, [*ring, sibling])

    def phase4(t, _):
        swap(2, t).wait()
        normal = normal1[tile(t)]
        d_hidden = d_res[tile(t)] + summed(own2, got3, t)
        sums[0] += fold(d_hidden * normal)
        sums[1] += fold(d_hidden)
        d_res1 = norm_back(d_hidden, normal, scale1[tile(t)], gain1)
        d_res[tile(t)] = d_res1
        sums[4] += fold(d_res1 * summed(own1, got1, t))
        d_attn = d_res1 * gate0
        left_t[:, tile(t)] = jnp.transpose(d_attn).astype(jnp.bfloat16)
        d_context = mul(d_attn.astype(jnp.bfloat16), w[:, at_out:at_in])
        d_mix[tile(t)] = (d_context * gate_ref[...]).astype(jnp.bfloat16)
        load(2, t).wait()
        hidden_t[:, tile(t)] = jnp.transpose(tokens[tile(t)].astype(jnp.float32)).astype(jnp.bfloat16)

    lax.fori_loop(0, tiles, phase4, None)
    weigh(left_t, context, at_out, own_width)

    def down_from(action, i, n):
        lax.fori_loop(0, n, lambda j, _: action(blocks - 1 - i - j), None)

    def pair_back(j, _):
        pair = pairs - 1 - j
        span = pl.multiple_of(pair * BLOCK, BLOCK)
        gate = gate_ref[:, pl.ds(pl.multiple_of(pair * PAIR, PAIR), PAIR)]

        def row_back(r, _):
            here = tall_row(r)
            same = segments(lengths_ref, r, (ROW, 1), 0) == segments(lengths_ref, r, (1, ROW), 1)
            spans = [pl.ds(pl.multiple_of(span + i * PAIR, PAIR), PAIR) for i in range(3)]
            parts, weighed = attend_back(
                same,
                *(qkv[here, lanes] for lanes in spans),
                stats[r, pair],
                d_mix[here, pl.ds(pl.multiple_of(pair * PAIR, PAIR), PAIR)],
            )
            lane = lax.broadcasted_iota(jnp.int32, heads.shape, 1)
            for head in (0, 1):
                value = weighed[head] / gate[:, head * HEAD_DIM : head * HEAD_DIM + 1]
                heads[...] += jnp.where(lane == 2 * pair + head, value, 0.0)
            for lanes, value in zip(spans, parts, strict=True):
                qkv[here, lanes] = value.astype(jnp.bfloat16)

            @pl.when(r == 1)
            def _():
                down_from(second, 2 * j, 2)
                down_from(first, 2 * j + 4, jnp.where(j == 2, 1, 2))

        lax.fori_loop(0, tall, row_back, None)

        def back(t, _):
            part = mul(qkv[tile(t), pl.ds(span, BLOCK)], w[:, pl.ds(span, BLOCK)], NT)
            normal1[tile(t)] = part + jnp.where(j == 0, 0.0, 1.0) * normal1[tile(t)]

        lax.fori_loop(0, tiles, back, None)
        w[:, pl.ds(span, BLOCK)] = mul(hidden_t[...], qkv[:, pl.ds(span, BLOCK)]).astype(jnp.bfloat16)
        first(pair)
        down_from(third, 2 * j, 2)

        @pl.when(j > 0)
        def _():
            down_from(last, 2 * j - 2, 2)

    lax.fori_loop(0, pairs, pair_back, None)

    def tokens_out(t):
        return pltpu.make_async_copy(
            d_res.at[tile(t)], grad_tokens_hbm.at[tile(t)], tile_sem.at[1, t]
        )

    def share(t, _):
        own2[tile(t)] = normal1[tile(t)].astype(jnp.bfloat16)
        swap(3, t).start()

    lax.fori_loop(0, tiles, share, None)

    here_plane = y * NX + x

    def line_of(i):
        return jnp.sum(sums[i], axis=0, keepdims=True)

    for i in range(4):
        small_plane[here_plane, i : i + 1, :] = line_of(i)
    attn_line, ffn_line = line_of(4), line_of(5)
    small_plane[here_plane, 4:5, :] = ffn_line * gates_ref[1] + attn_line * gates_ref[0]
    unit_line = jnp.sum(unit_sum[...], axis=0, keepdims=True) / unit_gate_ref[...]
    for i in range(units // width):
        small_plane[here_plane, 5 + i : 6 + i, :] = unit_line[:, i * width : (i + 1) * width]
    lane = lax.broadcasted_iota(jnp.int32, (1, width), 1)
    layer0 = jnp.sum(attn_line * hidden_gate, axis=1, keepdims=True)
    layer1 = jnp.sum(ffn_line * hidden_gate, axis=1, keepdims=True)
    pair_line = jnp.where(lane == 128, layer0, jnp.where(lane == 129, layer1, 0.0))
    small_plane[here_plane, 7:8, :] = pair_line
    small_plane[here_plane, 7:8, :128] = heads[0:1]

    def spread(buffer, base, targets, at):
        copies = [
            pltpu.make_async_remote_copy(
                src_ref=buffer.at[at],
                dst_ref=buffer.at[at],
                send_sem=small_send.at[base + i],
                recv_sem=small_recv.at[base + i],
                device_id=to,
                device_id_type=MESH,
            )
            for i, to in enumerate(targets)
        ]
        for one in copies:
            one.start()
        return copies

    def added(buffer, copies):
        for one in copies:
            one.wait_recv()
        total = buffer[0]
        for at in range(1, buffer.shape[0]):
            total = total + buffer[at]
        return total

    sent1 = spread(small_plane, 0, [(p, core) for p in plane[1:]], here_plane)
    down_from(second, 6, 2)

    def finish(t, _):
        swap(3, t).wait()
        d_res[tile(t)] += summed(own2, got2, t)
        tokens_out(t).start()

    lax.fori_loop(0, tiles, finish, None)
    down_from(second, 9, 2)
    down_from(second, 8, 1)
    small_line[z] = added(small_plane, sent1)
    sent2 = spread(small_line, 3, line_peers, z)
    down_from(last, 4, 2)
    down_from(third, 6, 2)
    down_from(second, 11, 1)
    down_from(third, 8, 3)
    down_from(last, 6, 2)
    total = added(small_line, sent2)
    small_out[...] = total
    norm_grad = pltpu.roll(total, (width - me * rows) % width, 1)[:, :128]
    norm_out[...] = norm_grad
    down_from(third, 11, 1)

    row8 = lax.broadcasted_iota(jnp.int32, (8, 128), 0)
    lane8 = lax.broadcasted_iota(jnp.int32, (8, 128), 1)

    def put(tile8, row, weight, update):
        here = row8 == row
        return jnp.where(here & (lane8 == 0), weight, jnp.where(here & (lane8 == 1), update, tile8))

    def square(block):
        return jnp.sum(jnp.sum(block * block, axis=0, keepdims=True), axis=1, keepdims=True)

    tile8 = jnp.zeros((8, 128), jnp.float32)
    master, first_moment, second_moment = (norms_ref[i] for i in range(3))
    update = lamb_moments(master, first_moment, second_moment, norm_grad[:4, : master.shape[1]], 0.0)[2]
    for i in range(4):
        tile8 = put(tile8, 4 + i, 0.5 * square(master[i : i + 1]), 0.5 * square(update[i : i + 1]))

    def matrix(tile8, p, start):
        master = params[p][...]
        grad = sums_ref[:, start : start + master.shape[1]]
        update = lamb_moments(master, params[4 + p][...], params[8 + p][...], grad, WEIGHT_DECAY)[2]
        return put(tile8, p, square(master), square(update))

    tile8 = matrix(matrix(tile8, 3, at_fo), 2, at_in)
    down_from(last, 8, 1)
    tile8 = matrix(tile8, 1, at_out)
    weights, updates = 0.0, 0.0
    for pair in range(pairs - 1, -1, -1):
        down_from(last, blocks - 1 - pair, 1)
        for part in range(3):
            lanes = slice(pair * PAIR, (pair + 1) * PAIR)
            master = params[0][part, :, lanes]
            start = (3 * pair + part) * PAIR
            grad = sums_ref[:, start : start + PAIR]
            update = lamb_moments(master, params[4][part, :, lanes], params[8][part, :, lanes], grad, WEIGHT_DECAY)[2]
            weights, updates = weights + square(master), updates + square(update)
    tile8 = put(tile8, 0, weights, updates)
    here_cores = core * (NX * NY) + here_plane
    norm_plane[here_cores] = tile8
    targets = [(p, core) for p in plane[1:]] + [(p, 1 - core) for p in plane]
    sent3 = spread(norm_plane, 6, targets, here_cores)
    norm_line[z] = added(norm_plane, sent3)
    sent4 = spread(norm_line, 13, line_peers, z)
    total_out[...] = added(norm_line, sent4)
    for one in (*sent1, *sent2, *sent3, *sent4):
        one.wait_send()

    def drain(c):
        for k in range(8):
            leg1(c, k).wait_send()
        for rz in range(NZ):
            leg2(c, rz).wait_send()
        for rz in (1, 2, 3):
            leg3(c, rz).wait_send()

    each(drain, 0, blocks)
    each(lambda t: tokens_out(t).wait(), 0, tiles)


def layer(lengths, layer_gates, gate_lanes, hidden_gate, unit_gate, norms, norm_shard, params, tokens, teacher):
    count, width = tokens.shape
    own_width, units, rows = gate_lanes.shape[1], unit_gate.shape[0], norms.shape[2]
    total = 4 * own_width + 2 * units
    tiles, tall, blocks = count // TILE, count // ROW, total // BLOCK
    vmem, smem = pl.BlockSpec(memory_space=pltpu.VMEM), pl.BlockSpec(memory_space=pltpu.SMEM)
    anywhere = pl.BlockSpec(memory_space=pl.ANY)
    low, full = jnp.bfloat16, jnp.float32
    return pl.pallas_call(
        layer_kernel,
        in_specs=[smem, smem] + [vmem] * (5 + len(params)) + [anywhere] * 2,
        out_specs=[anywhere] * 2 + [vmem] * 4,
        out_shape=[
            jax.ShapeDtypeStruct((count, width), low),
            jax.ShapeDtypeStruct((count, width), full),
            jax.ShapeDtypeStruct((rows, total), full),
            jax.ShapeDtypeStruct((8, width), full),
            jax.ShapeDtypeStruct((8, 128), full),
            jax.ShapeDtypeStruct((8, 128), full),
        ],
        scratch_shapes=[
            pltpu.VMEM((width, total), low),
            pltpu.VMEM((width, 128), low),
            pltpu.VMEM((count, width), low),
            pltpu.VMEM((count, 3 * own_width), low),
            pltpu.VMEM((count, own_width), low),
            pltpu.VMEM((count, own_width), low),
            pltpu.VMEM((tall, own_width // PAIR, 8, ROW), full),
            pltpu.VMEM((width, count), low),
            pltpu.VMEM((width, count), low),
            *[pltpu.VMEM((count, width), low)] * 5,
            pltpu.VMEM((count, width), full),
            pltpu.VMEM((count, 1), full),
            pltpu.VMEM((count, units), low),
            pltpu.VMEM((count, units), low),
            pltpu.VMEM((count, width), full),
            pltpu.VMEM((blocks, NZ, rows, BLOCK), full),
            pltpu.VMEM((8, width), full),
            pltpu.VMEM((6, 8, width), full),
            pltpu.VMEM((8, units), full),
            pltpu.VMEM((8, 128), full),
            pltpu.VMEM((NX * NY, 8, width), full),
            pltpu.VMEM((NZ, 8, width), full),
            pltpu.VMEM((2 * NX * NY, 8, 128), full),
            pltpu.VMEM((NZ, 8, 128), full),
            pltpu.SemaphoreType.DMA((3, tiles)),
            pltpu.SemaphoreType.DMA((2, tiles)),
            pltpu.SemaphoreType.DMA((blocks + 1, 15)),
            pltpu.SemaphoreType.DMA((blocks + 1, 16)),
            pltpu.SemaphoreType.DMA((4, tiles)),
            pltpu.SemaphoreType.DMA((4, tiles)),
            pltpu.SemaphoreType.DMA((blocks, 15)),
            pltpu.SemaphoreType.DMA((blocks, 15)),
            pltpu.SemaphoreType.DMA((16,)),
            pltpu.SemaphoreType.DMA((16,)),
            pltpu.SemaphoreType.REGULAR,
            pltpu.SemaphoreType.REGULAR,
        ],
        compiler_params=pltpu.CompilerParams(
            collective_id=0, has_side_effects=True, vmem_limit_bytes=62 << 20
        ),
        name="layer",
    )(lengths, layer_gates, gate_lanes, hidden_gate[None, :], unit_gate[None, :], norms, norm_shard, *params, tokens, teacher)


def spans(shape):
    if len(shape) == 2:
        return [(slice(None), slice(None))]
    pairs = shape[2] // PAIR
    return [
        (part, slice(None), slice(pair * PAIR, (pair + 1) * PAIR))
        for pair in range(pairs)
        for part in range(3)
    ]


def update_kernel(sums_ref, small_ref, norm_ref, total_ref, norms_ref, *refs):
    params, outs = refs[:12], refs[12:]
    weight_norm = jnp.sqrt(total_ref[:, 0:1])
    update_norm = jnp.sqrt(total_ref[:, 1:2])
    trust = weight_norm / update_norm

    def step(row, targets, at, values, decay):
        master, first_moment, second_moment, grad = values
        new_first, new_second, update = lamb_moments(
            master, first_moment, second_moment, grad, decay
        )
        new_master = master - LEARN_RATE * trust[row] * update
        made = (grad, new_first, new_second, new_master, new_master.astype(jnp.bfloat16))
        for target, value in zip(targets, made, strict=True):
            target[at] = value

    start = 0
    for p in range(4):
        targets = outs[5 * p : 5 * p + 5]
        for at in spans(params[p].shape):
            width = params[p][at].shape[-1]
            grad = sums_ref[:, start : start + width]
            values = (*(params[4 * i + p][at] for i in range(3)), grad)
            step(slice(p, p + 1), targets, at, values, WEIGHT_DECAY)
            start += width
    norm_grad = norm_ref[:4, : norms_ref.shape[2]]
    values = (*(norms_ref[i] for i in range(3)), norm_grad)
    step(slice(4, 8), outs[20:25], (Ellipsis,), values, 0.0)
    stats_out, heads_out, units_out, hidden_out, layers_out = outs[25:]
    lane = lax.broadcasted_iota(jnp.int32, (8, 128), 1)
    stats_out[...] = jnp.where(lane == 0, weight_norm, jnp.where(lane == 1, update_norm, trust))
    heads_out[...] = small_ref[7:8, : heads_out.shape[1]]
    width = small_ref.shape[1]
    for i in range(units_out.shape[1] // width):
        units_out[:, i * width : (i + 1) * width] = small_ref[5 + i : 6 + i, :]
    hidden_out[...] = small_ref[4:5, :]
    layers_out[...] = small_ref[7:8, 128:130]


def update(sums, small, norm_grad, totals, norms, params, sizes):
    vmem = pl.BlockSpec(memory_space=pltpu.VMEM)
    shapes = []
    for master in params[:4]:
        shapes += [jax.ShapeDtypeStruct(master.shape, jnp.float32)] * 4
        shapes += [jax.ShapeDtypeStruct(master.shape, jnp.bfloat16)]
    shapes += [jax.ShapeDtypeStruct(norms.shape[1:], jnp.float32)] * 4
    shapes += [jax.ShapeDtypeStruct(norms.shape[1:], jnp.bfloat16)]
    shapes += [jax.ShapeDtypeStruct((8, 128), jnp.float32)]
    shapes += [jax.ShapeDtypeStruct((1, size), jnp.float32) for size in sizes]
    return pl.pallas_call(
        update_kernel,
        in_specs=[vmem] * (5 + len(params)),
        out_specs=[vmem] * len(shapes),
        out_shape=shapes,
        compiler_params=pltpu.CompilerParams(vmem_limit_bytes=48 << 20),
        name="update",
    )(sums, small, norm_grad, totals, norms, *params)


def core_sum(part):
    part = part.astype(jnp.bfloat16)
    other = lax.ppermute(part, "head", [(0, 1), (1, 0)])
    return part.astype(jnp.float32) + other.astype(jnp.float32)


def plain_totals(sums, norm_grad, norms, params, head_count):
    found, start = [], 0
    for p in range(4):
        pair = jnp.zeros((2,), jnp.float32)
        for at in spans(params[p].shape):
            master, first_moment, second_moment = (params[4 * i + p][at] for i in range(3))
            grad = sums[:, start : start + master.shape[1]]
            update = lamb_moments(master, first_moment, second_moment, grad, WEIGHT_DECAY)[2]
            pair = pair + jnp.stack([jnp.sum(master * master), jnp.sum(update * update)])
            start += master.shape[1]
        found.append(pair)
    master, first_moment, second_moment = norms
    update = lamb_moments(master, first_moment, second_moment, norm_grad[:4, : norms.shape[2]], 0.0)[2]
    rows = jnp.stack([jnp.sum(master * master, axis=1), jnp.sum(update * update, axis=1)], axis=1)
    found = jnp.concatenate([jnp.stack(found), rows / head_count])
    return jnp.pad(lax.psum(found, ("dp", "head")), ((0, 0), (0, 126)))


def rows_first(qkv):
    return jnp.transpose(qkv, (1, 0, 2))


def plain_layer(lengths, layer_gates, gate_lanes, hidden_gate, unit_gate, norms, norm_shard, params, tokens, teacher):
    heads_here, rows = gate_lanes.shape[1] // HEAD_DIM, norms.shape[2]
    own_width, units = gate_lanes.shape[1], unit_gate.shape[0]
    shards = [params[p][at] for p in range(4) for at in spans(params[p].shape)]
    shards = jnp.concatenate(shards, axis=1).astype(jnp.bfloat16)
    w, norm_t = (lax.all_gather(s, "dp", axis=0, tiled=True) for s in (shards, norm_shard))
    norm_p = norm_t[:, :4].T.astype(jnp.float32)
    w_qkv, w_out_t, w_in, w_fo_t = jnp.split(
        w, (3 * own_width, 4 * own_width, 4 * own_width + units), axis=1
    )
    qkv = jnp.dot(tokens, w_qkv, preferred_element_type=jnp.float32).astype(jnp.bfloat16)
    context, stats = attention(qkv, lengths, gate_lanes)
    student, d_res1, d_context, grads, small = ffn(
        lengths,
        layer_gates,
        norm_p,
        hidden_gate,
        unit_gate,
        context,
        w_out_t,
        tokens,
        teacher,
        w_in,
        w_fo_t,
    )
    d_qkv, head_sums = attention_back(qkv, lengths, gate_lanes, stats, d_context)
    d_heads = jnp.sum(head_sums[:, :, 0, :2], axis=0).reshape(-1)
    grad_qkv = jnp.einsum("tc,tk->ck", tokens, d_qkv, preferred_element_type=jnp.float32)
    input_part = jnp.einsum("tk,ck->tc", d_qkv, w_qkv, preferred_element_type=jnp.float32)
    grad_tokens = d_res1 + core_sum(input_part)
    grad_fo, grad_in, grad_out = jnp.split(grads.astype(jnp.float32), (units, 2 * units), axis=1)
    grads = jnp.concatenate([grad_qkv, grad_out, grad_in, grad_fo], axis=1)
    sums = lax.psum_scatter(grads, "dp", scatter_dimension=0, tiled=True)
    small = lax.psum(small.at[7, :heads_here].set(d_heads), "dp")
    norm_grad = lax.dynamic_slice_in_dim(small, lax.axis_index("dp") * rows, rows, 1)
    norm_grad = jnp.pad(norm_grad, ((0, 0), (0, 128 - rows)))
    totals = plain_totals(sums, norm_grad, norms, params, lax.axis_size("head"))
    return student, grad_tokens, sums, small, norm_grad, totals


def local(
    tokens,
    teacher,
    lengths,
    head_gate,
    unit_gate,
    hidden_gate,
    layer_gates,
    master_qkv,
    first_qkv,
    second_qkv,
    master_attn_out,
    first_attn_out,
    second_attn_out,
    master_ffn_in,
    first_ffn_in,
    second_ffn_in,
    master_ffn_out,
    first_ffn_out,
    second_ffn_out,
    master_norms,
    first_norms,
    second_norms,
):
    ours = lax.axis_size("dp") == GRID and lax.axis_size("head") == 2
    gate_lanes = jnp.repeat(head_gate, HEAD_DIM)[None, :]
    params = [
        rows_first(master_qkv),
        master_attn_out.T,
        master_ffn_in,
        master_ffn_out.T,
        rows_first(first_qkv),
        first_attn_out.T,
        first_ffn_in,
        first_ffn_out.T,
        rows_first(second_qkv),
        second_attn_out.T,
        second_ffn_in,
        second_ffn_out.T,
    ]
    norms = jnp.stack([master_norms, first_norms, second_norms])
    norm_shard = jnp.pad(master_norms.T, ((0, 0), (0, 124))).astype(jnp.bfloat16)
    run = layer if ours else plain_layer
    student, grad_tokens, sums, small, norm_grad, totals = run(
        lengths,
        layer_gates,
        gate_lanes,
        hidden_gate,
        unit_gate,
        norms,
        norm_shard,
        params,
        tokens,
        teacher,
    )
    sizes = (head_gate.shape[0], unit_gate.shape[0], hidden_gate.shape[0], 2)
    made = update(sums, small, norm_grad, totals, norms, params, sizes)
    results = []
    for p in range(4):
        for value in made[5 * p : 5 * p + 5]:
            results.append(rows_first(value) if p == 0 else value if p == 2 else value.T)
    norm_results, (stats_rows, *gate_rows) = made[20:25], made[25:]
    gate_results = [row.reshape(-1) for row in gate_rows]
    return (
        student,
        grad_tokens,
        *gate_results,
        *results,
        *norm_results,
        stats_rows[:, :3].T,
    )


def solution(mesh):
    return jax.shard_map(
        local,
        mesh=mesh,
        in_specs=(
            P("dp", None),
            P("dp", None),
            P("dp", None),
            P("head"),
            P("head"),
            P(),
            P(),
            P("dp", None, "head"),
            P("dp", None, "head"),
            P("dp", None, "head"),
            P("head", "dp"),
            P("head", "dp"),
            P("head", "dp"),
            P("dp", "head"),
            P("dp", "head"),
            P("dp", "head"),
            P("head", "dp"),
            P("head", "dp"),
            P("head", "dp"),
            P(None, "dp"),
            P(None, "dp"),
            P(None, "dp"),
        ),
        out_specs=(
            P("dp", None),
            P("dp", None),
            P("head"),
            P("head"),
            P(),
            P(),
            P("dp", None, "head"),
            P("dp", None, "head"),
            P("dp", None, "head"),
            P("dp", None, "head"),
            P("dp", None, "head"),
            P("head", "dp"),
            P("head", "dp"),
            P("head", "dp"),
            P("head", "dp"),
            P("head", "dp"),
            P("dp", "head"),
            P("dp", "head"),
            P("dp", "head"),
            P("dp", "head"),
            P("dp", "head"),
            P("head", "dp"),
            P("head", "dp"),
            P("head", "dp"),
            P("head", "dp"),
            P("head", "dp"),
            P(None, "dp"),
            P(None, "dp"),
            P(None, "dp"),
            P(None, "dp"),
            P(None, "dp"),
            P(),
        ),
        check_vma=False,
    )
```

time: 269 us -> 244 us (0.907)
  Pallas kernels: 236 us -> 221 us
  other arithmetic: 8.84 us -> 3.22 us
  matrix products: 5.43 us -> 0 us
    pallas_call x5 -> x2, Pallas kernels: 236 us -> 221 us  [the longest x1 219 us: layer(): pl.pallas_call(layer_kernel, in_specs=[smem, smem] + [vmem] * (5 + len(pa...]
    dot_general x1 -> x0, matrix products: 5.43 us -> none  [local(): jnp.dot(tokens, w_qkv, preferred_element_type=jnp.float32)]
    convert_element_type x4 -> x0, other arithmetic: 5.38 us -> none  [the longest x1 1.64 us: local(): master_ffn_in.astype(jnp.bfloat16)]
    unnamed x61 -> x39, local copies, waits for them, and re-layouts: 12.7 us -> 14 us
where the time goes in v3:
time: 244 us
  Pallas kernels  221 us (91%)
  local copies, waits for them, and re-layouts  18.7 us (8%)
  other arithmetic  3.22 us (1%)
    pallas_call x1, Pallas kernels, layer(): pl.pallas_call(layer_kernel, in_specs=[smem, smem] + [vmem] * (5 + len(pa...  219 us
    unnamed x39, local copies, waits for them, and re-layouts  14 us

profile of v3, /device:TPU:0, one launch (start us, length us, event | category | flops | bytes accessed | tf_op | source)
XLA Modules:
  0.0 243.7 jit_solution(10111448560404867034)
XLA Ops:
  0.7 0.7 broadcast_in_dim.9
  1.4 0.6 broadcast_in_dim_reshape.3.gate_ref
  2.0 1.3 broadcast_in_dim.10.hidden_gate_ref
  3.3 1.3 broadcast_in_dim.11.unit_gate_ref
  4.6 1.3 pad_maximum_fusion.norms_ref
  5.9 0.7 convert.5
  6.6 0.1 copy.54
  6.7 0.6 pad.5.norm_shard_ref
  7.3 0.0 copy-start
  7.3 0.0 copy-start.1
  7.3 0.0 copy-start.2
  7.3 0.0 copy-start.3
  7.3 0.0 copy-start.4
  7.3 0.0 copy-start.5
  7.3 0.0 copy-start.6
  7.4 0.0 copy-start.13
  7.4 218.6 %layer.1 = (bf16[1536,768]{1,0:T(8,128)(2,1)}, f32[1536,768]{1,0:T(8,128)}, f32[48,4608]{1,0:T(8,128)}, f32[8,768]{1,0:T(8,128)}, f32[8,128]{1,0:T(8,128)}, /*index=5*/f32[8,128]{1,0:T(8,128)}) custom-call(s32[3,6]{1,0:T(4,128)} %lengths_ref.1, f32[2]{0:T(128)} %gates_ref.1, f32[1,384]{1,0:T(1,128)} %broadcast_in_dim_reshape.3.gate_ref, ...), custom_call_target="tpu_custom_call" | custom-call | tf_op jit(solution)/shard_map/layer/pallas_call | solution.py:1138
  226.0 0.0 copy-done
  226.0 0.0 copy-done.1
  226.0 0.0 copy-done.2
  226.0 0.0 copy-done.3
  226.0 0.0 copy-done.4
  226.0 0.0 copy-done.5
  226.0 0.0 copy-done.6
  226.0 0.0 copy-done.13
  226.0 0.0 copy-start.7
  226.0 0.9 copy-done.7
  227.0 0.0 copy-start.8
  227.0 0.9 copy-done.8
  227.9 0.0 copy-start.9
  227.9 1.2 copy-done.9
  229.1 0.0 copy-start.10
  229.1 0.9 copy-done.10
  230.0 0.0 copy-start.11
  230.0 0.9 copy-done.11
  230.8 0.0 copy-start.12
  230.8 0.9 copy-done.12
  231.7 0.0 copy-start.14
  231.7 0.7 copy-done.14
  232.5 0.0 copy-start.15
  232.5 0.7 copy-done.15
  233.1 0.0 copy-start.16
  233.1 0.7 copy-done.16
  233.8 2.4 update.1
  236.2 0.6 reduce
  236.8 0.6 reduce.1
  237.4 0.7 copy.55
  238.1 0.0 copy-start.17
  238.1 3.4 %copy.58 = bf16[1536,768]{1,0:T(8,128)(2,1)} copy(bf16[1536,768]{1,0:T(8,128)(2,1)} %get-tuple-element.168) | data formatting | bytes 4718592
  241.4 0.0 copy-done.17
  241.5 2.2 copy.59
  (1 shorter events, 0.0 us)
Async XLA Ops:
  7.3 218.6 %copy-start = (f32[48,1536]{1,0:T(8,128)S(1)}, f32[48,1536]{1,0:T(8,128)}, u32[]{:S(2)}) copy-start(f32[48,1536]{1,0:T(8,128)} %refs_2_.3) | copy-start | bytes 884740
  7.3 218.7 %copy-start.1 = (f32[1536,48]{0,1:T(8,128)S(1)}, f32[1536,48]{0,1:T(8,128)}, u32[]{:S(2)}) copy-start(f32[1536,48]{0,1:T(8,128)} %param.38) | copy-start | bytes 884740
  7.3 218.7 %copy-start.2 = (f32[48,1536]{1,0:T(8,128)S(1)}, f32[48,1536]{1,0:T(8,128)}, u32[]{:S(2)}) copy-start(f32[48,1536]{1,0:T(8,128)} %refs_6_.3) | copy-start | bytes 884740
  7.3 218.7 %copy-start.3 = (f32[1536,48]{0,1:T(8,128)S(1)}, f32[1536,48]{0,1:T(8,128)}, u32[]{:S(2)}) copy-start(f32[1536,48]{0,1:T(8,128)} %param.39) | copy-start | bytes 884740
  7.3 218.7 %copy-start.4 = (f32[48,1536]{1,0:T(8,128)S(1)}, f32[48,1536]{1,0:T(8,128)}, u32[]{:S(2)}) copy-start(f32[48,1536]{1,0:T(8,128)} %refs_10_.3) | copy-start | bytes 884740
  7.3 218.7 %copy-start.5 = (f32[1536,48]{0,1:T(8,128)S(1)}, f32[1536,48]{0,1:T(8,128)}, u32[]{:S(2)}) copy-start(f32[1536,48]{0,1:T(8,128)} %param.40) | copy-start | bytes 884740
  7.3 218.7 %copy-start.6 = (f32[48,3,384]{2,0,1:T(8,128)S(1)}, f32[48,3,384]{2,0,1:T(8,128)}, u32[]{:S(2)}) copy-start(f32[48,3,384]{2,0,1:T(8,128)} %param.29) | copy-start | bytes 663556
  7.4 218.7 %copy-start.13 = (f32[3,4,48]{2,1,0:T(4,128)S(1)}, f32[3,4,48]{2,1,0:T(4,128)}, u32[]{:S(2)}) copy-start(f32[3,4,48]{2,1,0:T(4,128)} %pad_maximum_fusion.norms_ref) | copy-start | bytes 6916
  226.0 0.9 copy-start.7
  227.0 0.9 copy-start.8
  227.9 1.2 copy-start.9
  229.1 0.9 copy-start.10
  230.0 0.9 copy-start.11
  230.8 0.9 copy-start.12
  231.7 0.7 copy-start.14
  232.5 0.7 copy-start.15
  233.1 0.7 copy-start.16
  238.1 3.4 %copy-start.17 = (f32[1536,768]{1,0:T(8,128)S(1)}, f32[1536,768]{1,0:T(8,128)}, u32[]{:S(2)}) copy-start(f32[1536,768]{1,0:T(8,128)} %get-tuple-element.169) | copy-start | bytes 14155780

commit v4 on v3

--- a/solution.py
+++ b/solution.py
@@ -521,14 +521,12 @@
 def layer_kernel(
     lengths_ref,
     gates_ref,
-    gate_ref,
+    head_gate_ref,
     hidden_gate_ref,
     unit_gate_ref,
-    norms_ref,
-    norm_shard_ref,
     *refs,
 ):
-    params, refs = refs[:12], refs[12:]
+    masters, norms_refs, moments_hbm, refs = refs[:4], refs[4:7], refs[7:15], refs[15:]
     (
         tokens_hbm,
         teacher_hbm,
@@ -566,6 +564,10 @@
         small_line,
         norm_plane,
         norm_line,
+        gate_row,
+        unit_row,
+        norm_pad,
+        fo_copy,
         load_sem,
         tile_sem,
         all_send,
@@ -576,15 +578,24 @@
         recv_sem,
         small_send,
         small_recv,
+        stash_sem,
+        moment_sem,
         free1,
         free2,
+        free3,
     ) = refs
     me, core = lax.axis_index("dp"), lax.axis_index("head")
     z, y, x = place(me)
     rows, blocks = sums_ref.shape[0], sums_ref.shape[1] // BLOCK
     count, width = tokens.shape
     tiles, tall = count // TILE, count // ROW
-    units, own_width = unit_gate_ref.shape[1], gate_ref.shape[1]
+    units, own_width = unit_gate_ref.shape[0], masters[1].shape[1]
+    lane = lax.broadcasted_iota(jnp.int32, (1, own_width), 1)
+    gate_lanes = jnp.zeros((1, own_width), jnp.float32)
+    for head in range(own_width // HEAD_DIM):
+        gate_lanes = jnp.where(lane // HEAD_DIM == head, head_gate_ref[head], gate_lanes)
+    gate_row[...] = gate_lanes
+    unit_row[...] = unit_gate_ref[...].reshape(1, units)
     pairs = own_width // PAIR
     at_out, at_in = 3 * own_width, 4 * own_width
     at_fo = at_in + units
@@ -666,6 +677,23 @@
             arrived(c, rz, 1, 0)
             move(c, (rz, 1, 0), far(c), slot(rz, 1, 1), 11 + i).start()
 
+    def all_turn(c):
+        arrived(c, 0, 1, 0)
+        for i, dz in enumerate((1, 3, 2)):
+            move(c, (0, 1, 0), line_peers[dz - 1][0], slot(NZ - dz, 1, 0), 4 + i).start()
+        move(c, (0, 1, 0), far(c), slot(0, 1, 1), 11).start()
+
+    def all_lined(c, ra):
+        for i, rz in enumerate((1, 3, 2)):
+            arrived(c, rz, ra, 0)
+            move(c, (rz, ra, 0), far(c), slot(rz, ra, 1), 8 + 4 * ra + i).start()
+
+    def all_own_line(c):
+        all_lined(c, 0)
+
+    def all_near_line(c):
+        all_lined(c, 1)
+
     def all_last(c):
         for ra in (0, 1):
             for rz in range(NZ):
@@ -679,54 +707,69 @@
     for pair in range(pairs):
         for part in range(3):
             lanes = slice((3 * pair + part) * PAIR, (3 * pair + part + 1) * PAIR)
-            w[mine, lanes] = params[0][part, :, pair * PAIR : (pair + 1) * PAIR].astype(jnp.bfloat16)
-    w_norm[mine] = norm_shard_ref[...]
-    w[mine, at_out:at_in] = params[1][...].astype(jnp.bfloat16)
-    each(all_first, 0, 4)
+            w[mine, lanes] = masters[0][part, :, pair * PAIR : (pair + 1) * PAIR].astype(jnp.bfloat16)
+    norm_pad[...] = jnp.zeros_like(norm_pad)
+    norm_pad[0:4, 0:rows] = norms_refs[0][...]
+    w_norm[mine] = jnp.transpose(norm_pad[...])[:rows].astype(jnp.bfloat16)
+    w[mine, at_out:at_in] = masters[1][...].astype(jnp.bfloat16)
+    each(all_first, 0, 2)
     all_first(blocks)
-    w[mine, at_in:at_fo] = params[2][...].astype(jnp.bfloat16)
-    w[mine, at_fo:] = params[3][...].astype(jnp.bfloat16)
+    w[mine, at_in:at_fo] = masters[2][...].astype(jnp.bfloat16)
+    w[mine, at_fo:] = masters[3][...].astype(jnp.bfloat16)
+    each(all_first, 2, blocks)
     sums[...] = jnp.zeros_like(sums)
-    unit_sum[...] = jnp.zeros_like(unit_sum)
     heads[...] = jnp.zeros_like(heads)
 
-    def upto(c):
-        return min(c, blocks) if isinstance(c, int) else jnp.minimum(c, blocks)
-
-    def serve(p):
-        each(all_second, 2 * p, 2 * p + 2)
-        each(all_first, 2 * p + 4, upto(2 * p + 6))
-        each(all_third, 2 * p, 2 * p + 2)
-
-    serve(0)
+    def two(action, p):
+        each(action, 2 * p, 2 * p + 2)
+
+    two(all_second, 0)
     all_second(blocks)
-    serve(1)
+    two(all_second, 1)
+    two(all_third, 0)
     all_third(blocks)
+    two(all_turn, 4)
+    two(all_turn, 5)
     each(lambda t: load(0, t).wait(), 0, tiles)
-    each(all_last, 0, 3)
-
-    def attend(r, _):
-        here = tall_row(r)
-        same = segments(lengths_ref, r, (ROW, 1), 0) == segments(lengths_ref, r, (1, ROW), 1)
-        for pair in range(pairs):
-            span = slice(3 * pair * PAIR, 3 * (pair + 1) * PAIR)
-            qkv[here, span] = mul(tokens[here], w[:, span]).astype(jnp.bfloat16)
-        for pair in range(pairs):
-            start = 3 * pair * PAIR
+
+    def pair_lanes(pair):
+        return pl.ds(pl.multiple_of(pair * PAIR, PAIR), PAIR)
+
+    def attend(pair, _):
+        all_last(pair)
+        span = pl.multiple_of(pair * BLOCK, BLOCK)
+
+        def row(r, _):
+            here = tall_row(r)
+            same = segments(lengths_ref, r, (ROW, 1), 0) == segments(lengths_ref, r, (1, ROW), 1)
+            part = mul(tokens[here], w[:, pl.ds(span, BLOCK)]).astype(jnp.bfloat16)
+            qkv[here, pl.ds(span, BLOCK)] = part
             mix, totals = attend_pair(
-                same, *(qkv[here, start + i * PAIR : start + (i + 1) * PAIR] for i in range(3))
+                same, *(part[:, i * PAIR : (i + 1) * PAIR] for i in range(3))
             )
             for head in (0, 1):
                 stats[r, pair, head : head + 1, :] = totals[head]
-            lanes = slice(pair * PAIR, (pair + 1) * PAIR)
-            context[here, lanes] = (mix * gate_ref[:, lanes]).astype(jnp.bfloat16)
-        serve(2 + r)
-
-    lax.fori_loop(0, tall, attend, None)
+            lanes = pair_lanes(pair)
+            context[here, lanes] = (mix * gate_row[:, lanes]).astype(jnp.bfloat16)
+
+            @pl.when((r == 1) & (pair < 2))
+            def _():
+                two(all_second, 2 + pair)
+                two(all_third, 1 + pair)
+
+            @pl.when((r == 1) & (pair == 2))
+            def _():
+                two(all_own_line, 4)
+                two(all_third, 3)
+
+        lax.fori_loop(0, tall, row, None)
+
+    lax.fori_loop(0, pairs, attend, None)
+    two(all_own_line, 5)
     all_last(3)
 
     def swap(step, t):
-        source, target = ((own1, got1), (own2, got2), (own2, got3), (own2, got2))[step]
+        source, target = ((own1, got1), (own2, got2), (own2, got3), (own2, got3))[step]
         return pltpu.make_async_remote_copy(
             src_ref=source.at[tile(t)],
             dst_ref=target.at[tile(t)],
@@ -745,7 +788,7 @@
     all_last(blocks)
     gains[...] = jnp.transpose(w_norm[...].astype(jnp.float32))[:8]
     gain1, bias1, gain2, bias2 = (gains[i : i + 1, :] for i in range(4))
-    hidden_gate = hidden_gate_ref[...]
+    hidden_gate = hidden_gate_ref[...].reshape(1, width)
     gate0, gate1 = hidden_gate * gates_ref[0], hidden_gate * gates_ref[1]
     each(all_last, 4, 8)
 
@@ -768,16 +811,22 @@
         for n in range(units // PART):
             up = mul(low, w[:, at_in + n * PART : at_in + (n + 1) * PART])
             below, density = normal_parts(up)
-            gate = unit_gate_ref[:, part_lanes(n)]
+            gate = unit_row[:, part_lanes(n)]
             gated[tile(t), part_lanes(n)] = (up * below * gate).astype(jnp.bfloat16)
             slope[tile(t), part_lanes(n)] = ((below + density) * gate).astype(jnp.bfloat16)
 
-        @pl.when(t == 2)
+        @pl.when(t == 1)
         def _():
-            serve(5)
+            two(all_near_line, 4)
+
+        @pl.when(t == 3)
+        def _():
+            two(all_near_line, 5)
 
     lax.fori_loop(0, tiles, phase2, None)
     each(all_last, 8, blocks)
+    stash_fo = pltpu.make_async_copy(w.at[:, at_fo:], fo_copy, stash_sem.at[2])
+    stash_fo.start()
 
     def down(t, _):
         part = mul(gated[tile(t)], w[:, at_fo:], NT)
@@ -817,35 +866,24 @@
         sums[5] += fold(d_res2 * ffn)
         d_ffn = d_res2 * gate1
         left_t[:, tile(t)] = jnp.transpose(d_ffn).astype(jnp.bfloat16)
-        d_ffn = d_ffn.astype(jnp.bfloat16)
-        for n in range(units // PART):
-            d_gated = mul(d_ffn, w[:, at_fo + n * PART : at_fo + (n + 1) * PART])
-            unit_sum[:, part_lanes(n)] += fold(
-                d_gated * gated[tile(t), part_lanes(n)].astype(jnp.float32)
-            )
-            d_up = d_gated * slope[tile(t), part_lanes(n)].astype(jnp.float32)
-            slope[tile(t), part_lanes(n)] = d_up.astype(jnp.bfloat16)
-        part = mul(slope[tile(t)], w[:, at_in:at_fo], NT)
-        own2[tile(t)] = part.astype(jnp.bfloat16)
-        swap(2, t).start()
 
     lax.fori_loop(0, tiles, phase3, None)
 
-    def spot(buffer, i):
+    late_fo = at_fo // BLOCK
+    grid_w = w.reshape(NZ, NY, NX, rows, w.shape[1])
+
+    def landing(c, stage, i=0):
+        buffer, n = (got2, c - late_fo) if c >= late_fo else (gated, c)
         across = buffer.shape[1] // BLOCK
-        return buffer.at[
-            pl.ds(pl.multiple_of((i // across) * rows, rows), rows),
-            pl.ds(pl.multiple_of((i % across) * BLOCK, BLOCK), BLOCK),
-        ]
-
-    def get1(c, k):
-        return spot(gated, c * 8 + k)
-
-    def get2(c, rz):
-        return spot(slope, c * 7 + rz)
-
-    def get3(c, i):
-        return spot(slope, c * 7 + 4 + i)
+        if stage == 1:
+            view = buffer.reshape(4, NZ, 2, rows, buffer.shape[1])
+            return view.at[n // across, :, :, :, pl.ds(n % across * BLOCK, BLOCK)]
+        if stage == 2:
+            view = buffer.reshape(8, NZ, rows, buffer.shape[1])
+            return view.at[4 + n // across, :, :, pl.ds(n % across * BLOCK, BLOCK)]
+        at = 24 * across + 3 * n + i
+        view = buffer.reshape(32, rows, buffer.shape[1])
+        return view.at[at // across, :, pl.ds(at % across * BLOCK, BLOCK)]
 
     def remote(source, target, c, k, to):
         return pltpu.make_async_remote_copy(
@@ -857,55 +895,64 @@
             device_id_type=MESH,
         )
 
-    def block_of(c, rz, ra, rb):
-        return w.at[rows_of(turned(c % 2, rz, ra, rb)), columns(c)]
-
-    def leg1(c, k):
-        return remote(block_of(c, k % NZ, k // NZ, 1), get1(c, k), c, k, far(c))
-
-    def leg2(c, rz):
-        return remote(block_of(c, rz, 1, 0), get2(c, rz), c, 8 + rz, near(c))
+    def half(c, other):
+        if c % 2:
+            return grid_w.at[:, :, 1 - x if other else x, :, columns(c)]
+        return grid_w.at[:, 1 - y if other else y, :, :, columns(c)]
+
+    def quarter(c, other):
+        if c % 2:
+            return grid_w.at[:, 1 - y if other else y, x, :, columns(c)]
+        return grid_w.at[:, y, 1 - x if other else x, :, columns(c)]
+
+    def side(c, other):
+        mine_at = y if c % 2 else x
+        return 1 - mine_at if other else mine_at
+
+    def leg1(c):
+        return remote(half(c, True), landing(c, 1), c, 0, far(c))
+
+    def leg2(c):
+        return remote(quarter(c, True), landing(c, 2), c, 1, near(c))
 
     def leg3(c, rz):
+        source = grid_w.at[lax.rem(z + rz, NZ), y, x, :, columns(c)]
         there = NZ - rz
-        to = line_peers[rz - 1][0]
-        return remote(block_of(c, rz, 0, 0), get3(c, there - 1), c, 11 + there, to)
+        return remote(source, landing(c, 3, there - 1), c, 1 + there, line_peers[rz - 1][0])
 
     def first(c):
-        for ra in (1, 0):
-            for rz in DEPTH:
-                leg1(c, rz + NZ * ra).start()
+        leg1(c).start()
 
     def second(c):
-        for ra in (1, 0):
-            for rz in DEPTH:
-                k = rz + NZ * ra
-                leg1(c, k).wait_recv()
-                block = block_of(c, rz, ra, 0)
-                total = block[...].astype(jnp.float32) + get1(c, k)[...].astype(jnp.float32)
-                if ra:
-                    block[...] = total.astype(jnp.bfloat16)
-                    leg2(c, rz).start()
-                else:
-                    keep[c, rz] = total
+        leg1(c).wait_recv()
+        came = landing(c, 1)
+        block = quarter(c, True)
+        total = block[...].astype(jnp.float32) + came[:, side(c, True)].astype(jnp.float32)
+        block[...] = total.astype(jnp.bfloat16)
+        leg2(c).start()
+        block = quarter(c, False)
+        total = block[...].astype(jnp.float32) + came[:, side(c, False)].astype(jnp.float32)
+        keep[c % 8] = total
 
     def third(c):
-        for rz in DEPTH:
-            leg2(c, rz).wait_recv()
-            total = keep[c, rz] + get2(c, rz)[...].astype(jnp.float32)
-            if rz:
-                block_of(c, rz, 0, 0)[...] = total.astype(jnp.bfloat16)
-                leg3(c, rz).start()
-            else:
-                keep[c, 0] = total
+        leg2(c).wait_recv()
+        total = keep[c % 8] + landing(c, 2)[...].astype(jnp.float32)
+        keep[c % 8] = total
+        quarter(c, False)[...] = total.astype(jnp.bfloat16)
+        for rz in (1, 3, 2):
+            leg3(c, rz).start()
 
     def last(c):
-        total = keep[c, 0]
         for rz in (1, 2, 3):
             leg3(c, rz).wait_recv()
+        total = keep[c % 8, z]
         for i in range(3):
-            total = total + get3(c, i)[...].astype(jnp.float32)
+            total = total + landing(c, 3, i)[...].astype(jnp.float32)
         sums_ref[:, columns(c)] = total
+
+    def down_from(action, i, n):
+        for j in range(i, i + n):
+            action(blocks - 1 - j)
 
     def weigh(left, right, start, size):
         for n in range(size // BLOCK):
@@ -917,13 +964,48 @@
             pl.semaphore_signal(semaphore, inc=1, device_id=peer, device_id_type=MESH)
         pl.semaphore_wait(semaphore, len(peers))
 
-    weigh(left_t, gated, at_fo, units)
-    ready(free1, ring[:2])
-    for c in (11, 10, 9, 8):
-        first(c)
-    weigh(hidden_t, slope, at_in, units)
     each(lambda t: student_out(t).wait(), 0, tiles)
-    ready(free2, [*ring, sibling])
+    stash_fo.wait()
+    ready(free1, ring)
+    for n in range(units // BLOCK - 1, -1, -1):
+        lanes = slice(n * BLOCK, (n + 1) * BLOCK)
+        grad = mul(left_t[...], gated[:, lanes])
+        w[:, at_fo + n * BLOCK : at_fo + (n + 1) * BLOCK] = grad.astype(jnp.bfloat16)
+        unit_sum[:, lanes] = fold(grad * fo_copy[:, lanes].astype(jnp.float32))
+        first(late_fo + n)
+
+    def phase3_units(t, _):
+        d_ffn = (d_res[tile(t)] * gate1).astype(jnp.bfloat16)
+        for n in range(units // PART):
+            d_gated = mul(d_ffn, fo_copy[:, part_lanes(n)])
+            d_up = d_gated * slope[tile(t), part_lanes(n)].astype(jnp.float32)
+            slope[tile(t), part_lanes(n)] = d_up.astype(jnp.bfloat16)
+        part = mul(slope[tile(t)], w[:, at_in:at_fo], NT)
+        own2[tile(t)] = part.astype(jnp.bfloat16)
+        swap(2, t).start()
+
+        @pl.when(t == 3)
+        def _():
+            down_from(second, 0, 2)
+
+    lax.fori_loop(0, tiles, phase3_units, None)
+    down_from(second, 2, 2)
+    ready(free2, ring)
+    down_from(third, 0, 2)
+    for n in range(units // BLOCK - 1, -1, -1):
+        weigh(hidden_t, slope.at[:, n * BLOCK : (n + 1) * BLOCK], at_in + n * BLOCK, BLOCK)
+        first(at_in // BLOCK + n)
+
+    def moment(i, p, n):
+        band = (8 * i + (0, 3, 4, 6)[p] + n) * rows
+        return normal1.at[band : band + rows, : own_width if p < 2 else width]
+
+    def moment_pieces(i):
+        qkv_m, out_m, in_m, fo_m = moments_hbm[4 * i : 4 * i + 4]
+        found = [(0, n, qkv_m.at[n]) for n in range(3)] + [(1, 0, out_m)]
+        for p, array in ((2, in_m), (3, fo_m)):
+            found += [(p, n, array.at[:, n * width : (n + 1) * width]) for n in range(2)]
+        return found
 
     def phase4(t, _):
         swap(2, t).wait()
@@ -937,20 +1019,39 @@
         d_attn = d_res1 * gate0
         left_t[:, tile(t)] = jnp.transpose(d_attn).astype(jnp.bfloat16)
         d_context = mul(d_attn.astype(jnp.bfloat16), w[:, at_out:at_in])
-        d_mix[tile(t)] = (d_context * gate_ref[...]).astype(jnp.bfloat16)
+        d_mix[tile(t)] = (d_context * gate_row[...]).astype(jnp.bfloat16)
         load(2, t).wait()
         hidden_t[:, tile(t)] = jnp.transpose(tokens[tile(t)].astype(jnp.float32)).astype(jnp.bfloat16)
 
     lax.fori_loop(0, tiles, phase4, None)
+    pl.semaphore_signal(free3, inc=1, device_id=sibling, device_id_type=MESH)
+    stash = [
+        pltpu.make_async_copy(
+            w.at[:, i * width : min((i + 1) * width, at_out)],
+            own1.at[i * width : (i + 1) * width, : min((i + 1) * width, at_out) - i * width],
+            stash_sem.at[i],
+        )
+        for i in range(2)
+    ]
+    for one in stash:
+        one.start()
+    moment_loads = [
+        pltpu.make_async_copy(source, moment(i, p, n), moment_sem.at[i, at])
+        for i in range(2)
+        for at, (p, n, source) in enumerate(moment_pieces(i))
+    ]
+    for one in moment_loads:
+        one.start()
     weigh(left_t, context, at_out, own_width)
-
-    def down_from(action, i, n):
-        lax.fori_loop(0, n, lambda j, _: action(blocks - 1 - i - j), None)
+    first(at_out // BLOCK)
+    down_from(third, 2, 2)
+    down_from(last, 0, 2)
+    down_from(second, 4, 2)
 
     def pair_back(j, _):
         pair = pairs - 1 - j
         span = pl.multiple_of(pair * BLOCK, BLOCK)
-        gate = gate_ref[:, pl.ds(pl.multiple_of(pair * PAIR, PAIR), PAIR)]
+        gate = gate_row[:, pl.ds(pl.multiple_of(pair * PAIR, PAIR), PAIR)]
 
         def row_back(r, _):
             here = tall_row(r)
@@ -969,25 +1070,37 @@
             for lanes, value in zip(spans, parts, strict=True):
                 qkv[here, lanes] = value.astype(jnp.bfloat16)
 
-            @pl.when(r == 1)
+            @pl.when((r == 1) & (j == 1))
             def _():
-                down_from(second, 2 * j, 2)
-                down_from(first, 2 * j + 4, jnp.where(j == 2, 1, 2))
+                down_from(second, 6, 2)
+
+            @pl.when((r == 1) & (j == 2))
+            def _():
+                down_from(second, 8, 1)
 
         lax.fori_loop(0, tall, row_back, None)
 
-        def back(t, _):
-            part = mul(qkv[tile(t), pl.ds(span, BLOCK)], w[:, pl.ds(span, BLOCK)], NT)
-            normal1[tile(t)] = part + jnp.where(j == 0, 0.0, 1.0) * normal1[tile(t)]
-
-        lax.fori_loop(0, tiles, back, None)
+        @pl.when(j == 0)
+        def _():
+            for one in stash:
+                one.wait()
+
         w[:, pl.ds(span, BLOCK)] = mul(hidden_t[...], qkv[:, pl.ds(span, BLOCK)]).astype(jnp.bfloat16)
-        first(pair)
-        down_from(third, 2 * j, 2)
-
-        @pl.when(j > 0)
+        for c in range(pairs):
+
+            @pl.when(pair == c)
+            def _(c=c):
+                first(c)
+
+        @pl.when(j == 0)
         def _():
-            down_from(last, 2 * j - 2, 2)
+            down_from(last, 2, 2)
+            down_from(third, 4, 2)
+
+        @pl.when(j == 1)
+        def _():
+            down_from(third, 6, 2)
+            down_from(last, 4, 2)
 
     lax.fori_loop(0, pairs, pair_back, None)
 
@@ -997,9 +1110,12 @@
         )
 
     def share(t, _):
-        own2[tile(t)] = normal1[tile(t)].astype(jnp.bfloat16)
+        part = mul(qkv[tile(t), :width], own1[:width], NT)
+        part = part + mul(qkv[tile(t), width:], own1[width:, : at_out - width], NT)
+        own2[tile(t)] = part.astype(jnp.bfloat16)
         swap(3, t).start()
 
+    pl.semaphore_wait(free3, 1)
     lax.fori_loop(0, tiles, share, None)
 
     here_plane = y * NX + x
@@ -1011,7 +1127,7 @@
         small_plane[here_plane, i : i + 1, :] = line_of(i)
     attn_line, ffn_line = line_of(4), line_of(5)
     small_plane[here_plane, 4:5, :] = ffn_line * gates_ref[1] + attn_line * gates_ref[0]
-    unit_line = jnp.sum(unit_sum[...], axis=0, keepdims=True) / unit_gate_ref[...]
+    unit_line = jnp.sum(unit_sum[...], axis=0, keepdims=True) / unit_row[...]
     for i in range(units // width):
         small_plane[here_plane, 5 + i : 6 + i, :] = unit_line[:, i * width : (i + 1) * width]
     lane = lax.broadcasted_iota(jnp.int32, (1, width), 1)
@@ -1046,23 +1162,20 @@
         return total
 
     sent1 = spread(small_plane, 0, [(p, core) for p in plane[1:]], here_plane)
-    down_from(second, 6, 2)
+    down_from(second, 9, 2)
+    down_from(third, 8, 1)
 
     def finish(t, _):
         swap(3, t).wait()
-        d_res[tile(t)] += summed(own2, got2, t)
+        d_res[tile(t)] += summed(own2, got3, t)
         tokens_out(t).start()
 
     lax.fori_loop(0, tiles, finish, None)
-    down_from(second, 9, 2)
-    down_from(second, 8, 1)
     small_line[z] = added(small_plane, sent1)
     sent2 = spread(small_line, 3, line_peers, z)
-    down_from(last, 4, 2)
-    down_from(third, 6, 2)
+    down_from(last, 6, 2)
     down_from(second, 11, 1)
-    down_from(third, 8, 3)
-    down_from(last, 6, 2)
+    down_from(third, 9, 2)
     total = added(small_line, sent2)
     small_out[...] = total
     norm_grad = pltpu.roll(total, (width - me * rows) % width, 1)[:, :128]
@@ -1080,17 +1193,31 @@
         return jnp.sum(jnp.sum(block * block, axis=0, keepdims=True), axis=1, keepdims=True)
 
     tile8 = jnp.zeros((8, 128), jnp.float32)
-    master, first_moment, second_moment = (norms_ref[i] for i in range(3))
+    master, first_moment, second_moment = (ref[...] for ref in norms_refs)
     update = lamb_moments(master, first_moment, second_moment, norm_grad[:4, : master.shape[1]], 0.0)[2]
     for i in range(4):
         tile8 = put(tile8, 4 + i, 0.5 * square(master[i : i + 1]), 0.5 * square(update[i : i + 1]))
 
+    def squares(p, n, lanes, start):
+        master = masters[0][n, :, lanes] if p == 0 else masters[p][:, lanes]
+        first_moment, second_moment = (
+            moment(i, p, n)[...] if p else moment(i, p, n)[:, lanes] for i in range(2)
+        )
+        grad = sums_ref[:, start : start + master.shape[1]]
+        update = lamb_moments(master, first_moment, second_moment, grad, WEIGHT_DECAY)[2]
+        return square(master), square(update)
+
     def matrix(tile8, p, start):
-        master = params[p][...]
-        grad = sums_ref[:, start : start + master.shape[1]]
-        update = lamb_moments(master, params[4 + p][...], params[8 + p][...], grad, WEIGHT_DECAY)[2]
-        return put(tile8, p, square(master), square(update))
-
+        size = masters[p].shape[1]
+        weights, updates = 0.0, 0.0
+        for n in range(max(size // width, 1)):
+            step = min(size, width)
+            found = squares(p, n, slice(n * step, (n + 1) * step), start + n * step)
+            weights, updates = weights + found[0], updates + found[1]
+        return put(tile8, p, weights, updates)
+
+    for one in moment_loads:
+        one.wait()
     tile8 = matrix(matrix(tile8, 3, at_fo), 2, at_in)
     down_from(last, 8, 1)
     tile8 = matrix(tile8, 1, at_out)
@@ -1099,11 +1226,8 @@
         down_from(last, blocks - 1 - pair, 1)
         for part in range(3):
             lanes = slice(pair * PAIR, (pair + 1) * PAIR)
-            master = params[0][part, :, lanes]
-            start = (3 * pair + part) * PAIR
-            grad = sums_ref[:, start : start + PAIR]
-            update = lamb_moments(master, params[4][part, :, lanes], params[8][part, :, lanes], grad, WEIGHT_DECAY)[2]
-            weights, updates = weights + square(master), updates + square(update)
+            found = squares(0, part, lanes, (3 * pair + part) * PAIR)
+            weights, updates = weights + found[0], updates + found[1]
     tile8 = put(tile8, 0, weights, updates)
     here_cores = core * (NX * NY) + here_plane
     norm_plane[here_cores] = tile8
@@ -1115,21 +1239,17 @@
     for one in (*sent1, *sent2, *sent3, *sent4):
         one.wait_send()
 
-    def drain(c):
-        for k in range(8):
-            leg1(c, k).wait_send()
-        for rz in range(NZ):
-            leg2(c, rz).wait_send()
+    for c in range(blocks):
+        leg1(c).wait_send()
+        leg2(c).wait_send()
         for rz in (1, 2, 3):
             leg3(c, rz).wait_send()
-
-    each(drain, 0, blocks)
     each(lambda t: tokens_out(t).wait(), 0, tiles)
 
 
-def layer(lengths, layer_gates, gate_lanes, hidden_gate, unit_gate, norms, norm_shard, params, tokens, teacher):
+def layer(lengths, layer_gates, head_gate, hidden_gate, unit_gate, norms, params, tokens, teacher):
     count, width = tokens.shape
-    own_width, units, rows = gate_lanes.shape[1], unit_gate.shape[0], norms.shape[2]
+    (rows, own_width), units = params[1].shape, unit_gate.shape[0]
     total = 4 * own_width + 2 * units
     tiles, tall, blocks = count // TILE, count // ROW, total // BLOCK
     vmem, smem = pl.BlockSpec(memory_space=pltpu.VMEM), pl.BlockSpec(memory_space=pltpu.SMEM)
@@ -1137,7 +1257,7 @@
     low, full = jnp.bfloat16, jnp.float32
     return pl.pallas_call(
         layer_kernel,
-        in_specs=[smem, smem] + [vmem] * (5 + len(params)) + [anywhere] * 2,
+        in_specs=[smem] * 3 + [vmem] * 9 + [anywhere] * 10,
         out_specs=[anywhere] * 2 + [vmem] * 4,
         out_shape=[
             jax.ShapeDtypeStruct((count, width), low),
@@ -1163,7 +1283,7 @@
             pltpu.VMEM((count, units), low),
             pltpu.VMEM((count, units), low),
             pltpu.VMEM((count, width), full),
-            pltpu.VMEM((blocks, NZ, rows, BLOCK), full),
+            pltpu.VMEM((8, NZ, rows, BLOCK), full),
             pltpu.VMEM((8, width), full),
             pltpu.VMEM((6, 8, width), full),
             pltpu.VMEM((8, units), full),
@@ -1172,16 +1292,23 @@
             pltpu.VMEM((NZ, 8, width), full),
             pltpu.VMEM((2 * NX * NY, 8, 128), full),
             pltpu.VMEM((NZ, 8, 128), full),
+            pltpu.VMEM((1, own_width), full),
+            pltpu.VMEM((1, units), full),
+            pltpu.VMEM((128, 128), full),
+            pltpu.VMEM((width, units), low),
             pltpu.SemaphoreType.DMA((3, tiles)),
             pltpu.SemaphoreType.DMA((2, tiles)),
             pltpu.SemaphoreType.DMA((blocks + 1, 15)),
             pltpu.SemaphoreType.DMA((blocks + 1, 16)),
             pltpu.SemaphoreType.DMA((4, tiles)),
             pltpu.SemaphoreType.DMA((4, tiles)),
-            pltpu.SemaphoreType.DMA((blocks, 15)),
-            pltpu.SemaphoreType.DMA((blocks, 15)),
+            pltpu.SemaphoreType.DMA((blocks, 5)),
+            pltpu.SemaphoreType.DMA((blocks, 5)),
             pltpu.SemaphoreType.DMA((16,)),
             pltpu.SemaphoreType.DMA((16,)),
+            pltpu.SemaphoreType.DMA((3,)),
+            pltpu.SemaphoreType.DMA((2, 8)),
+            pltpu.SemaphoreType.REGULAR,
             pltpu.SemaphoreType.REGULAR,
             pltpu.SemaphoreType.REGULAR,
         ],
@@ -1189,7 +1316,10 @@
             collective_id=0, has_side_effects=True, vmem_limit_bytes=62 << 20
         ),
         name="layer",
-    )(lengths, layer_gates, gate_lanes, hidden_gate[None, :], unit_gate[None, :], norms, norm_shard, *params, tokens, teacher)
+    )(lengths, layer_gates, head_gate, hidden_gate, unit_gate, *params[:4], *norms, *params[4:], tokens, teacher)
+
+
+PIECES = 4
 
 
 def spans(shape):
@@ -1203,8 +1333,43 @@
     ]
 
 
-def update_kernel(sums_ref, small_ref, norm_ref, total_ref, norms_ref, *refs):
-    params, outs = refs[:12], refs[12:]
+def update_kernel(count, small_ref, norm_ref, total_ref, *refs):
+    norms_refs, refs = refs[:3], refs[3:]
+    passed_in, sums_hbm, params_hbm, refs = refs[:count], refs[count], refs[count + 1 : count + 13], refs[count + 13 :]
+    passed_out, made_hbm, refs = refs[:count], refs[count : count + 20], refs[count + 20 :]
+    small_outs, refs = refs[:10], refs[10:]
+    sums_ref, params, outs = refs[0], refs[1:13], refs[13:33]
+    held, refs = refs[33 : 33 + count], refs[33 + count :]
+    pass_in, pass_out, in_sem, out_sem = refs
+    pieces = [
+        (i, n, pl.ds(n * (a.shape[0] // PIECES), a.shape[0] // PIECES))
+        for n in range(PIECES)
+        for i, a in enumerate(held)
+    ]
+    passes_in = [
+        pltpu.make_async_copy(passed_in[i].at[at], held[i].at[at], pass_in.at[i, n])
+        for i, n, at in pieces
+    ]
+    passes_out = [
+        pltpu.make_async_copy(held[i].at[at], passed_out[i].at[at], pass_out.at[i, n])
+        for i, n, at in pieces
+    ]
+    loads = [
+        pltpu.make_async_copy(source, target, in_sem.at[i])
+        for i, (source, target) in enumerate(
+            zip((*params_hbm, sums_hbm), (*params, sums_ref), strict=True)
+        )
+    ]
+    stores = [
+        pltpu.make_async_copy(source, target, out_sem.at[i])
+        for i, (source, target) in enumerate(zip(outs, made_hbm, strict=True))
+    ]
+    loads[12].start()
+    for p in range(4):
+        for i in range(3):
+            loads[4 * i + p].start()
+    for one in passes_in:
+        one.start()
     weight_norm = jnp.sqrt(total_ref[:, 0:1])
     update_norm = jnp.sqrt(total_ref[:, 1:2])
     trust = weight_norm / update_norm
@@ -1219,47 +1384,71 @@
         for target, value in zip(targets, made, strict=True):
             target[at] = value
 
+    loads[12].wait()
     start = 0
     for p in range(4):
+        for i in range(3):
+            loads[4 * i + p].wait()
         targets = outs[5 * p : 5 * p + 5]
         for at in spans(params[p].shape):
-            width = params[p][at].shape[-1]
+            width = params[p].shape[1] if len(at) == 2 else PAIR
             grad = sums_ref[:, start : start + width]
             values = (*(params[4 * i + p][at] for i in range(3)), grad)
             step(slice(p, p + 1), targets, at, values, WEIGHT_DECAY)
             start += width
-    norm_grad = norm_ref[:4, : norms_ref.shape[2]]
-    values = (*(norms_ref[i] for i in range(3)), norm_grad)
-    step(slice(4, 8), outs[20:25], (Ellipsis,), values, 0.0)
-    stats_out, heads_out, units_out, hidden_out, layers_out = outs[25:]
+        for one in stores[5 * p : 5 * p + 5]:
+            one.start()
+        if p == 0:
+            for one, other in zip(passes_in, passes_out, strict=True):
+                one.wait()
+                other.start()
+    norm_grad = norm_ref[:4, : norms_refs[0].shape[1]]
+    values = (*(ref[...] for ref in norms_refs), norm_grad)
+    step(slice(4, 8), small_outs[:5], (Ellipsis,), values, 0.0)
+    stats_out, heads_out, units_out, hidden_out, layers_out = small_outs[5:]
     lane = lax.broadcasted_iota(jnp.int32, (8, 128), 1)
-    stats_out[...] = jnp.where(lane == 0, weight_norm, jnp.where(lane == 1, update_norm, trust))
+    stats = jnp.where(lane == 0, weight_norm, jnp.where(lane == 1, update_norm, trust))
+    stats_out[...] = jnp.transpose(jnp.concatenate([stats] * 16, axis=0))[:3, :8]
     heads_out[...] = small_ref[7:8, : heads_out.shape[1]]
     width = small_ref.shape[1]
-    for i in range(units_out.shape[1] // width):
-        units_out[:, i * width : (i + 1) * width] = small_ref[5 + i : 6 + i, :]
-    hidden_out[...] = small_ref[4:5, :]
+    for i in range(units_out.shape[0] // width):
+        units_out[i * width : (i + 1) * width] = small_ref[5 + i : 6 + i, :].reshape(width)
+    hidden_out[...] = small_ref[4:5, :].reshape(width)
     layers_out[...] = small_ref[7:8, 128:130]
-
-
-def update(sums, small, norm_grad, totals, norms, params, sizes):
-    vmem = pl.BlockSpec(memory_space=pltpu.VMEM)
-    shapes = []
+    for one in (*stores, *passes_out):
+        one.wait()
+
+
+def update(passed, sums, small, norm_grad, totals, norms, params, sizes):
+    vmem, anywhere = pl.BlockSpec(memory_space=pltpu.VMEM), pl.BlockSpec(memory_space=pltpu.HBM)
+    big, little = [], []
     for master in params[:4]:
-        shapes += [jax.ShapeDtypeStruct(master.shape, jnp.float32)] * 4
-        shapes += [jax.ShapeDtypeStruct(master.shape, jnp.bfloat16)]
-    shapes += [jax.ShapeDtypeStruct(norms.shape[1:], jnp.float32)] * 4
-    shapes += [jax.ShapeDtypeStruct(norms.shape[1:], jnp.bfloat16)]
-    shapes += [jax.ShapeDtypeStruct((8, 128), jnp.float32)]
-    shapes += [jax.ShapeDtypeStruct((1, size), jnp.float32) for size in sizes]
-    return pl.pallas_call(
-        update_kernel,
-        in_specs=[vmem] * (5 + len(params)),
-        out_specs=[vmem] * len(shapes),
-        out_shape=shapes,
-        compiler_params=pltpu.CompilerParams(vmem_limit_bytes=48 << 20),
+        big += [jax.ShapeDtypeStruct(master.shape, jnp.float32)] * 4
+        big += [jax.ShapeDtypeStruct(master.shape, jnp.bfloat16)]
+    little += [jax.ShapeDtypeStruct(norms[0].shape, jnp.float32)] * 4
+    little += [jax.ShapeDtypeStruct(norms[0].shape, jnp.bfloat16)]
+    little += [jax.ShapeDtypeStruct((3, 8), jnp.float32)]
+    little += [jax.ShapeDtypeStruct(size, jnp.float32) for size in sizes]
+    through = [jax.ShapeDtypeStruct(a.shape, a.dtype) for a in passed]
+    made = pl.pallas_call(
+        functools.partial(update_kernel, len(passed)),
+        in_specs=[vmem] * 6 + [anywhere] * (len(passed) + 1 + len(params)),
+        out_specs=[anywhere] * (len(passed) + len(big)) + [vmem] * len(little),
+        out_shape=[*through, *big, *little],
+        scratch_shapes=[
+            pltpu.VMEM(sums.shape, jnp.float32),
+            *[pltpu.VMEM(a.shape, a.dtype) for a in params],
+            *[pltpu.VMEM(a.shape, a.dtype) for a in big],
+            *[pltpu.VMEM(a.shape, a.dtype) for a in passed],
+            pltpu.SemaphoreType.DMA((len(passed), PIECES)),
+            pltpu.SemaphoreType.DMA((len(passed), PIECES)),
+            pltpu.SemaphoreType.DMA((13,)),
+            pltpu.SemaphoreType.DMA((20,)),
+        ],
+        compiler_params=pltpu.CompilerParams(vmem_limit_bytes=60 << 20),
         name="update",
-    )(sums, small, norm_grad, totals, norms, *params)
+    )(small, norm_grad, totals, *norms, *passed, sums, *params)
+    return made[: len(passed)], made[len(passed) :]
 
 
 def core_sum(part):
@@ -1280,7 +1469,7 @@
             start += master.shape[1]
         found.append(pair)
     master, first_moment, second_moment = norms
-    update = lamb_moments(master, first_moment, second_moment, norm_grad[:4, : norms.shape[2]], 0.0)[2]
+    update = lamb_moments(master, first_moment, second_moment, norm_grad[:4, : master.shape[1]], 0.0)[2]
     rows = jnp.stack([jnp.sum(master * master, axis=1), jnp.sum(update * update, axis=1)], axis=1)
     found = jnp.concatenate([jnp.stack(found), rows / head_count])
     return jnp.pad(lax.psum(found, ("dp", "head")), ((0, 0), (0, 126)))
@@ -1290,13 +1479,15 @@
     return jnp.transpose(qkv, (1, 0, 2))
 
 
-def plain_layer(lengths, layer_gates, gate_lanes, hidden_gate, unit_gate, norms, norm_shard, params, tokens, teacher):
-    heads_here, rows = gate_lanes.shape[1] // HEAD_DIM, norms.shape[2]
-    own_width, units = gate_lanes.shape[1], unit_gate.shape[0]
+def plain_layer(lengths, layer_gates, head_gate, hidden_gate, unit_gate, norms, params, tokens, teacher):
+    heads_here, units = head_gate.shape[0], unit_gate.shape[0]
+    rows, own_width = params[1].shape
+    gate_lanes = jnp.repeat(head_gate, HEAD_DIM)[None, :]
+    norm_shard = norms[0].T.astype(jnp.bfloat16)
     shards = [params[p][at] for p in range(4) for at in spans(params[p].shape)]
     shards = jnp.concatenate(shards, axis=1).astype(jnp.bfloat16)
     w, norm_t = (lax.all_gather(s, "dp", axis=0, tiled=True) for s in (shards, norm_shard))
-    norm_p = norm_t[:, :4].T.astype(jnp.float32)
+    norm_p = norm_t.T.astype(jnp.float32)
     w_qkv, w_out_t, w_in, w_fo_t = jnp.split(
         w, (3 * own_width, 4 * own_width, 4 * own_width + units), axis=1
     )
@@ -1355,7 +1546,6 @@
     second_norms,
 ):
     ours = lax.axis_size("dp") == GRID and lax.axis_size("head") == 2
-    gate_lanes = jnp.repeat(head_gate, HEAD_DIM)[None, :]
     params = [
         rows_first(master_qkv),
         master_attn_out.T,
@@ -1370,23 +1560,23 @@
         second_ffn_in,
         second_ffn_out.T,
     ]
-    norms = jnp.stack([master_norms, first_norms, second_norms])
-    norm_shard = jnp.pad(master_norms.T, ((0, 0), (0, 124))).astype(jnp.bfloat16)
+    norms = [master_norms, first_norms, second_norms]
     run = layer if ours else plain_layer
     student, grad_tokens, sums, small, norm_grad, totals = run(
         lengths,
         layer_gates,
-        gate_lanes,
+        head_gate,
         hidden_gate,
         unit_gate,
         norms,
-        norm_shard,
         params,
         tokens,
         teacher,
     )
-    sizes = (head_gate.shape[0], unit_gate.shape[0], hidden_gate.shape[0], 2)
-    made = update(sums, small, norm_grad, totals, norms, params, sizes)
+    sizes = ((1, head_gate.shape[0]), unit_gate.shape, hidden_gate.shape, (1, 2))
+    (student, grad_tokens), made = update(
+        (student, grad_tokens), sums, small, norm_grad, totals, norms, params, sizes
+    )
     results = []
     for p in range(4):
         for value in made[5 * p : 5 * p + 5]:
@@ -1399,7 +1589,7 @@
         *gate_results,
         *results,
         *norm_results,
-        stats_rows[:, :3].T,
+        stats_rows,
     )
 
 

time: 244 us -> 196 us (0.80)
  Pallas kernels: 221 us -> 195 us
  local copies, waits for them, and re-layouts: 18.7 us -> 0 us
  other arithmetic: 3.22 us -> 0 us
    pallas_call x2, Pallas kernels: 221 us -> 195 us  [the longest x1 185 us: layer(): pl.pallas_call(layer_kernel, in_specs=[smem] * 3 + [vmem] * 9 + [anywhere...]
    unnamed x39 -> x0, local copies, waits for them, and re-layouts: 14 us -> none
    broadcast_in_dim x3 -> x0, local copies, waits for them, and re-layouts: 3.28 us -> none  [the longest x1 1.29 us: layer(): unit_gate[None, :]]
where the time goes in v4:
time: 196 us
  Pallas kernels  195 us (99%)
    pallas_call x1, Pallas kernels, layer(): pl.pallas_call(layer_kernel, in_specs=[smem] * 3 + [vmem] * 9 + [anywhere...  185 us
    pallas_call x1, Pallas kernels, update(): pl.pallas_call(functools.partial(update_kernel, len(passed)), in_specs=[v...  9.97 us

profile of v4, /device:TPU:0, one launch (start us, length us, event | category | flops | bytes accessed | tf_op | source)
XLA Modules:
  0.0 195.5 jit_solution(15538198755011656801)
XLA Ops:
  0.7 184.7 %layer.1 = (bf16[1536,768]{1,0:T(8,128)(2,1)}, f32[1536,768]{1,0:T(8,128)}, f32[48,4608]{1,0:T(8,128)}, f32[8,768]{1,0:T(8,128)}, f32[8,128]{1,0:T(8,128)}, /*index=5*/f32[8,128]{1,0:T(8,128)}) custom-call(s32[3,6]{1,0:T(4,128)} %lengths_ref.1, f32[2]{0:T(128)} %gates_ref.1, f32[6]{0:T(128)} %head_gate_ref.1, f32[768]{0:T(1024)} %hidden_gate_ref.1, ...), custom_call_target="tpu_custom_call" | custom-call | tf_op jit(solution)/shard_map/layer/pallas_call | solution.py:1258
  185.4 10.0 %update.1 = (bf16[1536,768]{1,0:T(8,128)(2,1)}, f32[1536,768]{1,0:T(8,128)}, f32[3,48,384]{2,1,0:T(8,128)}, f32[3,48,384]{2,1,0:T(8,128)}, f32[3,48,384]{2,1,0:T...) custom-call(f32[8,768]{1,0:T(8,128)} %get-tuple-element.70.small_ref, ...), custom_call_target="tpu_custom_call" | custom-call | tf_op jit(solution)/shard_map/update/pallas_call | solution.py:1433

commit v5 on v4

--- a/solution.py
+++ b/solution.py
@@ -824,6 +824,8 @@
             two(all_near_line, 5)
 
     lax.fori_loop(0, tiles, phase2, None)
+    each(all_sent, 0, 8)
+    all_sent(blocks)
     each(all_last, 8, blocks)
     stash_fo = pltpu.make_async_copy(w.at[:, at_fo:], fo_copy, stash_sem.at[2])
     stash_fo.start()
@@ -834,8 +836,7 @@
         swap(1, t).start()
 
     lax.fori_loop(0, tiles, down, None)
-    each(all_sent, 0, blocks)
-    all_sent(blocks)
+    each(all_sent, 8, blocks)
 
     def student_out(t):
         return pltpu.make_async_copy(
@@ -1233,18 +1234,17 @@
     norm_plane[here_cores] = tile8
     targets = [(p, core) for p in plane[1:]] + [(p, 1 - core) for p in plane]
     sent3 = spread(norm_plane, 6, targets, here_cores)
-    norm_line[z] = added(norm_plane, sent3)
-    sent4 = spread(norm_line, 13, line_peers, z)
-    total_out[...] = added(norm_line, sent4)
-    for one in (*sent1, *sent2, *sent3, *sent4):
-        one.wait_send()
-
     for c in range(blocks):
         leg1(c).wait_send()
         leg2(c).wait_send()
         for rz in (1, 2, 3):
             leg3(c, rz).wait_send()
     each(lambda t: tokens_out(t).wait(), 0, tiles)
+    norm_line[z] = added(norm_plane, sent3)
+    sent4 = spread(norm_line, 13, line_peers, z)
+    total_out[...] = added(norm_line, sent4)
+    for one in (*sent1, *sent2, *sent3, *sent4):
+        one.wait_send()
 
 
 def layer(lengths, layer_gates, head_gate, hidden_gate, unit_gate, norms, params, tokens, teacher):

time: 196 us -> 195 us (level)
  no operation moved by 1% of the time
where the time goes in v5:
time: 195 us
  Pallas kernels  194 us (99%)
    pallas_call x1, Pallas kernels, layer(): pl.pallas_call(layer_kernel, in_specs=[smem] * 3 + [vmem] * 9 + [anywhere...  184 us
    pallas_call x1, Pallas kernels, update(): pl.pallas_call(functools.partial(update_kernel, len(passed)), in_specs=[v...  9.97 us

profile of v5, /device:TPU:0, one launch (start us, length us, event | category | flops | bytes accessed | tf_op | source)
XLA Modules:
  0.0 195.2 jit_solution(11345191799297702863)
XLA Ops:
  0.7 184.3 %layer.1 = (bf16[1536,768]{1,0:T(8,128)(2,1)}, f32[1536,768]{1,0:T(8,128)}, f32[48,4608]{1,0:T(8,128)}, f32[8,768]{1,0:T(8,128)}, f32[8,128]{1,0:T(8,128)}, /*index=5*/f32[8,128]{1,0:T(8,128)}) custom-call(s32[3,6]{1,0:T(4,128)} %lengths_ref.1, f32[2]{0:T(128)} %gates_ref.1, f32[6]{0:T(128)} %head_gate_ref.1, f32[768]{0:T(1024)} %hidden_gate_ref.1, ...), custom_call_target="tpu_custom_call" | custom-call | tf_op jit(solution)/shard_map/layer/pallas_call | solution.py:1258
  185.0 10.0 %update.1 = (bf16[1536,768]{1,0:T(8,128)(2,1)}, f32[1536,768]{1,0:T(8,128)}, f32[3,48,384]{2,1,0:T(8,128)}, f32[3,48,384]{2,1,0:T(8,128)}, f32[3,48,384]{2,1,0:T...) custom-call(f32[8,768]{1,0:T(8,128)} %get-tuple-element.70.small_ref, ...), custom_call_target="tpu_custom_call" | custom-call | tf_op jit(solution)/shard_map/update/pallas_call | solution.py:1433
